TPU v7x, 512 devices: a whole 4x8x8 slice. The times are simulated.
512 devices in a mesh: comp: 4 (over x), row: 8 (over y_lo, core), col: 16 (over y_hi, z).
Axes of the slice: x: 4, y: 8 (y_hi: 2, y_lo: 4; y = y_hi * 4 + y_lo), z: 8, core: 2. Of those that a mesh axis runs over, the one named last changes fastest.
Arguments:
- atmosphere_level_state: float32 [4, 72, 262144], P(None, None, ('comp', 'row', 'col')), may hold values from -6 to 6
- atmosphere_mixing_map: float32 [72, 72], replicated, may hold values from -0.5 to 1, as said below
- sea_surface_temps: float32 [262144], P(('comp', 'row', 'col')), may hold values from -6 to 6
- tracers: float32 [2, 80, 256, 2048], P(None, None, ('comp', 'row'), 'col'), may hold values from -6 to 6
- currents: float32 [2, 256, 2048], P(None, ('comp', 'row'), 'col'), may hold values from -3 to 3
- ocean_advect_velocity: bfloat16 [2, 80, 256, 2048], P(None, None, ('comp', 'row'), 'col'), may hold values from -0.29882812 to 0.29882812
- ocean_mixing_map: float32 [80, 80], replicated, may hold values from -0.5 to 1, as said below
- ocean_cell_mask: int32 [256, 2048], P(('comp', 'row'), 'col'), may hold values 0 or 1
- remap_weight_tiles: bfloat16 [4, 128, 64, 4096], P('comp', ('row', 'col')), may hold values from 0 to 0.0078125
- outgoing_block_table: int32 [4, 128, 128, 2], P('comp', ('row', 'col')), may hold values from -1 to 7, as said below
- arrival_slot_table: int32 [4, 128, 64], P('comp', ('row', 'col')), may hold values from 0 to 255, as said below
Outputs:
- atm_final: float32 [4, 72, 262144], P(None, None, ('comp', 'row', 'col'))
- ocean_tracers: float32 [2, 80, 256, 2048], P(None, None, ('comp', 'row'), 'col')
- ocean_currents: float32 [2, 256, 2048], P(None, ('comp', 'row'), 'col')
- returned: float32 [3, 262144], P(None, ('comp', 'row', 'col'))
Inputs may be any that keep to these rules, and one draw needn't show every extreme that they name: outgoing_block_table[c, p, d, s] is the block, within device p's 8 blocks, that device p of band c sends to device d in slot s, or -1 where no contribution of d names that slot; in every band some source device has all its slots to every device named. arrival_slot_table[c, d, j] = p * 2 + s names the slot of source device p through which contribution j of device d arrives; one device d never names a slot twice. `ocean_cell_mask`: 1 marks an ocean cell, 0 land. `atmosphere_mixing_map`: a fixed linear map over one column's levels. `ocean_mixing_map`: a fixed linear map over one column's levels.
All inputs are finite; a program needn't handle non-finite values. No bound on the sum of `ocean_cell_mask` on one device may be relied on, other than what follows from the above.
Results may differ from a plain program's by a relative error of at most 0.0027.
Values may be sent and summed in bfloat16 or wider, within the bound.
No kernel may reach another device: no remote copies, remote signals or barrier semaphores. Data moves between devices by JAX's collectives and lax.ppermute only.
A program may use at most 64 MiB of HBM per device.

v0:
```python
import functools

import jax
import jax.numpy as jnp
import numpy as np
from jax import lax
from jax.experimental import pallas as pl
from jax.experimental.pallas import tpu as pltpu
from jax.sharding import PartitionSpec as P

STEPS = 6
HALO = 6
ROWS = 8
EXT = ROWS + 2 * HALO
WEST, EAST = EXT, EXT + 1
STRIPS = EXT + 2
LANES = 128
WIDE = 256
HIGHEST = lax.Precision.HIGHEST
VMEM_LIMIT = 48 * 1024 * 1024

heat_rate = 0.5
vapour_rate = 0.5
drag_rate = 0.3
saturation = 0.6
flux_gains = (0.3, 0.3, -0.3, -0.3)
diffusion = 0.15
surface_gain = (-0.3, 0.3)
surface_push = 0.3
current_drag = 0.1
coriolis = 0.2
turn = np.array([[1.0 - current_drag, coriolis], [-coriolis, 1.0 - current_drag]])

f32 = jnp.float32
bf16 = jnp.bfloat16
VMEM = pl.BlockSpec(memory_space=pltpu.VMEM)
HBM = pl.BlockSpec(memory_space=pltpu.HBM)


def call(body, out_shape, name, in_specs, out_specs=None, scratch=(), aliases=None):
    if out_specs is None:
        out_specs = jax.tree.map(lambda _: VMEM, out_shape)
    return pl.pallas_call(
        body,
        out_shape=out_shape,
        in_specs=in_specs,
        out_specs=out_specs,
        scratch_shapes=list(scratch),
        input_output_aliases=aliases or {},
        compiler_params=pltpu.CompilerParams(vmem_limit_bytes=VMEM_LIMIT),
        name=name,
    )


def shape(dims, dtype=f32):
    return jax.ShapeDtypeStruct(dims, dtype)


def exact(a, b):
    return jnp.dot(a, b, precision=HIGHEST, preferred_element_type=f32)


def times(a, b):
    return jnp.dot(a, b, preferred_element_type=f32)


def times_rows(a, b):
    return lax.dot_general(a, b, (((1,), (1,)), ((), ())), preferred_element_type=f32)


def iota(dims, axis):
    return lax.broadcasted_iota(jnp.int32, dims, axis)


def one_hot(condition):
    return condition.astype(f32).astype(bf16)


def halves(x):
    high = x.astype(bf16)
    return high, (x - high.astype(f32)).astype(bf16)


def flux_body(a_hbm, m_ref, sst_ref, table_ref, pay_ref, g_ref, top_ref, edge_ref, a_ref, sem):
    copy = pltpu.make_async_copy(a_hbm, a_ref, sem)
    copy.start()
    levels = m_ref.shape[0]
    bottom = levels - 1
    power = {1: m_ref[...]}
    power[2] = exact(power[1], power[1])
    power[3] = exact(power[1], power[2])
    power[4] = exact(power[2], power[2])
    power[5] = exact(power[2], power[3])
    power[6] = exact(power[3], power[3])
    first = (iota((1, levels), 1) == bottom).astype(f32)
    rows = [first] + [power[n][bottom:, :] for n in range(1, STEPS)]
    rows = jnp.concatenate(rows + [jnp.zeros((8 - STEPS, levels), f32)], axis=0)
    row_high, row_low = halves(rows)
    both = jnp.concatenate([row_high.astype(f32), row_low.astype(f32)], axis=0).astype(bf16)
    top_ref[...] = power[6]
    lane = iota((levels, 8), 1)
    edge = jnp.zeros((levels, 8), f32)
    for n in range(STEPS):
        edge = jnp.where(lane == n, power[STEPS - n][:, bottom:], edge)
    edge_ref[...] = edge
    copy.wait()
    base = []
    for v in range(4):
        high, low = halves(a_ref[v])
        one = times(both, high)
        base.append(one[:8] + one[8:] + times(row_high, low))
    corner = {n: power[n][bottom:, bottom:] for n in range(1, STEPS)}
    sst = sst_ref[...]
    gained = []
    fluxes = []
    east, north = jnp.zeros_like(sst), jnp.zeros_like(sst)
    for n in range(STEPS):
        now = []
        for v in range(4):
            value = base[v][n : n + 1]
            for k in range(n):
                value = value + corner[n - k] * gained[k][v]
            now.append(value)
        wind = jnp.sqrt(now[2] * now[2] + now[3] * now[3] + 1.0)
        flux = (
            heat_rate * wind * (sst - now[0]),
            vapour_rate * wind * (saturation * sst - now[1]),
            drag_rate * wind * now[2],
            drag_rate * wind * now[3],
        )
        fluxes.append(flux)
        gained.append([flux_gains[v] * flux[v] for v in range(4)])
        east, north = (
            turn[0, 0] * east + turn[0, 1] * north + flux[2],
            turn[1, 0] * east + turn[1, 1] * north + flux[3],
        )
    blank = [jnp.zeros_like(sst)] * (8 - STEPS)
    for v in range(4):
        g_ref[v] = jnp.concatenate([gained[n][v] for n in range(STEPS)] + blank, axis=0)
    pairs = [(fluxes[n][0], fluxes[n][1]) for n in range(STEPS)] + [(east, north)]
    peers = table_ref.shape[0]
    block = iota((8, LANES), 0)
    left = iota((8, LANES), 1) < 64
    even = block % 2 == 0
    for i, pair in enumerate(pairs):
        parts = []
        for side in range(2):
            spread = jnp.zeros((8, LANES), f32)
            for q in range(4):
                tile = jnp.broadcast_to(pair[side][:, q * LANES : (q + 1) * LANES], (8, LANES))
                spread = jnp.where(block // 2 == q, tile, spread)
            parts.append(jnp.where(even == (side == 0), spread, pltpu.roll(spread, 64, 1)))
        tile = jnp.where(left, parts[0], parts[1])
        pay_ref[:, i * LANES : (i + 1) * LANES] = jnp.concatenate([tile] * peers, axis=0).astype(bf16)
    table = [jnp.broadcast_to(table_ref[r : r + 1, :], (8, LANES)) for r in range(peers)]
    pay_ref[:, 7 * LANES :] = jnp.concatenate(table, axis=0).astype(bf16)


def atmosphere_body(a_hbm, g_ref, top_ref, edge_ref, out_hbm, a_ref, sems, out_sems):
    loads = [pltpu.make_async_copy(a_hbm.at[v], a_ref.at[v], sems.at[v]) for v in range(4)]
    stores = [pltpu.make_async_copy(a_ref.at[v], out_hbm.at[v], out_sems.at[v]) for v in range(4)]
    for copy in loads:
        copy.start()
    for v in range(4):
        loads[v].wait()
        a_ref[v] = exact(top_ref[...], a_ref[v]) + exact(edge_ref[...], g_ref[v])
        stores[v].start()
    for copy in stores:
        copy.wait()


def select_body(in_ref, out_ref):
    slots, blocks = out_ref.shape[0], in_ref.shape[0]
    peers = blocks // 8
    row, lane = iota((slots, LANES), 0), iota((slots, LANES), 1)
    entry = (row // (2 * peers)) * 2 + row % 2
    named = times_rows(one_hot(lane == entry), in_ref[:, 7 * LANES :])
    row, lane = iota((slots, blocks), 0), iota((slots, blocks), 1)
    chosen = (named == (lane % 8).astype(f32)) & (lane // 8 == (row // 2) % peers)
    chosen = one_hot(chosen)
    out_ref[...] = times(chosen, in_ref[:, : 7 * LANES]).astype(bf16)


def gather_body(in_ref, back_ref, out_ref):
    slots, blocks = back_ref.shape[0], in_ref.shape[0]
    peers = blocks // 8
    row, lane = iota((slots, LANES), 0), iota((slots, LANES), 1)
    entry = (row // (2 * peers)) * 2 + row % 2
    named = times_rows(in_ref[:, 7 * LANES :], one_hot(lane == entry))
    row, lane = iota((blocks, slots), 0), iota((blocks, slots), 1)
    chosen = (named == (row % 8).astype(f32)) & (row // 8 == (lane // 2) % peers)
    out_ref[...] = times(one_hot(chosen), back_ref[...])


def finish_body(in_ref, out_ref):
    peers = in_ref.shape[0] // 8
    total = in_ref[:8]
    for r in range(1, peers):
        total = total + in_ref[8 * r : 8 * r + 8]
    left = iota((1, LANES), 1) < 64
    for f in range(3):
        tile = total[:, (f // 2) * LANES : (f // 2 + 1) * LANES]
        other = pltpu.roll(tile, 64, 1)
        low, high = (tile, other) if f % 2 == 0 else (other, tile)
        for q in range(4):
            out_ref[f : f + 1, q * LANES : (q + 1) * LANES] = jnp.where(
                left, low[2 * q : 2 * q + 1], high[2 * q + 1 : 2 * q + 2]
            )


def cells_body(w_hbm, out_ref, w_ref, t_ref, low_ref, high_ref, sem):
    copy = pltpu.make_async_copy(w_hbm, w_ref, sem)
    copy.start()
    copy.wait()
    left = iota((16, LANES), 1) < 64
    tiles = w_ref.shape[1] // LANES
    for i in range(tiles):
        t_ref[i * 64 : (i + 1) * 64] = w_ref[:, i * LANES : (i + 1) * LANES].astype(f32)
    for i in range(tiles):
        k = [t_ref[pl.ds(i * 64 + s, 16, stride=4), :] for s in range(4)]
        moved = [pltpu.roll(x, 64, 1) for x in k]
        low_ref[pl.ds(2 * i, 16, stride=64), :] = jnp.where(left, k[0], moved[1])
        high_ref[pl.ds(2 * i, 16, stride=64), :] = jnp.where(left, k[2], moved[3])
        low_ref[pl.ds(2 * i + 1, 16, stride=64), :] = jnp.where(left, moved[0], k[1])
        high_ref[pl.ds(2 * i + 1, 16, stride=64), :] = jnp.where(left, moved[2], k[3])
    out_ref[:, :LANES] = low_ref[...].astype(bf16)
    out_ref[:, LANES:] = high_ref[...].astype(bf16)


def rows_body(x_hbm, v_ref, wet_ref, z_ref, x_ref, f_ref, sem):
    copy = pltpu.make_async_copy(x_hbm, x_ref, sem)
    copy.start()
    levels = x_ref.shape[1] // ROWS
    for t in range(2):
        f_ref[t] = v_ref[t].astype(f32)
    for r in range(ROWS):
        for t in range(2):
            z_ref[r, (2 + t) * levels : (3 + t) * levels, :] = f_ref[
                t, pl.ds(r, levels, stride=ROWS), :
            ].astype(bf16)
        wet = jnp.broadcast_to(wet_ref[r : r + 1, :].astype(f32), (16, LANES))
        z_ref[r, 4 * levels :, :] = wet.astype(bf16)
    copy.wait()
    for r in range(ROWS):
        for t in range(2):
            z_ref[r, t * levels : (t + 1) * levels, :] = x_ref[
                t, pl.ds(r, levels, stride=ROWS), :
            ].astype(bf16)


def packed_edges(rows, depth):
    lane = iota((depth, LANES), 1)
    first = jnp.zeros((depth, LANES), f32)
    last = jnp.zeros((depth, LANES), f32)
    for r, row in rows:
        here = (lane >= r * HALO) & (lane < (r + 1) * HALO)
        first = jnp.where(here, pltpu.roll(row, (r * HALO) % LANES, 1), first)
        last = jnp.where(here, pltpu.roll(row, (r * HALO + HALO) % LANES, 1), last)
    return first.astype(bf16), last.astype(bf16)


def pack_body(before_ref, z_ref, after_ref, first_ref, last_ref):
    depth = z_ref.shape[1]

    def part(i, carry):
        at = pl.ds(pl.multiple_of(i * 16, 16), 16)
        rows = [(r, before_ref[r, at, :].astype(f32)) for r in range(HALO)]
        rows += [(HALO + r, z_ref[r, at, :].astype(f32)) for r in range(ROWS)]
        rows += [(HALO + ROWS + r, after_ref[r, at, :].astype(f32)) for r in range(HALO)]
        first_ref[at, :], last_ref[at, :] = packed_edges(rows, 16)
        return carry

    lax.fori_loop(0, depth // 16, part, 0)


def pack_forcing_body(f_ref, before_ref, after_ref, first_ref, last_ref):
    rows = [(r + 1, before_ref[r].astype(f32)) for r in range(HALO - 1)]
    rows += [(HALO + r, f_ref[16 * r : 16 * r + 16]) for r in range(ROWS)]
    rows += [(HALO + ROWS + r, after_ref[r].astype(f32)) for r in range(HALO - 1)]
    first_ref[...], last_ref[...] = packed_edges(rows, 16)


def along_row(here, west, east, r, lane):
    eastward = jnp.where(
        lane == LANES - 1, pltpu.roll(east, LANES - 1 - HALO * r, 1), pltpu.roll(here, LANES - 1, 1)
    )
    westward = jnp.where(
        lane == 0, pltpu.roll(west, LANES - HALO + 1 - HALO * r, 1), pltpu.roll(here, 1, 1)
    )
    return eastward, westward


def gathered_edges(here, r, lane, to_west, to_east):
    to_west = jnp.where(
        lane == HALO * r + HALO - 1, pltpu.roll(here, HALO * r + HALO - 1, 1), to_west
    )
    to_east = jnp.where(lane == HALO * r, pltpu.roll(here, HALO * r + 1, 1), to_east)
    return to_west, to_east


def around_strips(west, east, to_west, to_east, lane):
    north, south = LANES - HALO, HALO
    return (
        (
            jnp.where(lane % HALO == HALO - 1, to_west, pltpu.roll(west, LANES - 1, 1)),
            pltpu.roll(west, 1, 1),
            pltpu.roll(west, north, 1),
            pltpu.roll(west, south, 1),
        ),
        (
            pltpu.roll(east, LANES - 1, 1),
            jnp.where(lane % HALO == 0, to_east, pltpu.roll(east, 1, 1)),
            pltpu.roll(east, north, 1),
            pltpu.roll(east, south, 1),
        ),
    )


def ocean_step(n, x_ref, coef_ref, mix_ref, cat_ref, store, force=None):
    levels = mix_ref.shape[0]
    low, high = n + 1, EXT - 2 - n
    last = n == STEPS - 1
    rows = list(range(low, high + 1))
    lane = iota((16, LANES), 1)
    level = iota((16, LANES), 0)

    def part(c, carry):
        at = pl.multiple_of(c * 16, 16)
        here_at = pl.ds(at, 16)

        def put(i, idx, here, east, west, north, south):
            stepped = (
                coef_ref[0, idx, here_at, :] * here
                + (coef_ref[1, idx, here_at, :] * east + coef_ref[2, idx, here_at, :] * west)
                + (coef_ref[3, idx, here_at, :] * north + coef_ref[4, idx, here_at, :] * south)
            )
            if force is not None:
                stepped = stepped + jnp.where(level + at == 0, force(idx), 0.0)
            upper, lower = halves(stepped)
            cols = pl.ds(i * LANES, LANES)
            cat_ref[here_at, cols] = upper
            cat_ref[pl.ds(levels + at, 16), cols] = upper
            cat_ref[pl.ds(2 * levels + at, 16), cols] = lower

        west, east = x_ref[WEST, here_at, :], x_ref[EAST, here_at, :]
        to_west, to_east = jnp.zeros_like(west), jnp.zeros_like(east)
        south, here = x_ref[low - 1, here_at, :], x_ref[low, here_at, :]
        for i, r in enumerate(rows):
            north = x_ref[r + 1, here_at, :]
            eastward, westward = along_row(here, west, east, r, lane)
            put(i, r, here, eastward, westward, north, south)
            if not last:
                to_west, to_east = gathered_edges(here, r, lane, to_west, to_east)
            south, here = here, north
        if not last:
            of_west, of_east = around_strips(west, east, to_west, to_east, lane)
            put(len(rows), WEST, west, *of_west)
            put(len(rows) + 1, EAST, east, *of_east)
        return carry

    lax.fori_loop(0, levels // 16, part, 0)
    targets = rows + ([] if last else [WEST, EAST])
    for lo in range(0, len(targets), 4):
        some = targets[lo : lo + 4]
        mixed = times(mix_ref[...], cat_ref[:, lo * LANES : (lo + len(some)) * LANES])
        for i, idx in enumerate(some):
            store(idx, mixed[:, i * LANES : (i + 1) * LANES])


def coefficient_body(
    before_ref, z_ref, after_ref, west_ref, east_ref, x_hbm, mix_ref,
    coef_ref, x1_ref, wet_ref, x_ref, x0_ref, near_ref, cat_ref, sem,
):
    copy = pltpu.make_async_copy(x_hbm, x_ref, sem)
    copy.start()
    levels = mix_ref.shape[0]

    def of(idx, at):
        if idx == WEST:
            return west_ref[at, :].astype(f32)
        if idx == EAST:
            return east_ref[at, :].astype(f32)
        if idx < HALO:
            return before_ref[idx, at, :].astype(f32)
        if idx < HALO + ROWS:
            return z_ref[idx - HALO, at, :].astype(f32)
        return after_ref[idx - HALO - ROWS, at, :].astype(f32)

    lane = iota((8, LANES), 1)
    wets = [of(idx, pl.ds(4 * levels, 16))[:8] for idx in range(STRIPS)]
    to_west, to_east = jnp.zeros_like(lane, f32), jnp.zeros_like(lane, f32)
    for idx in range(STRIPS):
        wet_ref[idx] = wets[idx]
    sides = {}
    for r in range(1, EXT - 1):
        east, west = along_row(wets[r], wets[WEST], wets[EAST], r, lane)
        sides[r] = (east, west, wets[r + 1], wets[r - 1])
        to_west, to_east = gathered_edges(wets[r], r, lane, to_west, to_east)
    sides[WEST], sides[EAST] = around_strips(wets[WEST], wets[EAST], to_west, to_east, lane)
    for idx, near in sides.items():
        for s in range(4):
            near_ref[s, idx] = wets[idx] * near[s]

    def part(c, carry):
        at = pl.multiple_of(c * 16, 16)
        here_at = pl.ds(at, 16)
        for idx in sides:
            along = 0.5 * of(idx, pl.ds(2 * levels + at, 16))
            across = 0.5 * of(idx, pl.ds(3 * levels + at, 16))
            near = []
            for s in range(4):
                one = near_ref[s, idx]
                near.append(jnp.concatenate([one, one], axis=0))
            c_east = near[0] * (diffusion - along)
            c_west = near[1] * (diffusion + along)
            c_north = near[2] * (diffusion - across)
            c_south = near[3] * (diffusion + across)
            coef_ref[0, idx, here_at, :] = 1.0 - ((c_east + c_west) + (c_north + c_south))
            coef_ref[1, idx, here_at, :] = c_east
            coef_ref[2, idx, here_at, :] = c_west
            coef_ref[3, idx, here_at, :] = c_north
            coef_ref[4, idx, here_at, :] = c_south
        for t in range(2):
            for idx in range(STRIPS):
                if not HALO <= idx < HALO + ROWS:
                    x0_ref[t, idx, here_at, :] = of(idx, pl.ds(t * levels + at, 16))
        return carry

    lax.fori_loop(0, levels // 16, part, 0)
    copy.wait()
    for t in range(2):
        for r in range(ROWS):
            x0_ref[t, HALO + r] = x_ref[t, pl.ds(r, levels, stride=ROWS), :]
    for t in range(2):

        def store(idx, value, t=t):
            x1_ref[t, idx] = value

        ocean_step(0, x0_ref.at[t], coef_ref, mix_ref, cat_ref, store)


def remap_body(slot_ref, in_ref, w_ref, u_ref, wet_ref, f_ref, up_ref, down_ref, u_out_ref, p_ref):
    slots = in_ref.shape[0]
    picked = one_hot(iota((64, slots), 1) == slot_ref[...])
    for i in range(7):
        p_ref[i * 64 : (i + 1) * 64, :] = times(picked, in_ref[:, i * LANES : (i + 1) * LANES])
    p_ref[7 * 64 :, :] = jnp.zeros((64, LANES), f32)
    left = iota((8, LANES), 1) < 64
    left_two = iota((16, LANES), 1) < 64
    for r in range(ROWS):
        sources = []
        for side in range(2):
            even, odd = [], []
            for pair in range(2):
                j = 4 * (2 * r + side) + 2 * pair
                one = p_ref[pl.ds(j, 8, stride=64), :]
                two = p_ref[pl.ds(j + 1, 8, stride=64), :]
                even.append(jnp.where(left, one, pltpu.roll(two, 64, 1)))
                odd.append(jnp.where(left, pltpu.roll(one, 64, 1), two))
            sources.append(jnp.concatenate(even, axis=1))
            sources.append(jnp.concatenate(odd, axis=1))
        sources = jnp.concatenate(sources, axis=0).astype(bf16)
        product = times_rows(sources, w_ref[r * LANES : (r + 1) * LANES, :])
        forcing = jnp.where(left_two, product[:16], product[16:])
        f_ref[16 * r : 16 * r + 16, :] = forcing
        if r < HALO - 1:
            down_ref[r] = forcing.astype(bf16)
        if r >= ROWS - HALO + 1:
            up_ref[r - (ROWS - HALO + 1)] = forcing.astype(bf16)
    whole = np.linalg.matrix_power(turn, STEPS)
    wet = wet_ref[...].astype(f32)
    push = [surface_push * f_ref[pl.ds(6 + 8 * v, ROWS, stride=16), :] for v in range(2)]
    for v in range(2):
        ahead = float(whole[v, 0]) * u_ref[0] + float(whole[v, 1]) * u_ref[1] + push[v]
        u_out_ref[v] = u_ref[v] + wet * (ahead - u_ref[v])


def returned_slots(fields, w_ref, slot_row, slots):
    blocks = 2 * ROWS
    block, lane = iota((blocks, LANES), 0), iota((blocks, LANES), 1)
    left = lane < 64
    spread = []
    for field in fields:
        parts = []
        for r in range(ROWS):
            mine = block == 2 * r + (lane >= 64).astype(jnp.int32)
            parts.append(jnp.where(mine, field[r : r + 1], 0.0))
        spread.append(jnp.concatenate(parts, axis=1))
    terms = times(jnp.concatenate(spread, axis=0).astype(bf16), w_ref[...])
    pieces = []
    for k in range(4):
        tiles = []
        for f in range(4):
            if f == 3:
                tiles.append(jnp.zeros((blocks, LANES), f32))
                continue
            tile = terms[f * blocks : (f + 1) * blocks, (k // 2) * LANES : (k // 2 + 1) * LANES]
            tiles.append(tile if k % 2 == f % 2 else pltpu.roll(tile, 64, 1))
        pieces.append(
            jnp.concatenate(
                [jnp.where(left, tiles[0], tiles[1]), jnp.where(left, tiles[2], tiles[3])], axis=1
            )
        )
    partial = jnp.concatenate(pieces, axis=0).astype(bf16)
    placed = one_hot(iota((slots, 64), 0) == slot_row)
    return times(placed, partial).astype(bf16)


def tracer_body(t, with_send, *refs):
    x1_ref, coef_ref, wet_ref, mix_ref, column_ref, f_ref, before_ref, after_ref, west_ref, east_ref = refs[:10]
    if with_send:
        w_ref, slot_ref, u_ref, out_hbm, send_ref = refs[10:15]
        one_ref, two_ref, force_ref, cat_ref, out_ref, sem, sst_ref = refs[15:]
    else:
        _, out_hbm, one_ref, two_ref, force_ref, cat_ref, out_ref, sem = refs[10:]
    levels = mix_ref.shape[0]
    column = jnp.broadcast_to(column_ref[:, 0:1], (levels, LANES))
    for idx in range(1, STRIPS):
        if idx == EXT - 1:
            continue
        if idx == WEST:
            forcing = west_ref[...].astype(f32)[8 * t : 8 * t + 8]
        elif idx == EAST:
            forcing = east_ref[...].astype(f32)[8 * t : 8 * t + 8]
        elif idx < HALO:
            forcing = before_ref[idx - 1].astype(f32)[8 * t : 8 * t + 8]
        elif idx < HALO + ROWS:
            row = 16 * (idx - HALO) + 8 * t
            forcing = f_ref[row : row + 8, :]
        else:
            forcing = after_ref[idx - HALO - ROWS].astype(f32)[8 * t : 8 * t + 8]
        forcing = surface_gain[t] * wet_ref[idx] * forcing
        force_ref[idx] = forcing
        one_ref[idx] = x1_ref[t, idx] + column * forcing[0:1]
    old, new = one_ref, two_ref
    for n in range(1, STEPS):

        def store(idx, value, new=new, n=n):
            if n < STEPS - 1:
                new[idx] = value
            else:
                out_ref[pl.ds(idx - HALO, levels, stride=ROWS), :] = value
                if with_send:
                    sst_ref[idx - HALO : idx - HALO + 1, :] = value[0:1]

        def force(idx, n=n):
            return force_ref[idx, n : n + 1, :]

        ocean_step(n, old, coef_ref, mix_ref, cat_ref, store, force)
        old, new = new, old
    copy = pltpu.make_async_copy(out_ref, out_hbm.at[t], sem)
    copy.start()
    if with_send:
        fields = [sst_ref[...], u_ref[0], u_ref[1]]
        fields = [field.astype(bf16).astype(f32) for field in fields]
        send_ref[...] = returned_slots(fields, w_ref, slot_ref[...], send_ref.shape[0])
    copy.wait()


def neighbours(size):
    up = [(i, i + 1) for i in range(size - 1)]
    return up, [(j, i) for i, j in up]


def on_device(
    atmosphere_level_state,
    atmosphere_mixing_map,
    sea_surface_temps,
    tracers,
    currents,
    ocean_advect_velocity,
    ocean_mixing_map,
    ocean_cell_mask,
    remap_weight_tiles,
    outgoing_block_table,
    arrival_slot_table,
):
    row_count, col_count = lax.axis_size("row"), lax.axis_size("col")
    slots = row_count * col_count * 2
    levels = tracers.shape[1]
    air_levels, air_columns = atmosphere_level_state.shape[1:]
    rows_axis = ("comp", "row")
    up, down = neighbours(lax.axis_size(rows_axis))
    right, leftward = neighbours(col_count)
    dma = pltpu.SemaphoreType.DMA

    arrival = arrival_slot_table.reshape(64)
    source = arrival // 2
    slot = (source % col_count) * (2 * row_count) + (source // col_count) * 2 + arrival % 2
    slot_column = slot.reshape(64, 1)
    slot_by_k = slot.reshape(2 * ROWS, 4).T.reshape(1, 64)

    table = outgoing_block_table.reshape(row_count, col_count * 2).astype(f32)
    table = jnp.pad(table, ((0, 0), (0, LANES - col_count * 2)), constant_values=-1.0)
    payload, gained, top, edge = call(
        flux_body,
        (
            shape((row_count * 8, 8 * LANES), bf16),
            shape((4, 8, air_columns)),
            shape((air_levels, air_levels)),
            shape((air_levels, 8)),
        ),
        "fluxes",
        [HBM, VMEM, VMEM, VMEM],
        scratch=[pltpu.VMEM(atmosphere_level_state.shape, f32), dma],
    )(atmosphere_level_state, atmosphere_mixing_map, sea_surface_temps[None], table)
    row_blocks = lax.all_to_all(payload, "row", 0, 0, tiled=True)
    chosen = call(select_body, shape((slots, 7 * LANES), bf16), "select", [VMEM])(row_blocks)
    arrived = lax.all_to_all(chosen, "col", 0, 0, tiled=True)

    atm_final = call(
        atmosphere_body,
        shape(atmosphere_level_state.shape),
        "atmosphere",
        [HBM, VMEM, VMEM, VMEM],
        HBM,
        scratch=[pltpu.VMEM(atmosphere_level_state.shape, f32), dma((4,)), dma((4,))],
    )(atmosphere_level_state, gained, top, edge)

    flat = tracers.reshape(2, levels * ROWS, LANES)
    depth = 4 * levels + 16
    z = call(
        rows_body,
        shape((ROWS, depth, LANES), bf16),
        "rows",
        [HBM, VMEM, VMEM],
        scratch=[pltpu.VMEM(flat.shape, f32), pltpu.VMEM(flat.shape, f32), dma],
    )(flat, ocean_advect_velocity.reshape(flat.shape), ocean_cell_mask)
    before = lax.ppermute(z[ROWS - HALO :], rows_axis, up)
    after = lax.ppermute(z[:HALO], rows_axis, down)
    edge_shape = shape((depth, LANES), bf16)
    first, last = call(pack_body, (edge_shape, edge_shape), "pack", [VMEM] * 3)(before, z, after)
    east_in = lax.ppermute(first, "col", leftward)
    west_in = lax.ppermute(last, "col", right)
    cells = call(
        cells_body,
        shape((ROWS * LANES, WIDE), bf16),
        "cells",
        [HBM],
        scratch=[
            pltpu.VMEM((64, 4096), bf16),
            pltpu.VMEM((32 * 64, LANES), f32),
            pltpu.VMEM((ROWS * LANES, LANES), f32),
            pltpu.VMEM((ROWS * LANES, LANES), f32),
            dma,
        ],
    )(remap_weight_tiles.reshape(64, 4096))
    rounded = lax.reduce_precision(ocean_mixing_map, 8, 7)
    upper, lower = rounded.astype(bf16), (ocean_mixing_map - rounded).astype(bf16)
    mix = jnp.concatenate([upper, lower, upper], axis=1)
    wide = (STRIPS, levels, LANES)
    cat = pltpu.VMEM((3 * levels, EXT * LANES), bf16)
    coef, x1, wet = call(
        coefficient_body,
        (shape((5, *wide)), shape((2, *wide)), shape((STRIPS, 8, LANES))),
        "coefficients",
        [VMEM] * 5 + [HBM, VMEM],
        scratch=[
            pltpu.VMEM(flat.shape, f32),
            pltpu.VMEM((2, *wide), f32),
            pltpu.VMEM((4, STRIPS, 8, LANES), f32),
            cat,
            dma,
        ],
    )(before, z, after, west_in, east_in, flat, mix)

    edge_rows = shape((HALO - 1, 16, LANES), bf16)
    forcing, send_up, send_down, ocean_currents = call(
        remap_body,
        (shape((ROWS * 16, LANES)), edge_rows, edge_rows, shape(currents.shape)),
        "remap",
        [VMEM] * 5,
        scratch=[pltpu.VMEM((8 * 64, LANES), f32)],
    )(slot_column, arrived, cells, currents, ocean_cell_mask)
    f_before = lax.ppermute(send_up, rows_axis, up)
    f_after = lax.ppermute(send_down, rows_axis, down)
    strip = shape((16, LANES), bf16)
    f_first, f_last = call(pack_forcing_body, (strip, strip), "pack_forcing", [VMEM] * 3)(
        forcing, f_before, f_after
    )
    f_east = lax.ppermute(f_first, "col", leftward)
    f_west = lax.ppermute(f_last, "col", right)

    shared = (
        x1, coef, wet, mix, ocean_mixing_map, forcing, f_before, f_after, f_west, f_east,
    )
    scratch = [
        pltpu.VMEM(wide, f32),
        pltpu.VMEM(wide, f32),
        pltpu.VMEM((STRIPS, 8, LANES), f32),
        cat,
        pltpu.VMEM((levels * ROWS, LANES), f32),
        dma,
    ]
    warm, terms = call(
        functools.partial(tracer_body, 0, True),
        (shape(flat.shape), shape((slots, WIDE), bf16)),
        "temperature",
        [VMEM] * 13,
        (HBM, VMEM),
        scratch=scratch + [pltpu.VMEM((ROWS, LANES), f32)],
    )(*shared, cells, slot_by_k, ocean_currents)
    back = lax.all_to_all(terms, "col", 0, 0, tiled=True)
    sums = call(gather_body, shape((row_count * 8, WIDE)), "gather", [VMEM, VMEM])(row_blocks, back)
    home = lax.all_to_all(sums, "row", 0, 0, tiled=True)
    returned = call(finish_body, shape((3, air_columns)), "finish", [VMEM])(home)
    both = call(
        functools.partial(tracer_body, 1, False),
        shape(flat.shape),
        "salinity",
        [VMEM] * 10 + [HBM],
        HBM,
        scratch=scratch,
        aliases={10: 0},
    )(*shared, warm)
    return (atm_final, both.reshape(tracers.shape), ocean_currents, returned)


def solution(mesh):
    return jax.shard_map(
        on_device,
        mesh=mesh,
        in_specs=(
            P(None, None, ("comp", "row", "col")),
            P(),
            P(("comp", "row", "col")),
            P(None, None, ("comp", "row"), "col"),
            P(None, ("comp", "row"), "col"),
            P(None, None, ("comp", "row"), "col"),
            P(),
            P(("comp", "row"), "col"),
            P("comp", ("row", "col"), None, None),
            P("comp", ("row", "col"), None, None),
            P("comp", ("row", "col"), None),
        ),
        out_specs=(
            P(None, None, ("comp", "row", "col")),
            P(None, None, ("comp", "row"), "col"),
            P(None, ("comp", "row"), "col"),
            P(None, ("comp", "row", "col")),
        ),
        check_vma=False,
    )
```

profile of v0, /device:TPU:11, one launch (start us, length us, event | category | flops | bytes accessed | tf_op | source)
XLA Modules:
  0.0 154.5 jit_solution(34731274908286350)
XLA Ops:
  0.7 0.7 convert_element_type.12
  1.6 1.1 copy-done.2
  2.7 0.8 copy-done.29
  3.4 0.7 copy-done.38
  4.1 1.5 fluxes.1
  5.7 10.6 %all_to_all.44 = bf16[8,8,1024]{2,1,0:T(8,128)(2,1)S(1)} all-to-all(bf16[8,8,1024]{2,1,0:T(8,128)(2,1)S(1)} %bitcast.27), channel_id=1, replica_groups=mesh['comp'=4,'row'=8,'col'=16] {'row'}, dimensions={0} | all-to-all | bytes 262144 | tf_op jit(solution)/shard_map/all_to_all | solution.py:607
  16.3 1.2 select.78
  18.1 13.1 %all-to-all-start.1 = ((bf16[16,16,896]{2,1,0:T(8,128)(2,1)}), bf16[16,16,896]{2,1,0:T(8,128)(2,1)S(1)}, u32[]{:S(2)}, u32[]{:S(2)}) async-start(bf16[16,16,896]{2,1,0:T(8,128)(2,1)} %bitcast.6), calls=%async_computation.1 | async-start | bytes 917504 | tf_op jit(solution)/shard_map/all_to_all | solution.py:609
  31.3 1.1 copy-done
  32.4 1.0 copy-done.19
  33.3 0.7 copy-done.34
  34.5 1.1 fusion.22
  35.5 2.6 %collective-permute-start = (bf16[6,336,128]{2,1,0:T(8,128)(2,1)}, bf16[6,336,128]{2,1,0:T(8,128)(2,1)S(1)}, u32[]{:S(2)}, u32[]{:S(2)}) collective-permute-start(bf16[6,336,128]{2,1,0:T(8,128)(2,1)} %get-tuple-element.39), channel_id=1, source_target_pairs={{0,16},{16,32},{32,48},{48,64},{64,80},{80,96},{96,112},{112,128},... | collective-permute-start | bytes 1548296 | tf_op jit(solution)/shard_map/ppermute | solution.py:629
  38.2 2.3 %collective-permute-start.1 = (bf16[6,336,128]{2,1,0:T(8,128)(2,1)}, bf16[6,336,128]{2,1,0:T(8,128)(2,1)S(1)}, u32[]{:S(2)}, u32[]{:S(2)}) collective-permute-start(bf16[6,336,128]{2,1,0:T(8,128)(2,1)} %get-tuple-element.38), channel_id=1, source_target_pairs={{16,0},{32,16},{48,32},{64,48},{80,64},{96,80},{112,96},{128,112},... | collective-permute-start | bytes 1548296 | tf_op jit(solution)/shard_map/ppermute | solution.py:630
  40.7 1.2 cells.1.w_ref.refs_10_
  43.2 7.1 %all-to-all-done.1 = bf16[16,16,896]{2,1,0:T(8,128)(2,1)S(1)} async-done(((bf16[16,16,896]{2,1,0:T(8,128)(2,1)}), bf16[16,16,896]{2,1,0:T(8,128)(2,1)S(1)}, u32[]{:S(2)}, u32[]{:S(2)}) %all-to-all-start.1) | async-done | bytes 458784 | tf_op jit(solution)/shard_map/all_to_all | solution.py:609
  50.3 1.3 remap.1
  51.6 2.4 %collective-permute-start.4 = (bf16[5,16,128]{2,1,0:T(8,128)(2,1)S(1)}, bf16[5,16,128]{2,1,0:T(8,128)(2,1)S(1)}, u32[]{:S(2)}, u32[]{:S(2)}) collective-permute-start(bf16[5,16,128]{2,1,0:T(8,128)(2,1)S(1)} %get-tuple-element.31), channel_id=1, source_target_pairs={{0,16},{16,32},{32,48},{48,64},{64,80},{80,96},{96,112},{112,128},... | collective-permute-start | bytes 61448 | tf_op jit(solution)/shard_map/ppermute | solution.py:675
  54.0 2.8 %collective-permute-start.5 = (bf16[5,16,128]{2,1,0:T(8,128)(2,1)S(1)}, bf16[5,16,128]{2,1,0:T(8,128)(2,1)S(1)}, u32[]{:S(2)}, u32[]{:S(2)}) collective-permute-start(bf16[5,16,128]{2,1,0:T(8,128)(2,1)S(1)} %get-tuple-element.32), channel_id=1, source_target_pairs={{16,0},{32,16},{48,32},{64,48},{80,64},{96,80},{112,96},{128,112},... | collective-permute-start | bytes 61448 | tf_op jit(solution)/shard_map/ppermute | solution.py:676
  56.8 1.6 %collective-permute-done.1.after_ref = bf16[6,336,128]{2,1,0:T(8,128)(2,1)S(1)} collective-permute-done((bf16[6,336,128]{2,1,0:T(8,128)(2,1)}, bf16[6,336,128]{2,1,0:T(8,128)(2,1)S(1)}, u32[]{:S(2)}, u32[]{:S(2)}) %collective-permute-start.1) | collective-permute-done | bytes 516128 | tf_op jit(solution)/shard_map/ppermute | solution.py:630
  58.4 2.4 %pack.1 = (bf16[336,128]{1,0:T(8,128)(2,1)S(1)}, bf16[336,128]{1,0:T(8,128)(2,1)S(1)}) custom-call(bf16[6,336,128]{2,1,0:T(8,128)(2,1)S(1)} %collective-permute-done.before_ref, bf16[8,336,128]{2,1,0:T(8,128)(2,1)S(1)} %rows.1.z_ref, bf16[6,336,128]{2,1,0:T(8,128)(2,1)S(1)} %collective-permute-done.1.after_ref), custom_call_target="tpu_custom_call" | custom-call | tf_op jit(solution)/shard_map/pack/pallas_call | solution.py:632
  60.8 3.0 %collective-permute-start.2 = (bf16[336,128]{1,0:T(8,128)(2,1)S(1)}, bf16[336,128]{1,0:T(8,128)(2,1)S(1)}, u32[]{:S(2)}, u32[]{:S(2)}) collective-permute-start(bf16[336,128]{1,0:T(8,128)(2,1)S(1)} %get-tuple-element.24), channel_id=1, source_target_pairs={{0,1},{1,2},{2,3},{3,4},{4,5},{5,6},{6,7},{7,8},{8,9},{9,10},{10,1... | collective-permute-start | bytes 258056 | tf_op jit(solution)/shard_map/ppermute | solution.py:634
  63.8 1.3 collective-permute-start.3
  65.1 0.7 pack_forcing.1
  65.8 4.0 %collective-permute-start.6 = (bf16[16,128]{1,0:T(8,128)(2,1)}, bf16[16,128]{1,0:T(8,128)(2,1)S(1)}, u32[]{:S(2)}, u32[]{:S(2)}) collective-permute-start(bf16[16,128]{1,0:T(8,128)(2,1)} %get-tuple-element.33), channel_id=1, source_target_pairs={{0,1},{1,2},{2,3},{3,4},{4,5},{5,6},{6,7},{7,8},{8,9},{9,10},{10,1... | collective-permute-start | bytes 12296 | tf_op jit(solution)/shard_map/ppermute | solution.py:682
  69.8 1.3 collective-permute-start.7
  71.1 0.7 pad_maximum_fusion.mix_ref.refs_3_
  73.8 1.1 copy-done.1
  74.9 1.0 copy-done.5
  76.0 0.8 copy-done.8
  76.7 0.9 copy-done.24
  77.6 0.9 copy-done.26
  78.5 6.6 %coefficients.1 = (f32[5,22,80,128]{3,2,1,0:T(8,128)}, f32[2,22,80,128]{3,2,1,0:T(8,128)S(1)}, f32[22,8,128]{2,1,0:T(8,128)S(1)}) custom-call(bf16[6,336,128]{2,1,0:T(8,128)(2,1)S(1)} %collective-permute-done.before_ref, bf16[8,336,128]{2,1,0:T(8,128)(2,1)S(1)} %rows.1.z_ref, bf16[6,336,128]{2,1,0:T(8,128)(2,1)S(1)} %copy-done.5, ...), custom_call_target="tpu_custom_call" | custom-call | tf_op jit(solution)/shard_map/coefficients/pallas_call | solution.py:653
  85.2 0.9 copy-done.11
  86.1 0.8 copy-done.15
  86.9 0.7 copy-done.21
  87.6 0.7 copy-done.37
  88.9 10.7 %temperature.1 = (f32[2,640,128]{2,1,0:T(8,128)}, bf16[256,256]{1,0:T(8,128)(2,1)S(1)}) custom-call(f32[2,22,80,128]{3,2,1,0:T(8,128)S(1)} %get-tuple-element.26.refs_0_, f32[5,22,80,128]{3,2,1,0:T(8,128)} %get-tuple-element.27.refs_1_, f32[22,8,128]{2,1,0:T(8,128)S(1)} %get-tuple-element.28.refs_2_, bf16[80,240]{1,0:T(8,128)(2,1)S(1)} %copy-done.8, ...), custom_call_target="tpu_custom_call" | custom-call | tf_op jit(solution)/shard_map/temperature/pallas_call | solution.py:695
  99.6 27.0 %all_to_all.45 = bf16[16,16,256]{2,1,0:T(8,128)(2,1)S(1)} all-to-all(bf16[16,16,256]{2,1,0:T(8,128)(2,1)S(1)} %bitcast.28), channel_id=1, replica_groups=mesh['comp'=4,'row'=8,'col'=16] {'col'}, dimensions={0} | all-to-all | bytes 262144 | tf_op jit(solution)/shard_map/all_to_all | solution.py:703
  126.6 0.9 gather.1
  127.5 9.5 %all-to-all-start.3 = ((f32[8,8,256]{2,1,0:T(8,128)}), f32[8,8,256]{2,1,0:T(8,128)S(1)}, u32[]{:S(2)}, u32[]{:S(2)}) async-start(f32[8,8,256]{2,1,0:T(8,128)} %bitcast.13), calls=%async_computation.3 | async-start | bytes 131072 | tf_op jit(solution)/shard_map/all_to_all | solution.py:705
  137.0 0.8 copy-done.28
  137.8 0.8 copy-done.31
  138.6 0.8 copy-done.33
  139.4 2.9 %atmosphere.1 = f32[4,72,512]{2,1,0:T(8,128)} custom-call(f32[4,72,512]{2,1,0:T(8,128)S(1)} %copy-done.3, f32[4,8,512]{2,1,0:T(8,128)S(1)} %copy-done.28, f32[72,72]{1,0:T(8,128)S(1)} %copy-done.31, f32[72,8]{1,0:T(8,128)S(1)} %copy-done.33), custom_call_target="tpu_custom_call" | custom-call | tf_op jit(solution)/shard_map/atmosphere/pallas_call | solution.py:611
  142.4 0.9 copy-done.18
  143.2 10.6 %salinity.1 = f32[2,640,128]{2,1,0:T(8,128)} custom-call(f32[2,22,80,128]{3,2,1,0:T(8,128)S(1)} %get-tuple-element.26.refs_0_, f32[5,22,80,128]{3,2,1,0:T(8,128)} %get-tuple-element.27.refs_1_, f32[22,8,128]{2,1,0:T(8,128)S(1)} %copy-done.18, bf16[80,240]{1,0:T(8,128)(2,1)S(1)} %copy-done.9, ...), custom_call_target="tpu_custom_call", output_to_operand_aliasing={{}: (10, {})} | custom-call | tf_op jit(solution)/shard_map/salinity/pallas_call | solution.py:707
  153.8 0.7 finish.1
  (84 shorter events, 5.5 us)
Async XLA Ops:
  0.6 49.6 %copy-start.35 = (s32[8,128]{1,0:T(8,128)S(1)}, s32[8,128]{1,0:T(8,128)}, u32[]{:S(2)}) copy-start(s32[8,128]{1,0:T(8,128)} %wet_ref.3) | copy-start | bytes 12292
  0.6 39.9 %copy-start.40 = (s32[1,1,64]{2,1,0:T(1,128)S(1)}, s32[1,1,64]{2,1,0:T(1,128)}, u32[]{:S(2)}) copy-start(s32[1,1,64]{2,1,0:T(1,128)} %param.21) | copy-start | bytes 772
  0.7 42.5 %copy-start.14 = (f32[80,80]{1,0:T(8,128)S(1)}, f32[80,80]{1,0:T(8,128)}, u32[]{:S(2)}) copy-start(f32[80,80]{1,0:T(8,128)} %refs_4_.3) | copy-start | bytes 76804
  0.7 49.6 %copy-start.36 = (f32[2,8,128]{2,1,0:T(8,128)S(1)}, f32[2,8,128]{2,1,0:T(8,128)}, u32[]{:S(2)}) copy-start(f32[2,8,128]{2,1,0:T(8,128)} %u_ref.1) | copy-start | bytes 24580
  1.6 1.1 copy-start.2
  2.7 0.8 copy-start.29
  3.4 0.7 copy-start.38
  4.1 36.6 %copy-start.13 = (bf16[1,1,64,4096]{3,2,1,0:T(8,128)(2,1)S(1)}, bf16[1,1,64,4096]{3,2,1,0:T(8,128)(2,1)}, u32[]{:S(2)}) copy-start(bf16[1,1,64,4096]{3,2,1,0:T(8,128)(2,1)} %param.19) | copy-start | bytes 1572868
  5.6 11.8 %copy-start.27 = (f32[4,8,512]{2,1,0:T(8,128)}, f32[4,8,512]{2,1,0:T(8,128)S(1)}, u32[]{:S(2)}) copy-start(f32[4,8,512]{2,1,0:T(8,128)S(1)} %get-tuple-element.21.g_ref) | copy-start | bytes 196612
  5.7 11.8 %copy-start.30 = (f32[72,72]{1,0:T(8,128)}, f32[72,72]{1,0:T(8,128)S(1)}, u32[]{:S(2)}) copy-start(f32[72,72]{1,0:T(8,128)S(1)} %get-tuple-element.22.top_ref) | copy-start | bytes 62212
  5.7 11.8 %copy-start.32 = (f32[72,8]{1,0:T(8,128)}, f32[72,8]{1,0:T(8,128)S(1)}, u32[]{:S(2)}) copy-start(f32[72,8]{1,0:T(8,128)S(1)} %get-tuple-element.23.edge_ref) | copy-start | bytes 6916
  17.5 0.7 copy-start.6
  18.1 32.1 %all-to-all-start.1 = ((bf16[16,16,896]{2,1,0:T(8,128)(2,1)}), bf16[16,16,896]{2,1,0:T(8,128)(2,1)S(1)}, u32[]{:S(2)}, u32[]{:S(2)}) async-start(bf16[16,16,896]{2,1,0:T(8,128)(2,1)} %bitcast.6), calls=%async_computation.1 | async-start | bytes 917504 | tf_op jit(solution)/shard_map/all_to_all | solution.py:609
  31.3 1.1 copy-start
  32.3 1.0 copy-start.19
  33.3 0.7 copy-start.34
  35.5 21.3 %collective-permute-start = (bf16[6,336,128]{2,1,0:T(8,128)(2,1)}, bf16[6,336,128]{2,1,0:T(8,128)(2,1)S(1)}, u32[]{:S(2)}, u32[]{:S(2)}) collective-permute-start(bf16[6,336,128]{2,1,0:T(8,128)(2,1)} %get-tuple-element.39), channel_id=1, source_target_pairs={{0,16},{16,32},{32,48},{48,64},{64,80},{80,96},{96,112},{112,128},... | collective-permute-start | bytes 1548296 | tf_op jit(solution)/shard_map/ppermute | solution.py:629
  38.2 20.2 %collective-permute-start.1 = (bf16[6,336,128]{2,1,0:T(8,128)(2,1)}, bf16[6,336,128]{2,1,0:T(8,128)(2,1)S(1)}, u32[]{:S(2)}, u32[]{:S(2)}) collective-permute-start(bf16[6,336,128]{2,1,0:T(8,128)(2,1)} %get-tuple-element.38), channel_id=1, source_target_pairs={{16,0},{32,16},{48,32},{64,48},{80,64},{96,80},{112,96},{128,112},... | collective-permute-start | bytes 1548296 | tf_op jit(solution)/shard_map/ppermute | solution.py:630
  51.6 13.6 %copy-start.10 = (f32[128,128]{1,0:T(8,128)}, f32[128,128]{1,0:T(8,128)S(1)}, u32[]{:S(2)}) copy-start(f32[128,128]{1,0:T(8,128)S(1)} %get-tuple-element.30.f_ref.refs_5_) | copy-start | bytes 196612
  51.6 13.5 %collective-permute-start.4 = (bf16[5,16,128]{2,1,0:T(8,128)(2,1)S(1)}, bf16[5,16,128]{2,1,0:T(8,128)(2,1)S(1)}, u32[]{:S(2)}, u32[]{:S(2)}) collective-permute-start(bf16[5,16,128]{2,1,0:T(8,128)(2,1)S(1)} %get-tuple-element.31), channel_id=1, source_target_pairs={{0,16},{16,32},{32,48},{48,64},{64,80},{80,96},{96,112},{112,128},... | collective-permute-start | bytes 61448 | tf_op jit(solution)/shard_map/ppermute | solution.py:675
  54.0 11.1 %collective-permute-start.5 = (bf16[5,16,128]{2,1,0:T(8,128)(2,1)S(1)}, bf16[5,16,128]{2,1,0:T(8,128)(2,1)S(1)}, u32[]{:S(2)}, u32[]{:S(2)}) collective-permute-start(bf16[5,16,128]{2,1,0:T(8,128)(2,1)S(1)} %get-tuple-element.32), channel_id=1, source_target_pairs={{16,0},{32,16},{48,32},{64,48},{80,64},{96,80},{112,96},{128,112},... | collective-permute-start | bytes 61448 | tf_op jit(solution)/shard_map/ppermute | solution.py:676
  58.4 14.1 %copy-start.4 = (bf16[6,336,128]{2,1,0:T(8,128)(2,1)}, bf16[6,336,128]{2,1,0:T(8,128)(2,1)S(1)}, u32[]{:S(2)}) copy-start(bf16[6,336,128]{2,1,0:T(8,128)(2,1)S(1)} %collective-permute-done.1.after_ref) | copy-start | bytes 1548292
  60.8 11.8 %collective-permute-start.2 = (bf16[336,128]{1,0:T(8,128)(2,1)S(1)}, bf16[336,128]{1,0:T(8,128)(2,1)S(1)}, u32[]{:S(2)}, u32[]{:S(2)}) collective-permute-start(bf16[336,128]{1,0:T(8,128)(2,1)S(1)} %get-tuple-element.24), channel_id=1, source_target_pairs={{0,1},{1,2},{2,3},{3,4},{4,5},{5,6},{6,7},{7,8},{8,9},{9,10},{10,1... | collective-permute-start | bytes 258056 | tf_op jit(solution)/shard_map/ppermute | solution.py:634
  63.8 9.4 %collective-permute-start.3 = (bf16[336,128]{1,0:T(8,128)(2,1)S(1)}, bf16[336,128]{1,0:T(8,128)(2,1)S(1)}, u32[]{:S(2)}, u32[]{:S(2)}) collective-permute-start(bf16[336,128]{1,0:T(8,128)(2,1)S(1)} %get-tuple-element.25), channel_id=1, source_target_pairs={{1,0},{2,1},{3,2},{4,3},{5,4},{6,5},{7,6},{8,7},{9,8},{10,9},{11,1... | collective-permute-start | bytes 258056 | tf_op jit(solution)/shard_map/ppermute | solution.py:633
  65.1 0.7 copy-start.20
  65.8 19.3 %collective-permute-start.6 = (bf16[16,128]{1,0:T(8,128)(2,1)}, bf16[16,128]{1,0:T(8,128)(2,1)S(1)}, u32[]{:S(2)}, u32[]{:S(2)}) collective-permute-start(bf16[16,128]{1,0:T(8,128)(2,1)} %get-tuple-element.33), channel_id=1, source_target_pairs={{0,1},{1,2},{2,3},{3,4},{4,5},{5,6},{6,7},{7,8},{8,9},{9,10},{10,1... | collective-permute-start | bytes 12296 | tf_op jit(solution)/shard_map/ppermute | solution.py:682
  69.8 15.3 %collective-permute-start.7 = (bf16[16,128]{1,0:T(8,128)(2,1)}, bf16[16,128]{1,0:T(8,128)(2,1)}, u32[]{:S(2)}, u32[]{:S(2)}) collective-permute-start(bf16[16,128]{1,0:T(8,128)(2,1)} %get-tuple-element.34), channel_id=1, source_target_pairs={{1,0},{2,1},{3,2},{4,3},{5,4},{6,5},{7,6},{8,7},{9,8},{10,9},{11,1... | collective-permute-start | bytes 12296 | tf_op jit(solution)/shard_map/ppermute | solution.py:681
  73.8 1.1 copy-start.1
  74.9 1.0 copy-start.5
  76.0 0.8 copy-start.8
  76.7 0.9 copy-start.24
  77.6 0.9 copy-start.26
  78.5 48.1 %copy-start.7 = (bf16[8,8,1024]{2,1,0:T(8,128)(2,1)S(1)}, bf16[8,8,1024]{2,1,0:T(8,128)(2,1)}, u32[]{:S(2)}) copy-start(bf16[8,8,1024]{2,1,0:T(8,128)(2,1)} %copy-done.6) | copy-start | bytes 393220
  85.1 42.4 %copy-start.17 = (f32[22,8,128]{2,1,0:T(8,128)}, f32[22,8,128]{2,1,0:T(8,128)S(1)}, u32[]{:S(2)}) copy-start(f32[22,8,128]{2,1,0:T(8,128)S(1)} %get-tuple-element.28.refs_2_) | copy-start | bytes 270340
  85.1 51.8 %copy-start.3 = (f32[4,72,512]{2,1,0:T(8,128)S(1)}, f32[4,72,512]{2,1,0:T(8,128)}, u32[]{:S(2)}) copy-start(f32[4,72,512]{2,1,0:T(8,128)} %a_hbm.3) | copy-start | bytes 1769476
  85.2 0.9 copy-start.11
  86.1 0.8 copy-start.15
  86.9 0.7 copy-start.21
  87.6 0.7 copy-start.37
  88.9 53.4 %copy-start.9 = (bf16[80,240]{1,0:T(8,128)(2,1)S(1)}, bf16[80,240]{1,0:T(8,128)(2,1)}, u32[]{:S(2)}) copy-start(bf16[80,240]{1,0:T(8,128)(2,1)} %pad_maximum_fusion.mix_ref.refs_3_) | copy-start | bytes 115204
  88.9 53.4 %copy-start.12 = (f32[128,128]{1,0:T(8,128)S(1)}, f32[128,128]{1,0:T(8,128)}, u32[]{:S(2)}) copy-start(f32[128,128]{1,0:T(8,128)} %copy-done.10) | copy-start | bytes 196612
  88.9 53.4 %copy-start.16 = (f32[80,80]{1,0:T(8,128)S(1)}, f32[80,80]{1,0:T(8,128)}, u32[]{:S(2)}) copy-start(f32[80,80]{1,0:T(8,128)} %refs_4_.3) | copy-start | bytes 76804
  88.9 53.4 %copy-start.22 = (bf16[5,16,128]{2,1,0:T(8,128)(2,1)S(1)}, bf16[5,16,128]{2,1,0:T(8,128)(2,1)}, u32[]{:S(2)}) copy-start(bf16[5,16,128]{2,1,0:T(8,128)(2,1)} %copy-done.20) | copy-start | bytes 61444
  127.5 26.3 %all-to-all-start.3 = ((f32[8,8,256]{2,1,0:T(8,128)}), f32[8,8,256]{2,1,0:T(8,128)S(1)}, u32[]{:S(2)}, u32[]{:S(2)}) async-start(f32[8,8,256]{2,1,0:T(8,128)} %bitcast.13), calls=%async_computation.3 | async-start | bytes 131072 | tf_op jit(solution)/shard_map/all_to_all | solution.py:705
  137.0 0.8 copy-start.28
  137.8 0.8 copy-start.31
  138.6 0.8 copy-start.33
  142.3 0.9 copy-start.18
  (3 other events, 1.9 us)
where the time goes:
time: 156 us; the launch traced here: 155 us
  starting transfers between devices  42.3 us (27%)
  Pallas kernels  41.1 us (26%)
  blocking collectives  37.6 us (24%)
  local copies, waits for them, and re-layouts  21.6 us (14%)
  waiting for transfers between devices  8.7 us (6%)
  other arithmetic  2.16 us (1%)
    all_to_all x1, blocking collectives, on_device(): back = lax.all_to_all(terms, 'col', 0, 0, tiled=True)  27 us
    unnamed x83, local copies, waits for them, and re-layouts  19.4 us
    all_to_all x1, starting transfers between devices, on_device(): arrived = lax.all_to_all(chosen, 'col', 0, 0, tiled=True)  13.1 us
    pallas_call x1, Pallas kernels, on_device(): call(functools.partial(tracer_body, 0, True), (shape(flat.shape), shape((...  10.7 us
    all_to_all x1, blocking collectives, on_device(): row_blocks = lax.all_to_all(payload, 'row', 0, 0, tiled=True)  10.6 us
    pallas_call x1, Pallas kernels, on_device(): call(functools.partial(tracer_body, 1, False), shape(flat.shape), 'salini...  10.6 us
    all_to_all x1, starting transfers between devices, on_device(): home = lax.all_to_all(sums, 'row', 0, 0, tiled=True)  9.47 us
    all_to_all x1, waiting for transfers between devices, on_device(): arrived = lax.all_to_all(chosen, 'col', 0, 0, tiled=True)  7.1 us
  transfers between devices with their start and end apart: 10, of which 2 were waited for; matrix products, arithmetic and copies ran while one was open for 3% of the time, Pallas kernels for 17%

commit v1 on v0

v1 whole, which is shorter than its diff:
```python
import functools

import jax
import jax.numpy as jnp
import numpy as np
from jax import lax
from jax.experimental import pallas as pl
from jax.experimental.pallas import tpu as pltpu
from jax.sharding import PartitionSpec as P

STEPS = 6
HALO = 6
ROWS = 8
EXT = ROWS + 2 * HALO
REACH = 2 * HALO
GROUP = 3
EDGES = -(-EXT // GROUP)
TILES = EXT + EDGES
SIDE = 2 * (HALO + REACH)
LANES = 128
WIDE = 256
HIGHEST = lax.Precision.HIGHEST
MIB = 1024 * 1024

heat_rate = 0.5
vapour_rate = 0.5
drag_rate = 0.3
saturation = 0.6
flux_gains = (0.3, 0.3, -0.3, -0.3)
diffusion = 0.15
surface_gain = (-0.3, 0.3)
surface_push = 0.3
current_drag = 0.1
coriolis = 0.2
turn = np.array([[1.0 - current_drag, coriolis], [-coriolis, 1.0 - current_drag]])

f32 = jnp.float32
bf16 = jnp.bfloat16
VMEM = pl.BlockSpec(memory_space=pltpu.VMEM)
HBM = pl.BlockSpec(memory_space=pltpu.HBM)
SMEM = pl.BlockSpec(memory_space=pltpu.SMEM)


def call(body, out_shape, name, in_specs, out_specs=None, scratch=(), aliases=None, limit=8, micros=1):
    if out_specs is None:
        out_specs = jax.tree.map(lambda _: VMEM, out_shape)
    return pl.pallas_call(
        body,
        out_shape=out_shape,
        in_specs=in_specs,
        out_specs=out_specs,
        scratch_shapes=list(scratch),
        input_output_aliases=aliases or {},
        compiler_params=pltpu.CompilerParams(vmem_limit_bytes=limit * MIB),
        cost_estimate=pl.CostEstimate(
            flops=int(micros * 1e9), bytes_accessed=int(micros * 3e6), transcendentals=0
        ),
        name=name,
    )


def shape(dims, dtype=f32):
    return jax.ShapeDtypeStruct(dims, dtype)


def exact(a, b):
    return jnp.dot(a, b, precision=HIGHEST, preferred_element_type=f32)


def times(a, b):
    return jnp.dot(a, b, preferred_element_type=f32)


def times_rows(a, b):
    return lax.dot_general(a, b, (((1,), (1,)), ((), ())), preferred_element_type=f32)


def iota(dims, axis):
    return lax.broadcasted_iota(jnp.int32, dims, axis)


def one_hot(condition):
    return condition.astype(f32).astype(bf16)


def halves(x):
    high = x.astype(bf16)
    return high, (x - high.astype(f32)).astype(bf16)


def moves():
    pack = np.zeros((EXT, LANES, 2, LANES), np.float32)
    spread = np.zeros((2, LANES, EDGES, LANES), np.float32)
    own = np.zeros((GROUP, LANES, LANES), np.float32)
    for r in range(EXT):
        at = SIDE * (r // EDGES)
        for c in range(HALO):
            pack[r, c, 0, HALO * r + c] = 1
            pack[r, LANES - HALO + c, 1, HALO * r + c] = 1
            spread[0, HALO * r + c, r % EDGES, at + SIDE - HALO + c] = 1
            spread[1, HALO * r + c, r % EDGES, at + c] = 1
    for k in range(GROUP):
        for c in range(REACH):
            own[k, c, SIDE * k + HALO + c] = 1
            own[k, LANES - REACH + c, SIDE * k + HALO + REACH + c] = 1
    return (
        jnp.asarray(pack.reshape(EXT * LANES, 2 * LANES), bf16),
        jnp.asarray(spread.reshape(2 * LANES, EDGES * LANES), bf16),
        jnp.asarray(own.reshape(GROUP * LANES, LANES), bf16),
    )


def flux_body(table_ref, a_ref, m_ref, sst_ref, pay_ref, g_ref, top_ref, edge_ref, block_ref):
    levels = m_ref.shape[0]
    bottom = levels - 1
    power = {1: m_ref[...]}
    power[2] = exact(power[1], power[1])
    power[3] = exact(power[1], power[2])
    power[4] = exact(power[2], power[2])
    power[5] = exact(power[2], power[3])
    power[6] = exact(power[3], power[3])
    first = (iota((1, levels), 1) == bottom).astype(f32)
    rows = [first] + [power[n][bottom:, :] for n in range(1, STEPS)]
    rows = jnp.concatenate(rows + [jnp.zeros((8 - STEPS, levels), f32)], axis=0)
    row_high, row_low = halves(rows)
    both = jnp.concatenate([row_high.astype(f32), row_low.astype(f32)], axis=0).astype(bf16)
    top_ref[...] = power[6]
    lane = iota((levels, 8), 1)
    edge = jnp.zeros((levels, 8), f32)
    for n in range(STEPS):
        edge = jnp.where(lane == n, power[STEPS - n][:, bottom:], edge)
    edge_ref[...] = edge
    base = []
    for v in range(4):
        high, low = halves(a_ref[v])
        one = times(both, high)
        base.append(one[:8] + one[8:] + times(row_high, low))
    corner = {n: power[n][bottom:, bottom:] for n in range(1, STEPS)}
    sst = sst_ref[...]
    gained = []
    fluxes = []
    east, north = jnp.zeros_like(sst), jnp.zeros_like(sst)
    for n in range(STEPS):
        now = []
        for v in range(4):
            value = base[v][n : n + 1]
            for k in range(n):
                value = value + corner[n - k] * gained[k][v]
            now.append(value)
        wind = jnp.sqrt(now[2] * now[2] + now[3] * now[3] + 1.0)
        flux = (
            heat_rate * wind * (sst - now[0]),
            vapour_rate * wind * (saturation * sst - now[1]),
            drag_rate * wind * now[2],
            drag_rate * wind * now[3],
        )
        fluxes.append(flux)
        gained.append([flux_gains[v] * flux[v] for v in range(4)])
        east, north = (
            turn[0, 0] * east + turn[0, 1] * north + flux[2],
            turn[1, 0] * east + turn[1, 1] * north + flux[3],
        )
    blank = [jnp.zeros_like(sst)] * (8 - STEPS)
    for v in range(4):
        g_ref[v] = jnp.concatenate([gained[n][v] for n in range(STEPS)] + blank, axis=0)
    pairs = [(fluxes[n][0], fluxes[n][1]) for n in range(STEPS)] + [(east, north)]
    block = iota((8, LANES), 0)
    left = iota((8, LANES), 1) < 64
    even = block % 2 == 0
    for i, pair in enumerate(pairs):
        parts = []
        for side in range(2):
            spread = jnp.zeros((8, LANES), f32)
            for q in range(4):
                tile = jnp.broadcast_to(pair[side][:, q * LANES : (q + 1) * LANES], (8, LANES))
                spread = jnp.where(block // 2 == q, tile, spread)
            parts.append(jnp.where(even == (side == 0), spread, pltpu.roll(spread, 64, 1)))
        block_ref[pl.ds(i, 8, stride=8), :] = jnp.where(left, parts[0], parts[1])
    block_ref[pl.ds(7, 8, stride=8), :] = jnp.zeros((8, LANES), f32)
    for d in range(pay_ref.shape[0] // 16):
        chosen = []
        for side in range(2):
            at = jnp.maximum(table_ref[side, d], 0) * 8
            chosen.append(block_ref[pl.ds(pl.multiple_of(at, 8), 8), :])
        pay_ref[16 * d : 16 * d + 16, :] = jnp.concatenate(chosen, axis=0).astype(bf16)


def atmosphere_body(a_ref, g_ref, top_ref, edge_ref, out_ref):
    for v in range(4):
        out_ref[v] = exact(top_ref[...], a_ref[v]) + exact(edge_ref[...], g_ref[v])


def finish_body(table_ref, in_ref, out_ref):
    rows = in_ref.shape[0]
    block, lane = iota((8, rows), 0), iota((8, rows), 1)
    ones = []
    for side in range(2):
        named = table_ref[side : side + 1, :] == block
        for f in range(3):
            ones.append((named & (lane % 4 == f)).astype(f32))
    ones = jnp.concatenate(ones, axis=0).astype(bf16)
    high, low = halves(in_ref[...])
    sums = times(ones, high) + times(ones, low)
    left = iota((1, LANES), 1) < 64
    for f in range(3):
        low = sums[8 * f : 8 * f + 8] + pltpu.roll(sums[24 + 8 * f : 32 + 8 * f], 64, 1)
        high = pltpu.roll(low, 64, 1)
        for q in range(4):
            out_ref[f : f + 1, q * LANES : (q + 1) * LANES] = jnp.where(
                left, low[2 * q : 2 * q + 1], high[2 * q + 1 : 2 * q + 2]
            )


def cells_body(w_ref, out_ref, t_ref, low_ref, high_ref):
    left = iota((16, LANES), 1) < 64
    tiles = w_ref.shape[1] // LANES
    for i in range(tiles):
        t_ref[i * 64 : (i + 1) * 64] = w_ref[:, i * LANES : (i + 1) * LANES].astype(f32)
    for i in range(tiles):
        k = [t_ref[pl.ds(i * 64 + s, 16, stride=4), :] for s in range(4)]
        moved = [pltpu.roll(x, 64, 1) for x in k]
        low_ref[pl.ds(2 * i, 16, stride=64), :] = jnp.where(left, k[0], moved[1])
        high_ref[pl.ds(2 * i, 16, stride=64), :] = jnp.where(left, k[2], moved[3])
        low_ref[pl.ds(2 * i + 1, 16, stride=64), :] = jnp.where(left, moved[0], k[1])
        high_ref[pl.ds(2 * i + 1, 16, stride=64), :] = jnp.where(left, moved[2], k[3])
    out_ref[:, :LANES] = low_ref[...].astype(bf16)
    out_ref[:, LANES:] = high_ref[...].astype(bf16)


def rows_body(x_ref, v_ref, wet_ref, z_ref, f_ref):
    levels = x_ref.shape[1] // ROWS
    for t in range(2):
        f_ref[t] = v_ref[t].astype(f32)
    for r in range(ROWS):
        for t in range(2):
            z_ref[r, (2 + t) * levels : (3 + t) * levels, :] = f_ref[
                t, pl.ds(r, levels, stride=ROWS), :
            ].astype(bf16)
        wet = jnp.broadcast_to(wet_ref[r : r + 1, :].astype(f32), (16, LANES))
        z_ref[r, 4 * levels :, :] = wet.astype(bf16)
    for r in range(ROWS):
        for t in range(2):
            z_ref[r, t * levels : (t + 1) * levels, :] = x_ref[
                t, pl.ds(r, levels, stride=ROWS), :
            ].astype(bf16)


def widened(before_ref, own_ref, after_ref):
    rows = [before_ref[r] for r in range(HALO)]
    rows += [own_ref[r] for r in range(ROWS)]
    return rows + [after_ref[r] for r in range(HALO)]


def pack_body(before_ref, z_ref, after_ref, pack_ref, first_ref, last_ref):
    rows = widened(before_ref, z_ref, after_ref)
    packed = times(jnp.concatenate(rows, axis=1), pack_ref[...]).astype(bf16)
    first_ref[...] = packed[:, :LANES]
    last_ref[...] = packed[:, LANES:]


def forcing_rows(f_ref, before_ref, after_ref):
    blank = [jnp.zeros((16, LANES), bf16)]
    rows = blank + [before_ref[r] for r in range(HALO - 1)]
    rows += [f_ref[16 * r : 16 * r + 16].astype(bf16) for r in range(ROWS)]
    return rows + [after_ref[r] for r in range(HALO - 1)] + blank


def pack_forcing_body(f_ref, before_ref, after_ref, pack_ref, first_ref, last_ref):
    rows = forcing_rows(f_ref, before_ref, after_ref)
    packed = times(jnp.concatenate(rows, axis=1), pack_ref[...]).astype(bf16)
    first_ref[...] = packed[:, :LANES]
    last_ref[...] = packed[:, LANES:]


def edge_tile(g, rows, sides, spread_ref, own_ref):
    mine = [rows[r] for r in range(g, EXT, EDGES)]
    return times(jnp.concatenate(mine, axis=1), own_ref[: len(mine) * LANES, :]) + times(
        sides, spread_ref[:, g * LANES : (g + 1) * LANES]
    )


def around(idx, get):
    here = get(idx)
    if idx < EXT:
        north, south = get(idx + 1), get(idx - 1)
    else:
        north = get(idx + 1) if idx + 1 < TILES else pltpu.roll(get(EXT), LANES - SIDE, 1)
        south = get(idx - 1) if idx > EXT else pltpu.roll(get(TILES - 1), SIDE, 1)
    return here, pltpu.roll(here, LANES - 1, 1), pltpu.roll(here, 1, 1), north, south


def ocean_step(n, x_ref, coef_ref, mix_ref, cat_ref, store, force=None):
    levels = mix_ref.shape[0]
    tiles = list(range(n + 1, EXT - 1 - n)) + list(range(EXT, TILES))
    first = iota((8, LANES), 0) == 0
    for lo in range(0, len(tiles), 4):
        some = tiles[lo : lo + 4]
        slot = (lo // 4) % 2
        for at in range(0, levels, 16):
            for i, idx in enumerate(some):
                here, east, west, north, south = around(idx, lambda j: x_ref[j, at : at + 16, :])
                stepped = (
                    coef_ref[0, idx, at : at + 16, :] * here
                    + (coef_ref[1, idx, at : at + 16, :] * east
                       + coef_ref[2, idx, at : at + 16, :] * west)
                    + (coef_ref[3, idx, at : at + 16, :] * north
                       + coef_ref[4, idx, at : at + 16, :] * south)
                )
                if force is not None and at == 0:
                    top = stepped[:8] + jnp.where(first, force(idx), 0.0)
                    stepped = jnp.concatenate([top, stepped[8:]], axis=0)
                upper, lower = halves(stepped)
                cols = slice(i * LANES, (i + 1) * LANES)
                cat_ref[slot, at : at + 16, cols] = upper
                cat_ref[slot, levels + at : levels + at + 16, cols] = upper
                cat_ref[slot, 2 * levels + at : 2 * levels + at + 16, cols] = lower
        mixed = times(mix_ref[...], cat_ref[slot, :, : len(some) * LANES])
        for i, idx in enumerate(some):
            store(idx, mixed[:, i * LANES : (i + 1) * LANES])


def coefficient_body(
    before_ref, z_ref, after_ref, west_ref, east_ref, x_ref, mix_ref, spread_ref, own_ref,
    coef_ref, x1_ref, salt_ref, wet_ref, x0_ref, near_ref, edge_ref, cat_ref,
):
    levels = mix_ref.shape[0]
    rows = widened(before_ref, z_ref, after_ref)
    sides = jnp.concatenate([east_ref[...], west_ref[...]], axis=1)
    for g in range(EDGES):
        edge_ref[g] = edge_tile(g, rows, sides, spread_ref, own_ref).astype(bf16)

    def of(idx, at):
        if idx >= EXT:
            return edge_ref[idx - EXT, at, :].astype(f32)
        if idx < HALO:
            return before_ref[idx, at, :].astype(f32)
        if idx < HALO + ROWS:
            return z_ref[idx - HALO, at, :].astype(f32)
        return after_ref[idx - HALO - ROWS, at, :].astype(f32)

    wets = [of(idx, pl.ds(4 * levels, 16))[:8] for idx in range(TILES)]
    for idx in range(TILES):
        wet_ref[idx] = wets[idx]
    inner = list(range(1, EXT - 1)) + list(range(EXT, TILES))
    for idx in inner:
        here, *near = around(idx, lambda j: wets[j])
        for s in range(4):
            near_ref[s, idx] = here * near[s]

    def part(c, carry):
        at = pl.multiple_of(c * 16, 16)
        here_at = pl.ds(at, 16)
        for idx in inner:
            along = 0.5 * of(idx, pl.ds(2 * levels + at, 16))
            across = 0.5 * of(idx, pl.ds(3 * levels + at, 16))
            near = []
            for s in range(4):
                one = near_ref[s, idx]
                near.append(jnp.concatenate([one, one], axis=0))
            c_east = near[0] * (diffusion - along)
            c_west = near[1] * (diffusion + along)
            c_north = near[2] * (diffusion - across)
            c_south = near[3] * (diffusion + across)
            coef_ref[0, idx, here_at, :] = 1.0 - ((c_east + c_west) + (c_north + c_south))
            coef_ref[1, idx, here_at, :] = c_east
            coef_ref[2, idx, here_at, :] = c_west
            coef_ref[3, idx, here_at, :] = c_north
            coef_ref[4, idx, here_at, :] = c_south
        for t, to_ref in enumerate((x0_ref, salt_ref)):
            for idx in range(TILES):
                if not HALO <= idx < HALO + ROWS:
                    to_ref[idx, here_at, :] = of(idx, pl.ds(t * levels + at, 16))
        return carry

    lax.fori_loop(0, levels // 16, part, 0)
    for t, to_ref in enumerate((x0_ref, salt_ref)):
        for r in range(ROWS):
            to_ref[HALO + r] = x_ref[t, pl.ds(r, levels, stride=ROWS), :]

    def store(idx, value):
        x1_ref[idx] = value

    ocean_step(0, x0_ref, coef_ref, mix_ref, cat_ref, store)


def remap_body(arrival_ref, in_ref, w_ref, u_ref, wet_ref, f_ref, up_ref, down_ref, u_out_ref):
    def pick(j):
        t = arrival_ref[0, j]
        at = pl.multiple_of((t >> 1) * 16, 16)
        window = in_ref[pl.ds(at, 16), :].astype(f32)
        return jnp.where((t & 1) == 1, window[8:], window[:8])

    left = iota((8, LANES), 1) < 64
    left_two = iota((16, LANES), 1) < 64
    for r in range(ROWS):
        sources = []
        for side in range(2):
            even, odd = [], []
            for pair in range(2):
                j = 4 * (2 * r + side) + 2 * pair
                one, two = pick(j), pick(j + 1)
                even.append(jnp.where(left, one, pltpu.roll(two, 64, 1)))
                odd.append(jnp.where(left, pltpu.roll(one, 64, 1), two))
            sources.append(jnp.concatenate(even, axis=1))
            sources.append(jnp.concatenate(odd, axis=1))
        sources = jnp.concatenate(sources, axis=0).astype(bf16)
        product = times_rows(sources, w_ref[r * LANES : (r + 1) * LANES, :])
        forcing = jnp.where(left_two, product[:16], product[16:])
        f_ref[16 * r : 16 * r + 16, :] = forcing
        if r < HALO - 1:
            down_ref[r] = forcing.astype(bf16)
        if r >= ROWS - HALO + 1:
            up_ref[r - (ROWS - HALO + 1)] = forcing.astype(bf16)
    whole = np.linalg.matrix_power(turn, STEPS)
    wet = wet_ref[...].astype(f32)
    push = [surface_push * f_ref[pl.ds(6 + 8 * v, ROWS, stride=16), :] for v in range(2)]
    for v in range(2):
        ahead = float(whole[v, 0]) * u_ref[0] + float(whole[v, 1]) * u_ref[1] + push[v]
        u_out_ref[v] = u_ref[v] + wet * (ahead - u_ref[v])


def returned_rows(fields, w_ref, place, rows):
    blocks = 2 * ROWS
    block, lane = iota((blocks, LANES), 0), iota((blocks, LANES), 1)
    spread = []
    for field in fields:
        parts = []
        for r in range(ROWS):
            mine = block == 2 * r + (lane >= 64).astype(jnp.int32)
            parts.append(jnp.where(mine, field[r : r + 1], 0.0))
        spread.append(jnp.concatenate(parts, axis=1))
    terms = times(jnp.concatenate(spread, axis=0).astype(bf16), w_ref[...])
    high_parts, low_parts, ones = [], [], []
    target = iota((rows, LANES), 0)
    for f in range(len(fields)):
        mine = terms[f * blocks : (f + 1) * blocks]
        pieces = []
        for half in range(2):
            for k in range(4):
                piece = mine[:, (k // 2) * LANES : (k // 2 + 1) * LANES]
                if k % 2 != half:
                    piece = pltpu.roll(piece, 64, 1)
                pieces.append(jnp.where((lane >= 64) == (half == 1), piece, 0.0))
        high, low = halves(jnp.concatenate(pieces, axis=0))
        high_parts.append(high)
        low_parts.append(low)
        ones.append(one_hot(target == place + f))
    return times(
        jnp.concatenate(ones + ones, axis=1), jnp.concatenate(high_parts + low_parts, axis=0)
    )


def tracer_body(t, *refs):
    x_ref, coef_ref, wet_ref, mix_ref, f_ref, before_ref, after_ref, west_ref, east_ref = refs[:9]
    spread_ref, own_ref = refs[9:11]
    if t == 0:
        column_ref, w_ref, place_ref, u_ref, out_ref, send_ref = refs[11:17]
        one_ref, two_ref, force_ref, cat_ref, sst_ref = refs[17:]
    else:
        out_ref, one_ref, two_ref, force_ref, cat_ref = refs[11:]
    levels = mix_ref.shape[0]
    rows = forcing_rows(f_ref, before_ref, after_ref)
    sides = jnp.concatenate([east_ref[...], west_ref[...]], axis=1)
    for idx in range(1, TILES):
        if idx == EXT - 1:
            continue
        if HALO <= idx < HALO + ROWS:
            row = 16 * (idx - HALO)
            forcing = f_ref[row : row + 16, :]
        elif idx < EXT:
            forcing = rows[idx].astype(f32)
        else:
            forcing = edge_tile(idx - EXT, rows, sides, spread_ref, own_ref)
        force_ref[idx] = surface_gain[t] * wet_ref[idx] * forcing[8 * t : 8 * t + 8]
    if t == 0:
        column = jnp.broadcast_to(column_ref[:, 0:1], (levels, LANES))
        for idx in range(1, TILES):
            if idx != EXT - 1:
                one_ref[idx] = x_ref[idx] + column * force_ref[idx, 0:1, :]
        old, new = one_ref, two_ref
    else:
        old, new = x_ref, one_ref
    for n in range(1 if t == 0 else 0, STEPS):

        def store(idx, value, new=new):
            new[idx] = value

        def force(idx, n=n):
            return force_ref[idx, n : n + 1, :]

        ocean_step(n, old, coef_ref, mix_ref, cat_ref, store, force)
        if t == 1 and n == 0:
            old, new = one_ref, two_ref
        else:
            old, new = new, old
    lane = iota((16, LANES), 1)
    for r in range(ROWS):
        idx = HALO + r
        at = SIDE * (idx // EDGES) + HALO
        edge = EXT + idx % EDGES
        for lo in range(0, levels, 16):
            side = old[edge, lo : lo + 16, :]
            value = jnp.where(
                lane < HALO, pltpu.roll(side, (LANES - at) % LANES, 1), old[idx, lo : lo + 16, :]
            )
            here = at + REACH + HALO
            value = jnp.where(
                lane >= LANES - HALO, pltpu.roll(side, (LANES - HALO - here) % LANES, 1), value
            )
            out_ref[pl.ds(lo * ROWS + r, 16, stride=ROWS), :] = value
            if t == 0 and lo == 0:
                sst_ref[r : r + 1, :] = value[0:1]
    if t == 0:
        fields = [sst_ref[...], u_ref[0], u_ref[1]]
        fields = [field.astype(bf16).astype(f32) for field in fields]
        send_ref[...] = returned_rows(fields, w_ref, place_ref[...], send_ref.shape[0])


def neighbours(size):
    up = [(i, i + 1) for i in range(size - 1)]
    return up, [(j, i) for i, j in up]


def on_device(
    atmosphere_level_state,
    atmosphere_mixing_map,
    sea_surface_temps,
    tracers,
    currents,
    ocean_advect_velocity,
    ocean_mixing_map,
    ocean_cell_mask,
    remap_weight_tiles,
    outgoing_block_table,
    arrival_slot_table,
):
    band = ("row", "col")
    peers = lax.axis_size(band)
    levels = tracers.shape[1]
    air_levels, air_columns = atmosphere_level_state.shape[1:]
    rows_axis = ("comp", "row")
    up, down = neighbours(lax.axis_size(rows_axis))
    right, leftward = neighbours(lax.axis_size("col"))
    pack_moves, spread_moves, own_moves = moves()

    table = outgoing_block_table.reshape(peers, 2).T
    arrival = arrival_slot_table.reshape(1, 64)
    by_k = arrival.reshape(2 * ROWS, 4).T.reshape(1, 64)
    place = jnp.concatenate(
        [jnp.where(by_k % 2 == side, (by_k // 2) * 4, -64) for side in range(2)], axis=1
    )

    payload, gained, top, edge = call(
        flux_body,
        (
            shape((peers * 16, LANES), bf16),
            shape((4, 8, air_columns)),
            shape((air_levels, air_levels)),
            shape((air_levels, 8)),
        ),
        "fluxes",
        [SMEM, VMEM, VMEM, VMEM],
        scratch=[pltpu.VMEM((64, LANES), f32)],
        micros=2,
    )(table, atmosphere_level_state, atmosphere_mixing_map, sea_surface_temps[None])
    arrived = lax.all_to_all(payload, band, 0, 0, tiled=True)

    flat = tracers.reshape(2, levels * ROWS, LANES)
    depth = 4 * levels + 16
    z = call(
        rows_body,
        shape((ROWS, depth, LANES), bf16),
        "rows",
        [VMEM] * 3,
        scratch=[pltpu.VMEM(flat.shape, f32)],
    )(flat, ocean_advect_velocity.reshape(flat.shape), ocean_cell_mask)
    before = lax.ppermute(z[ROWS - HALO :], rows_axis, up)
    after = lax.ppermute(z[:HALO], rows_axis, down)
    edge_shape = shape((depth, LANES), bf16)
    first, last = call(pack_body, (edge_shape, edge_shape), "pack", [VMEM] * 4)(
        before, z, after, pack_moves
    )
    east_in = lax.ppermute(first, "col", leftward)
    west_in = lax.ppermute(last, "col", right)
    cells = call(
        cells_body,
        shape((ROWS * LANES, WIDE), bf16),
        "cells",
        [VMEM],
        scratch=[
            pltpu.VMEM((32 * 64, LANES), f32),
            pltpu.VMEM((ROWS * LANES, LANES), f32),
            pltpu.VMEM((ROWS * LANES, LANES), f32),
        ],
    )(remap_weight_tiles.reshape(64, 4096))
    rounded = lax.reduce_precision(ocean_mixing_map, 8, 7)
    upper, lower = rounded.astype(bf16), (ocean_mixing_map - rounded).astype(bf16)
    mix = jnp.concatenate([upper, lower, upper], axis=1)
    wide = (TILES, levels, LANES)
    cat = pltpu.VMEM((2, 3 * levels, 4 * LANES), bf16)
    coef, x1, salt, wet = call(
        coefficient_body,
        (shape((5, *wide)), shape(wide), shape(wide), shape((TILES, 8, LANES))),
        "coefficients",
        [VMEM] * 9,
        scratch=[
            pltpu.VMEM(wide, f32),
            pltpu.VMEM((4, TILES, 8, LANES), f32),
            pltpu.VMEM((EDGES, depth, LANES), bf16),
            cat,
        ],
        limit=24,
        micros=4,
    )(before, z, after, west_in, east_in, flat, mix, spread_moves, own_moves)
    arrived, coef = lax.optimization_barrier((arrived, coef))

    edge_rows = shape((HALO - 1, 16, LANES), bf16)
    forcing, send_up, send_down, ocean_currents = call(
        remap_body,
        (shape((ROWS * 16, LANES)), edge_rows, edge_rows, shape(currents.shape)),
        "remap",
        [SMEM] + [VMEM] * 4,
    )(arrival, arrived, cells, currents, ocean_cell_mask)
    f_before = lax.ppermute(send_up, rows_axis, up)
    f_after = lax.ppermute(send_down, rows_axis, down)
    strip = shape((16, LANES), bf16)
    f_first, f_last = call(pack_forcing_body, (strip, strip), "pack_forcing", [VMEM] * 4)(
        forcing, f_before, f_after, pack_moves
    )
    f_east = lax.ppermute(f_first, "col", leftward)
    f_west = lax.ppermute(f_last, "col", right)

    shared = (coef, wet, mix, forcing, f_before, f_after, f_west, f_east, spread_moves, own_moves)
    scratch = [
        pltpu.VMEM(wide, f32),
        pltpu.VMEM(wide, f32),
        pltpu.VMEM((TILES, 8, LANES), f32),
        cat,
    ]
    warm, terms = call(
        functools.partial(tracer_body, 0),
        (shape(flat.shape[1:]), shape((peers * 4, LANES))),
        "temperature",
        [VMEM] * 15,
        scratch=scratch + [pltpu.VMEM((ROWS, LANES), f32)],
        limit=24,
        micros=6,
    )(x1, *shared, ocean_mixing_map, cells, place, ocean_currents)
    home = lax.all_to_all(terms, band, 0, 0, tiled=True)
    gained, terms = lax.optimization_barrier((gained, terms))
    atm_final = call(
        atmosphere_body,
        shape(atmosphere_level_state.shape),
        "atmosphere",
        [VMEM] * 4,
        micros=3,
    )(atmosphere_level_state, gained, top, edge)
    cold = call(
        functools.partial(tracer_body, 1),
        shape(flat.shape[1:]),
        "salinity",
        [VMEM] * 11,
        scratch=scratch,
        limit=24,
        micros=6,
    )(salt, *shared)
    returned = call(finish_body, shape((3, air_columns)), "finish", [VMEM, VMEM])(
        jnp.repeat(table, 4, axis=1), home
    )
    ocean_tracers = jnp.stack([warm, cold]).reshape(tracers.shape)
    return (atm_final, ocean_tracers, ocean_currents, returned)


def solution(mesh):
    return jax.shard_map(
        on_device,
        mesh=mesh,
        in_specs=(
            P(None, None, ("comp", "row", "col")),
            P(),
            P(("comp", "row", "col")),
            P(None, None, ("comp", "row"), "col"),
            P(None, ("comp", "row"), "col"),
            P(None, None, ("comp", "row"), "col"),
            P(),
            P(("comp", "row"), "col"),
            P("comp", ("row", "col"), None, None),
            P("comp", ("row", "col"), None, None),
            P("comp", ("row", "col"), None),
        ),
        out_specs=(
            P(None, None, ("comp", "row", "col")),
            P(None, None, ("comp", "row"), "col"),
            P(None, ("comp", "row"), "col"),
            P(None, ("comp", "row", "col")),
        ),
        check_vma=False,
    )
```

time: 156 us -> 127 us (0.81)
  the two profiles are of different devices: /device:TPU:11 before, /device:TPU:1 now
where the time goes in v1:
time: 127 us; the launch traced here: 126 us
  starting transfers between devices  63 us (50%)
  local copies, waits for them, and re-layouts  21.8 us (17%)
  Pallas kernels  21.1 us (17%)
  waiting for transfers between devices  17.5 us (14%)
  other arithmetic  1.79 us (1%)
    all_to_all x1, starting transfers between devices, on_device(): home = lax.all_to_all(terms, band, 0, 0, tiled=True)  25.6 us
    unnamed x67, local copies, waits for them, and re-layouts  20.5 us
    all_to_all x1, starting transfers between devices, on_device(): arrived = lax.all_to_all(payload, band, 0, 0, tiled=True)  13.4 us
    ppermute x1, starting transfers between devices, on_device(): after = lax.ppermute(z[:HALO], rows_axis, down)  5.51 us
    ppermute x1, starting transfers between devices, on_device(): before = lax.ppermute(z[ROWS - HALO:], rows_axis, up)  4.58 us
    pallas_call x1, Pallas kernels, on_device(): call(functools.partial(tracer_body, 0), (shape(flat.shape[1:]), shape((pe...  4.58 us
    all_to_all x1, waiting for transfers between devices, on_device(): home = lax.all_to_all(terms, band, 0, 0, tiled=True)  4.54 us
    ppermute x1, waiting for transfers between devices, on_device(): west_in = lax.ppermute(last, 'col', right)  4.34 us
  transfers between devices with their start and end apart: 10, of which 5 were waited for; matrix products, arithmetic and copies ran while one was open for 2% of the time, Pallas kernels for 11%

profile of v1, /device:TPU:1, one launch (start us, length us, event | category | flops | bytes accessed | tf_op | source)
XLA Modules:
  0.0 126.3 jit_solution(16128339717724488567)
XLA Ops:
  0.6 1.1 copy-done.2
  1.7 1.0 copy-done.6
  2.7 0.7 copy-done.9
  3.4 0.2 rows.1.z_ref
  3.7 0.9 fusion.3
  4.6 4.6 %collective-permute-start = (bf16[6,336,128]{2,1,0:T(8,128)(2,1)}, bf16[6,336,128]{2,1,0:T(8,128)(2,1)S(1)}, u32[]{:S(2)}, u32[]{:S(2)}) collective-permute-start(bf16[6,336,128]{2,1,0:T(8,128)(2,1)} %get-tuple-element.50), channel_id=1, source_target_pairs={{0,16},{16,32},{32,48},{48,64},{64,80},{80,96},{96,112},{112,128},... | collective-permute-start | bytes 1548296 | tf_op jit(solution)/shard_map/ppermute | solution.py:577
  9.2 5.5 %collective-permute-start.1 = (bf16[6,336,128]{2,1,0:T(8,128)(2,1)S(1)}, bf16[6,336,128]{2,1,0:T(8,128)(2,1)S(1)}, u32[]{:S(2)}, u32[]{:S(2)}) collective-permute-start(bf16[6,336,128]{2,1,0:T(8,128)(2,1)S(1)} %get-tuple-element.49), channel_id=1, source_target_pairs={{16,0},{32,16},{48,32},{64,48},{80,64},{96,80},{112,96},{128,112},... | collective-permute-start | bytes 1548296 | tf_op jit(solution)/shard_map/ppermute | solution.py:578
  14.8 3.0 %fluxes.1 = (bf16[2048,128]{1,0:T(8,128)(2,1)}, f32[4,8,512]{2,1,0:T(8,128)S(1)}, f32[72,72]{1,0:T(8,128)S(1)}, f32[72,8]{1,0:T(8,128)S(1)}) custom-call(s32[2,128]{1,0:T(2,128)S(1)} %bitcast.19, f32[4,72,512]{2,1,0:T(8,128)S(1)} %copy-done.4, f32[72,72]{1,0:T(8,128)S(1)} %copy-done.7, f32[1,512]{1,0:T(1,128)S(1)} %bitcast.25), custom_call_target="tpu_custom_call" | custom-call | flops 2000000000 | bytes 6000000 | tf_op jit(solution)/shard_map/fluxes/pallas_call | solution.py:553
  17.7 0.6 copy-done.27
  18.3 0.6 copy-done.31
  19.0 13.4 %all-to-all-start = ((bf16[128,16,128]{2,1,0:T(8,128)(2,1)}), bf16[128,16,128]{2,1,0:T(8,128)(2,1)S(1)}, u32[]{:S(2)}, u32[]{:S(2)}) async-start(bf16[128,16,128]{2,1,0:T(8,128)(2,1)} %bitcast.5), calls=%async_computation | async-start | bytes 1048576 | tf_op jit(solution)/shard_map/all_to_all | solution.py:566
  32.3 0.5 broadcast.196
  32.8 0.7 reduce.3
  33.8 0.1 pad_maximum_fusion.1.mix_ref.refs_3_
  33.9 1.4 %copy-done.13 = bf16[2560,256]{1,0:T(8,128)(2,1)S(1)} copy-done((bf16[2560,256]{1,0:T(8,128)(2,1)S(1)}, bf16[2560,256]{1,0:T(8,128)(2,1)}, u32[]{:S(2)}) %copy-start.13) | copy-done | bytes 1310744
  35.3 0.6 pack.1
  35.9 3.3 %collective-permute-start.2 = (bf16[336,128]{1,0:T(8,128)(2,1)S(1)}, bf16[336,128]{1,0:T(8,128)(2,1)S(1)}, u32[]{:S(2)}, u32[]{:S(2)}) collective-permute-start(bf16[336,128]{1,0:T(8,128)(2,1)S(1)} %get-tuple-element.26), channel_id=1, source_target_pairs={{0,1},{1,2},{2,3},{3,4},{4,5},{5,6},{6,7},{7,8},{8,9},{9,10},{10,1... | collective-permute-start | bytes 258056 | tf_op jit(solution)/shard_map/ppermute | solution.py:584
  39.2 1.3 %collective-permute-start.3 = (bf16[336,128]{1,0:T(8,128)(2,1)S(1)}, bf16[336,128]{1,0:T(8,128)(2,1)S(1)}, u32[]{:S(2)}, u32[]{:S(2)}) collective-permute-start(bf16[336,128]{1,0:T(8,128)(2,1)S(1)} %get-tuple-element.27), channel_id=1, source_target_pairs={{1,0},{2,1},{3,2},{4,3},{5,4},{6,5},{7,6},{8,7},{9,8},{10,9},{11,1... | collective-permute-start | bytes 258056 | tf_op jit(solution)/shard_map/ppermute | solution.py:583
  40.6 1.1 cells.1.w_ref.refs_12_
  41.7 0.8 copy-done.18
  42.5 4.3 %collective-permute-done.2.west_ref = bf16[336,128]{1,0:T(8,128)(2,1)S(1)} collective-permute-done((bf16[336,128]{1,0:T(8,128)(2,1)S(1)}, bf16[336,128]{1,0:T(8,128)(2,1)S(1)}, u32[]{:S(2)}, u32[]{:S(2)}) %collective-permute-start.2) | collective-permute-done | bytes 86048 | tf_op jit(solution)/shard_map/ppermute | solution.py:584
  46.8 2.9 %collective-permute-done.3.east_ref = bf16[336,128]{1,0:T(8,128)(2,1)S(1)} collective-permute-done((bf16[336,128]{1,0:T(8,128)(2,1)S(1)}, bf16[336,128]{1,0:T(8,128)(2,1)S(1)}, u32[]{:S(2)}, u32[]{:S(2)}) %collective-permute-start.3) | collective-permute-done | bytes 86048 | tf_op jit(solution)/shard_map/ppermute | solution.py:583
  49.7 2.9 %coefficients.1 = (f32[5,27,80,128]{3,2,1,0:T(8,128)S(1)}, f32[27,80,128]{2,1,0:T(8,128)S(1)}, f32[27,80,128]{2,1,0:T(8,128)S(1)}, f32[27,8,128]{2,1,0:T(8,128)S(1)}) custom-call(bf16[6,336,128]{2,1,0:T(8,128)(2,1)S(1)} %collective-permute-done.before_ref, bf16[8,336,128]{2,1,0:T(8,128)(2,1)S(1)} %rows.1.z_ref, ...), custom_call_target="tpu_custom_call" | custom-call | flops 4000000000 | bytes 12000000 | tf_op jit(solution)/shard_map/coefficients/pallas_call | solution.py:601
  52.6 2.4 %copy-done.20 = f32[5,27,80,128]{3,2,1,0:T(8,128)} copy-done((f32[5,27,80,128]{3,2,1,0:T(8,128)}, f32[5,27,80,128]{3,2,1,0:T(8,128)S(1)}, u32[]{:S(2)}) %copy-start.20) | copy-done | bytes 5529624
  55.1 1.0 copy-done.23
  56.1 1.0 copy-done.25
  57.1 0.6 copy-done.29
  57.8 1.0 copy-done.19
  58.8 1.5 %remap.1 = (f32[128,128]{1,0:T(8,128)S(1)}, bf16[5,16,128]{2,1,0:T(8,128)(2,1)S(1)}, bf16[5,16,128]{2,1,0:T(8,128)(2,1)S(1)}, f32[2,8,128]{2,1,0:T(8,128)}) custom-call(s32[1,64]{1,0:T(1,128)S(1)} %bitcast.26, bf16[2048,128]{1,0:T(8,128)(2,1)S(1)} %bitcast.15, bf16[1024,256]{1,0:T(8,128)(2,1)S(1)} %copy-done.19, f32[2,8,128]{2,1,0:T(8,128)S(1)} %copy-done.8, ...), custom_call_target="tpu_custom_call" | custom-call | flops 1000000000 | bytes 3000000 | tf_op jit(solution)/shard_map/remap/pallas_call | solution.py:618
  60.3 2.2 %collective-permute-start.4 = (bf16[5,16,128]{2,1,0:T(8,128)(2,1)S(1)}, bf16[5,16,128]{2,1,0:T(8,128)(2,1)S(1)}, u32[]{:S(2)}, u32[]{:S(2)}) collective-permute-start(bf16[5,16,128]{2,1,0:T(8,128)(2,1)S(1)} %get-tuple-element.35), channel_id=1, source_target_pairs={{0,16},{16,32},{32,48},{48,64},{64,80},{80,96},{96,112},{112,128},... | collective-permute-start | bytes 61448 | tf_op jit(solution)/shard_map/ppermute | solution.py:624
  62.5 2.1 %collective-permute-start.5 = (bf16[5,16,128]{2,1,0:T(8,128)(2,1)S(1)}, bf16[5,16,128]{2,1,0:T(8,128)(2,1)S(1)}, u32[]{:S(2)}, u32[]{:S(2)}) collective-permute-start(bf16[5,16,128]{2,1,0:T(8,128)(2,1)S(1)} %get-tuple-element.36), channel_id=1, source_target_pairs={{16,0},{32,16},{48,32},{64,48},{80,64},{96,80},{112,96},{128,112},... | collective-permute-start | bytes 61448 | tf_op jit(solution)/shard_map/ppermute | solution.py:625
  64.6 3.0 %collective-permute-done.5.after_ref.refs_6_ = bf16[5,16,128]{2,1,0:T(8,128)(2,1)S(1)} collective-permute-done((bf16[5,16,128]{2,1,0:T(8,128)(2,1)S(1)}, bf16[5,16,128]{2,1,0:T(8,128)(2,1)S(1)}, u32[]{:S(2)}, u32[]{:S(2)}) %collective-permute-start.5) | collective-permute-done | bytes 20512 | tf_op jit(solution)/shard_map/ppermute | solution.py:625
  67.6 0.3 pack_forcing.1
  67.9 3.8 %collective-permute-start.6 = (bf16[16,128]{1,0:T(8,128)(2,1)S(1)}, bf16[16,128]{1,0:T(8,128)(2,1)S(1)}, u32[]{:S(2)}, u32[]{:S(2)}) collective-permute-start(bf16[16,128]{1,0:T(8,128)(2,1)S(1)} %get-tuple-element.37), channel_id=1, source_target_pairs={{0,1},{1,2},{2,3},{3,4},{4,5},{5,6},{6,7},{7,8},{8,9},{9,10},{10,1... | collective-permute-start | bytes 12296 | tf_op jit(solution)/shard_map/ppermute | solution.py:631
  71.7 1.3 %collective-permute-start.7 = (bf16[16,128]{1,0:T(8,128)(2,1)S(1)}, bf16[16,128]{1,0:T(8,128)(2,1)S(1)}, u32[]{:S(2)}, u32[]{:S(2)}) collective-permute-start(bf16[16,128]{1,0:T(8,128)(2,1)S(1)} %get-tuple-element.38), channel_id=1, source_target_pairs={{1,0},{2,1},{3,2},{4,3},{5,4},{6,5},{7,6},{8,7},{9,8},{10,9},{11,1... | collective-permute-start | bytes 12296 | tf_op jit(solution)/shard_map/ppermute | solution.py:630
  73.1 0.1 reshape.221.table_ref
  73.3 2.7 %collective-permute-done.7.refs_8_ = bf16[16,128]{1,0:T(8,128)(2,1)S(1)} collective-permute-done((bf16[16,128]{1,0:T(8,128)(2,1)S(1)}, bf16[16,128]{1,0:T(8,128)(2,1)S(1)}, u32[]{:S(2)}, u32[]{:S(2)}) %collective-permute-start.7) | collective-permute-done | bytes 4128 | tf_op jit(solution)/shard_map/ppermute | solution.py:630
  76.0 2.6 %copy-done.21 = f32[5,27,80,128]{3,2,1,0:T(8,128)S(1)} copy-done((f32[5,27,80,128]{3,2,1,0:T(8,128)S(1)}, f32[5,27,80,128]{3,2,1,0:T(8,128)}, u32[]{:S(2)}) %copy-start.21) | copy-done | bytes 5529624
  78.6 1.2 copy-done.26
  79.8 4.6 %temperature.1 = (f32[640,128]{1,0:T(8,128)S(1)}, f32[512,128]{1,0:T(8,128)}) custom-call(f32[27,80,128]{2,1,0:T(8,128)S(1)} %copy-done.26, f32[5,27,80,128]{3,2,1,0:T(8,128)S(1)} %copy-done.21, f32[27,8,128]{2,1,0:T(8,128)S(1)} %copy-done.30, bf16[80,240]{1,0:T(8,128)(2,1)S(1)} %pad_maximum_fusion.1.mix_ref.refs_3_, ...), custom_call_target="tpu_custom_call" | custom-call | flops 6000000000 | bytes 18000000 | tf_op jit(solution)/shard_map/temperature/pallas_call | solution.py:640
  84.4 25.6 %all-to-all-start.1 = ((f32[128,4,128]{2,1,0:T(4,128)}), f32[128,4,128]{2,1,0:T(4,128)S(1)}, u32[]{:S(2)}, u32[]{:S(2)}) async-start(f32[128,4,128]{2,1,0:T(4,128)} %bitcast.13), calls=%async_computation.1 | async-start | bytes 524288 | tf_op jit(solution)/shard_map/all_to_all | solution.py:649
  110.0 2.6 %copy-done.22 = f32[5,27,80,128]{3,2,1,0:T(8,128)S(1)} copy-done((f32[5,27,80,128]{3,2,1,0:T(8,128)S(1)}, f32[5,27,80,128]{3,2,1,0:T(8,128)}, u32[]{:S(2)}) %copy-start.22) | copy-done | bytes 5529624
  112.6 1.2 copy-done.24
  113.9 4.2 %salinity.1 = f32[640,128]{1,0:T(8,128)S(1)} custom-call(f32[27,80,128]{2,1,0:T(8,128)S(1)} %copy-done.24, f32[5,27,80,128]{3,2,1,0:T(8,128)S(1)} %copy-done.22, f32[27,8,128]{2,1,0:T(8,128)S(1)} %copy-done.30, bf16[80,240]{1,0:T(8,128)(2,1)S(1)} %pad_maximum_fusion.1.mix_ref.refs_3_, f32[128,128]{1,0:T(8,128)S(1)} %get-tuple-element.34.f_ref.refs_4_, ...), custom_call_target="tpu_custom_call" | custom-call | flops 6000000000 | bytes 18000000 | tf_op jit(solution)/shard_map/salinity/pallas_call | solution.py:658
  118.0 0.9 pad_maximum_fusion
  119.0 1.9 %atmosphere.1 = f32[4,72,512]{2,1,0:T(8,128)} custom-call(f32[4,72,512]{2,1,0:T(8,128)S(1)} %copy-done.4, f32[4,8,512]{2,1,0:T(8,128)S(1)} %copy-done.28, f32[72,72]{1,0:T(8,128)S(1)} %get-tuple-element.42.top_ref, f32[72,8]{1,0:T(8,128)S(1)} %copy-done.32), custom_call_target="tpu_custom_call" | custom-call | flops 3000000000 | bytes 9000000 | tf_op jit(solution)/shard_map/atmosphere/pallas_call | solution.py:651
  120.8 4.5 %all-to-all-done.1 = f32[128,4,128]{2,1,0:T(4,128)S(1)} async-done(((f32[128,4,128]{2,1,0:T(4,128)}), f32[128,4,128]{2,1,0:T(4,128)S(1)}, u32[]{:S(2)}, u32[]{:S(2)}) %all-to-all-start.1) | async-done | bytes 262176 | tf_op jit(solution)/shard_map/all_to_all | solution.py:649
  125.4 0.9 finish.1
  (63 shorter events, 0.6 us)
Async XLA Ops:
  0.6 1.1 copy-start.2
  1.7 1.0 copy-start.6
  2.7 0.7 copy-start.9
  3.6 11.1 %copy-start.1 = (s32[1,1,128,2]{2,3,1,0:T(2,128)S(1)}, s32[1,1,128,2]{2,3,1,0:T(2,128)}, u32[]{:S(2)}) copy-start(s32[1,1,128,2]{2,3,1,0:T(2,128)} %param.23) | copy-start | bytes 3076
  3.6 11.1 %copy-start.4 = (f32[4,72,512]{2,1,0:T(8,128)S(1)}, f32[4,72,512]{2,1,0:T(8,128)}, u32[]{:S(2)}) copy-start(f32[4,72,512]{2,1,0:T(8,128)} %a_ref.3) | copy-start | bytes 1769476
  3.7 11.1 %copy-start.7 = (f32[72,72]{1,0:T(8,128)S(1)}, f32[72,72]{1,0:T(8,128)}, u32[]{:S(2)}) copy-start(f32[72,72]{1,0:T(8,128)} %m_ref.1) | copy-start | bytes 62212
  3.7 11.1 %copy-start.11 = (f32[512]{0:T(512)S(1)}, f32[512]{0:T(512)}, u32[]{:S(2)}) copy-start(f32[512]{0:T(512)} %param.16) | copy-start | bytes 6148
  4.6 29.3 %collective-permute-start = (bf16[6,336,128]{2,1,0:T(8,128)(2,1)}, bf16[6,336,128]{2,1,0:T(8,128)(2,1)S(1)}, u32[]{:S(2)}, u32[]{:S(2)}) collective-permute-start(bf16[6,336,128]{2,1,0:T(8,128)(2,1)} %get-tuple-element.50), channel_id=1, source_target_pairs={{0,16},{16,32},{32,48},{48,64},{64,80},{80,96},{96,112},{112,128},... | collective-permute-start | bytes 1548296 | tf_op jit(solution)/shard_map/ppermute | solution.py:577
  9.2 24.8 %collective-permute-start.1 = (bf16[6,336,128]{2,1,0:T(8,128)(2,1)S(1)}, bf16[6,336,128]{2,1,0:T(8,128)(2,1)S(1)}, u32[]{:S(2)}, u32[]{:S(2)}) collective-permute-start(bf16[6,336,128]{2,1,0:T(8,128)(2,1)S(1)} %get-tuple-element.49), channel_id=1, source_target_pairs={{16,0},{32,16},{48,32},{64,48},{80,64},{96,80},{112,96},{128,112},... | collective-permute-start | bytes 1548296 | tf_op jit(solution)/shard_map/ppermute | solution.py:578
  14.7 18.1 %copy-start.12 = (s32[1,1,64]{2,1,0:T(1,128)S(1)}, s32[1,1,64]{2,1,0:T(1,128)}, u32[]{:S(2)}) copy-start(s32[1,1,64]{2,1,0:T(1,128)} %param.24) | copy-start | bytes 772
  14.7 19.0 %copy-start = (f32[80,80]{1,0:T(8,128)S(1)}, f32[80,80]{1,0:T(8,128)}, u32[]{:S(2)}) copy-start(f32[80,80]{1,0:T(8,128)} %refs_11_.1) | copy-start | bytes 76804
  17.7 0.6 copy-start.27
  18.3 0.6 copy-start.31
  19.0 38.8 %all-to-all-start = ((bf16[128,16,128]{2,1,0:T(8,128)(2,1)}), bf16[128,16,128]{2,1,0:T(8,128)(2,1)S(1)}, u32[]{:S(2)}, u32[]{:S(2)}) async-start(bf16[128,16,128]{2,1,0:T(8,128)(2,1)} %bitcast.5), calls=%async_computation | async-start | bytes 1048576 | tf_op jit(solution)/shard_map/all_to_all | solution.py:566
  33.9 6.6 %copy-start.5 = (bf16[1,1,64,4096]{3,2,1,0:T(8,128)(2,1)S(1)}, bf16[1,1,64,4096]{3,2,1,0:T(8,128)(2,1)}, u32[]{:S(2)}) copy-start(bf16[1,1,64,4096]{3,2,1,0:T(8,128)(2,1)} %param.22) | copy-start | bytes 1572868
  33.9 1.4 %copy-start.13 = (bf16[2560,256]{1,0:T(8,128)(2,1)S(1)}, bf16[2560,256]{1,0:T(8,128)(2,1)}, u32[]{:S(2)}) copy-start(bf16[2560,256]{1,0:T(8,128)(2,1)} %constant.43.clone.pack_ref) | copy-start | bytes 3932164
  35.9 10.9 %collective-permute-start.2 = (bf16[336,128]{1,0:T(8,128)(2,1)S(1)}, bf16[336,128]{1,0:T(8,128)(2,1)S(1)}, u32[]{:S(2)}, u32[]{:S(2)}) collective-permute-start(bf16[336,128]{1,0:T(8,128)(2,1)S(1)} %get-tuple-element.26), channel_id=1, source_target_pairs={{0,1},{1,2},{2,3},{3,4},{4,5},{5,6},{6,7},{7,8},{8,9},{9,10},{10,1... | collective-permute-start | bytes 258056 | tf_op jit(solution)/shard_map/ppermute | solution.py:584
  39.2 10.5 %collective-permute-start.3 = (bf16[336,128]{1,0:T(8,128)(2,1)S(1)}, bf16[336,128]{1,0:T(8,128)(2,1)S(1)}, u32[]{:S(2)}, u32[]{:S(2)}) collective-permute-start(bf16[336,128]{1,0:T(8,128)(2,1)S(1)} %get-tuple-element.27), channel_id=1, source_target_pairs={{1,0},{2,1},{3,2},{4,3},{5,4},{6,5},{7,6},{8,7},{9,8},{10,9},{11,1... | collective-permute-start | bytes 258056 | tf_op jit(solution)/shard_map/ppermute | solution.py:583
  40.5 9.2 %copy-start.3 = (f32[2,80,8,128]{3,2,1,0:T(8,128)S(1)}, f32[2,80,8,128]{3,2,1,0:T(8,128)}, u32[]{:S(2)}) copy-start(f32[2,80,8,128]{3,2,1,0:T(8,128)} %param.17) | copy-start | bytes 1966084
  40.5 9.2 %copy-start.15 = (bf16[256,896]{1,0:T(8,128)(2,1)S(1)}, bf16[256,896]{1,0:T(8,128)(2,1)}, u32[]{:S(2)}) copy-start(bf16[256,896]{1,0:T(8,128)(2,1)} %constant.44.clone.spread_ref.refs_9_) | copy-start | bytes 1376260
  40.6 9.1 %copy-start.16 = (bf16[384,128]{1,0:T(8,128)(2,1)S(1)}, bf16[384,128]{1,0:T(8,128)(2,1)}, u32[]{:S(2)}) copy-start(bf16[384,128]{1,0:T(8,128)(2,1)} %constant.45.clone.own_ref.refs_10_) | copy-start | bytes 294916
  41.7 0.8 copy-start.18
  42.5 15.3 %copy-start.8 = (f32[2,8,128]{2,1,0:T(8,128)S(1)}, f32[2,8,128]{2,1,0:T(8,128)}, u32[]{:S(2)}) copy-start(f32[2,8,128]{2,1,0:T(8,128)} %u_ref.1) | copy-start | bytes 24580
  42.5 15.3 %copy-start.10 = (s32[8,128]{1,0:T(8,128)S(1)}, s32[8,128]{1,0:T(8,128)}, u32[]{:S(2)}) copy-start(s32[8,128]{1,0:T(8,128)} %wet_ref.3) | copy-start | bytes 12292
  52.6 2.4 %copy-start.20 = (f32[5,27,80,128]{3,2,1,0:T(8,128)}, f32[5,27,80,128]{3,2,1,0:T(8,128)S(1)}, u32[]{:S(2)}) copy-start(f32[5,27,80,128]{3,2,1,0:T(8,128)S(1)} %get-tuple-element.31.refs_1_) | copy-start | bytes 16588804
  55.1 1.0 copy-start.23
  56.1 1.0 copy-start.25
  57.1 0.6 copy-start.29
  57.8 1.0 copy-start.19
  58.8 8.8 %copy-start.14 = (bf16[2560,256]{1,0:T(8,128)(2,1)S(1)}, bf16[2560,256]{1,0:T(8,128)(2,1)}, u32[]{:S(2)}) copy-start(bf16[2560,256]{1,0:T(8,128)(2,1)} %constant.43.clone.pack_ref) | copy-start | bytes 3932164
  60.3 4.3 %collective-permute-start.4 = (bf16[5,16,128]{2,1,0:T(8,128)(2,1)S(1)}, bf16[5,16,128]{2,1,0:T(8,128)(2,1)S(1)}, u32[]{:S(2)}, u32[]{:S(2)}) collective-permute-start(bf16[5,16,128]{2,1,0:T(8,128)(2,1)S(1)} %get-tuple-element.35), channel_id=1, source_target_pairs={{0,16},{16,32},{32,48},{48,64},{64,80},{80,96},{96,112},{112,128},... | collective-permute-start | bytes 61448 | tf_op jit(solution)/shard_map/ppermute | solution.py:624
  62.5 5.1 %collective-permute-start.5 = (bf16[5,16,128]{2,1,0:T(8,128)(2,1)S(1)}, bf16[5,16,128]{2,1,0:T(8,128)(2,1)S(1)}, u32[]{:S(2)}, u32[]{:S(2)}) collective-permute-start(bf16[5,16,128]{2,1,0:T(8,128)(2,1)S(1)} %get-tuple-element.36), channel_id=1, source_target_pairs={{16,0},{32,16},{48,32},{64,48},{80,64},{96,80},{112,96},{128,112},... | collective-permute-start | bytes 61448 | tf_op jit(solution)/shard_map/ppermute | solution.py:625
  67.6 8.4 %copy-start.17 = (f32[2,8,128]{2,1,0:T(8,128)S(1)}, f32[2,8,128]{2,1,0:T(8,128)}, u32[]{:S(2)}) copy-start(f32[2,8,128]{2,1,0:T(8,128)} %get-tuple-element.23.refs_14_) | copy-start | bytes 24580
  67.6 8.4 %copy-start.30 = (f32[27,8,128]{2,1,0:T(8,128)S(1)}, f32[27,8,128]{2,1,0:T(8,128)}, u32[]{:S(2)}) copy-start(f32[27,8,128]{2,1,0:T(8,128)} %copy-done.29) | copy-start | bytes 331780
  67.9 5.4 %collective-permute-start.6 = (bf16[16,128]{1,0:T(8,128)(2,1)S(1)}, bf16[16,128]{1,0:T(8,128)(2,1)S(1)}, u32[]{:S(2)}, u32[]{:S(2)}) collective-permute-start(bf16[16,128]{1,0:T(8,128)(2,1)S(1)} %get-tuple-element.37), channel_id=1, source_target_pairs={{0,1},{1,2},{2,3},{3,4},{4,5},{5,6},{6,7},{7,8},{8,9},{9,10},{10,1... | collective-permute-start | bytes 12296 | tf_op jit(solution)/shard_map/ppermute | solution.py:631
  71.7 4.4 %collective-permute-start.7 = (bf16[16,128]{1,0:T(8,128)(2,1)S(1)}, bf16[16,128]{1,0:T(8,128)(2,1)S(1)}, u32[]{:S(2)}, u32[]{:S(2)}) collective-permute-start(bf16[16,128]{1,0:T(8,128)(2,1)S(1)} %get-tuple-element.38), channel_id=1, source_target_pairs={{1,0},{2,1},{3,2},{4,3},{5,4},{6,5},{7,6},{8,7},{9,8},{10,9},{11,1... | collective-permute-start | bytes 12296 | tf_op jit(solution)/shard_map/ppermute | solution.py:630
  76.0 2.6 %copy-start.21 = (f32[5,27,80,128]{3,2,1,0:T(8,128)S(1)}, f32[5,27,80,128]{3,2,1,0:T(8,128)}, u32[]{:S(2)}) copy-start(f32[5,27,80,128]{3,2,1,0:T(8,128)} %copy-done.20) | copy-start | bytes 16588804
  78.6 1.2 copy-start.26
  84.4 41.0 %all-to-all-start.1 = ((f32[128,4,128]{2,1,0:T(4,128)}), f32[128,4,128]{2,1,0:T(4,128)S(1)}, u32[]{:S(2)}, u32[]{:S(2)}) async-start(f32[128,4,128]{2,1,0:T(4,128)} %bitcast.13), calls=%async_computation.1 | async-start | bytes 524288 | tf_op jit(solution)/shard_map/all_to_all | solution.py:649
  110.0 2.6 %copy-start.22 = (f32[5,27,80,128]{3,2,1,0:T(8,128)S(1)}, f32[5,27,80,128]{3,2,1,0:T(8,128)}, u32[]{:S(2)}) copy-start(f32[5,27,80,128]{3,2,1,0:T(8,128)} %copy-done.20) | copy-start | bytes 16588804
  112.6 1.2 copy-start.24
  118.0 0.9 copy-start.28
  118.0 0.9 copy-start.32

commit v2 on v1

--- a/solution.py
+++ b/solution.py
@@ -110,26 +110,25 @@
     )
 
 
-def flux_body(table_ref, a_ref, m_ref, sst_ref, pay_ref, g_ref, top_ref, edge_ref, block_ref):
-    levels = m_ref.shape[0]
-    bottom = levels - 1
+def mixing_powers(m_ref):
     power = {1: m_ref[...]}
     power[2] = exact(power[1], power[1])
     power[3] = exact(power[1], power[2])
     power[4] = exact(power[2], power[2])
     power[5] = exact(power[2], power[3])
     power[6] = exact(power[3], power[3])
+    return power
+
+
+def flux_body(table_ref, a_ref, m_ref, sst_ref, pay_ref, g_hbm, block_ref, g_ref, sem):
+    levels = m_ref.shape[0]
+    bottom = levels - 1
+    power = mixing_powers(m_ref)
     first = (iota((1, levels), 1) == bottom).astype(f32)
     rows = [first] + [power[n][bottom:, :] for n in range(1, STEPS)]
     rows = jnp.concatenate(rows + [jnp.zeros((8 - STEPS, levels), f32)], axis=0)
     row_high, row_low = halves(rows)
     both = jnp.concatenate([row_high.astype(f32), row_low.astype(f32)], axis=0).astype(bf16)
-    top_ref[...] = power[6]
-    lane = iota((levels, 8), 1)
-    edge = jnp.zeros((levels, 8), f32)
-    for n in range(STEPS):
-        edge = jnp.where(lane == n, power[STEPS - n][:, bottom:], edge)
-    edge_ref[...] = edge
     base = []
     for v in range(4):
         high, low = halves(a_ref[v])
@@ -163,6 +162,8 @@
     blank = [jnp.zeros_like(sst)] * (8 - STEPS)
     for v in range(4):
         g_ref[v] = jnp.concatenate([gained[n][v] for n in range(STEPS)] + blank, axis=0)
+    copy = pltpu.make_async_copy(g_ref, g_hbm, sem)
+    copy.start()
     pairs = [(fluxes[n][0], fluxes[n][1]) for n in range(STEPS)] + [(east, north)]
     block = iota((8, LANES), 0)
     left = iota((8, LANES), 1) < 64
@@ -183,11 +184,18 @@
             at = jnp.maximum(table_ref[side, d], 0) * 8
             chosen.append(block_ref[pl.ds(pl.multiple_of(at, 8), 8), :])
         pay_ref[16 * d : 16 * d + 16, :] = jnp.concatenate(chosen, axis=0).astype(bf16)
-
-
-def atmosphere_body(a_ref, g_ref, top_ref, edge_ref, out_ref):
+    copy.wait()
+
+
+def atmosphere_body(a_ref, g_ref, m_ref, out_ref):
+    levels = m_ref.shape[0]
+    power = mixing_powers(m_ref)
+    lane = iota((levels, 8), 1)
+    edge = jnp.zeros((levels, 8), f32)
+    for n in range(STEPS):
+        edge = jnp.where(lane == n, power[STEPS - n][:, levels - 1 :], edge)
     for v in range(4):
-        out_ref[v] = exact(top_ref[...], a_ref[v]) + exact(edge_ref[...], g_ref[v])
+        out_ref[v] = exact(power[STEPS], a_ref[v]) + exact(edge, g_ref[v])
 
 
 def finish_body(table_ref, in_ref, out_ref):
@@ -550,19 +558,20 @@
         [jnp.where(by_k % 2 == side, (by_k // 2) * 4, -64) for side in range(2)], axis=1
     )
 
-    payload, gained, top, edge = call(
+    payload, gained = call(
         flux_body,
-        (
-            shape((peers * 16, LANES), bf16),
-            shape((4, 8, air_columns)),
-            shape((air_levels, air_levels)),
-            shape((air_levels, 8)),
-        ),
+        (shape((peers * 16, LANES), bf16), shape((4, 8, air_columns))),
         "fluxes",
         [SMEM, VMEM, VMEM, VMEM],
-        scratch=[pltpu.VMEM((64, LANES), f32)],
-        micros=2,
+        (VMEM, HBM),
+        scratch=[
+            pltpu.VMEM((64, LANES), f32),
+            pltpu.VMEM((4, 8, air_columns), f32),
+            pltpu.SemaphoreType.DMA,
+        ],
+        micros=3,
     )(table, atmosphere_level_state, atmosphere_mixing_map, sea_surface_temps[None])
+    payload, wet_rows = lax.optimization_barrier((payload, ocean_cell_mask))
     arrived = lax.all_to_all(payload, band, 0, 0, tiled=True)
 
     flat = tracers.reshape(2, levels * ROWS, LANES)
@@ -573,7 +582,7 @@
         "rows",
         [VMEM] * 3,
         scratch=[pltpu.VMEM(flat.shape, f32)],
-    )(flat, ocean_advect_velocity.reshape(flat.shape), ocean_cell_mask)
+    )(flat, ocean_advect_velocity.reshape(flat.shape), wet_rows)
     before = lax.ppermute(z[ROWS - HALO :], rows_axis, up)
     after = lax.ppermute(z[:HALO], rows_axis, down)
     edge_shape = shape((depth, LANES), bf16)
@@ -598,6 +607,23 @@
     mix = jnp.concatenate([upper, lower, upper], axis=1)
     wide = (TILES, levels, LANES)
     cat = pltpu.VMEM((2, 3 * levels, 4 * LANES), bf16)
+    edge_rows = shape((HALO - 1, 16, LANES), bf16)
+    forcing, send_up, send_down, ocean_currents = call(
+        remap_body,
+        (shape((ROWS * 16, LANES)), edge_rows, edge_rows, shape(currents.shape)),
+        "remap",
+        [SMEM] + [VMEM] * 4,
+    )(arrival, arrived, cells, currents, ocean_cell_mask)
+    f_before = lax.ppermute(send_up, rows_axis, up)
+    f_after = lax.ppermute(send_down, rows_axis, down)
+    strip = shape((16, LANES), bf16)
+    f_first, f_last = call(pack_forcing_body, (strip, strip), "pack_forcing", [VMEM] * 4)(
+        forcing, f_before, f_after, pack_moves
+    )
+    f_first, f_last, mix = lax.optimization_barrier((f_first, f_last, mix))
+    f_east = lax.ppermute(f_first, "col", leftward)
+    f_west = lax.ppermute(f_last, "col", right)
+
     coef, x1, salt, wet = call(
         coefficient_body,
         (shape((5, *wide)), shape(wide), shape(wide), shape((TILES, 8, LANES))),
@@ -612,24 +638,6 @@
         limit=24,
         micros=4,
     )(before, z, after, west_in, east_in, flat, mix, spread_moves, own_moves)
-    arrived, coef = lax.optimization_barrier((arrived, coef))
-
-    edge_rows = shape((HALO - 1, 16, LANES), bf16)
-    forcing, send_up, send_down, ocean_currents = call(
-        remap_body,
-        (shape((ROWS * 16, LANES)), edge_rows, edge_rows, shape(currents.shape)),
-        "remap",
-        [SMEM] + [VMEM] * 4,
-    )(arrival, arrived, cells, currents, ocean_cell_mask)
-    f_before = lax.ppermute(send_up, rows_axis, up)
-    f_after = lax.ppermute(send_down, rows_axis, down)
-    strip = shape((16, LANES), bf16)
-    f_first, f_last = call(pack_forcing_body, (strip, strip), "pack_forcing", [VMEM] * 4)(
-        forcing, f_before, f_after, pack_moves
-    )
-    f_east = lax.ppermute(f_first, "col", leftward)
-    f_west = lax.ppermute(f_last, "col", right)
-
     shared = (coef, wet, mix, forcing, f_before, f_after, f_west, f_east, spread_moves, own_moves)
     scratch = [
         pltpu.VMEM(wide, f32),
@@ -652,9 +660,9 @@
         atmosphere_body,
         shape(atmosphere_level_state.shape),
         "atmosphere",
-        [VMEM] * 4,
+        [VMEM] * 3,
         micros=3,
-    )(atmosphere_level_state, gained, top, edge)
+    )(atmosphere_level_state, gained, atmosphere_mixing_map)
     cold = call(
         functools.partial(tracer_body, 1),
         shape(flat.shape[1:]),

time: 127 us -> 113 us (0.89)
  local copies, waits for them, and re-layouts: 21.8 us -> 13.8 us
  waiting for transfers between devices: 17.5 us -> 12.1 us
  starting transfers between devices: 63 us -> 60.6 us
  Pallas kernels: 21.1 us -> 22.4 us
    unnamed x67 -> x59, local copies, waits for them, and re-layouts: 20.5 us -> 10.6 us
    all_to_all x1, waiting for transfers between devices: 0.01 us -> 9.76 us  [on_device(): arrived = lax.all_to_all(payload, band, 0, 0, tiled=True)]
    all_to_all x1, starting transfers between devices: 13.4 us -> 18.4 us  [on_device(): arrived = lax.all_to_all(payload, band, 0, 0, tiled=True)]
    ppermute x1, waiting for transfers between devices: 4.34 us -> 0.01 us  [on_device(): west_in = lax.ppermute(last, 'col', right)]
    ppermute x1, starting transfers between devices: 5.51 us -> 1.92 us  [on_device(): after = lax.ppermute(z[:HALO], rows_axis, down)]
    ppermute x1, waiting for transfers between devices: 2.97 us -> 0.01 us  [on_device(): f_after = lax.ppermute(send_down, rows_axis, down)]
    ppermute x1, waiting for transfers between devices: 2.89 us -> 0.01 us  [on_device(): east_in = lax.ppermute(first, 'col', leftward)]
    ppermute x1, waiting for transfers between devices: 2.74 us -> 0.07 us  [on_device(): f_east = lax.ppermute(f_first, 'col', leftward)]
  transfers between devices with their start and end apart: 10 -> 10, of which waited for: 5 -> 3; matrix products, arithmetic and copies ran while one was open for 2% -> 5% of each run, Pallas kernels for 11% -> 12%
where the time goes in v2:
time: 113 us; the launch traced here: 112 us
  starting transfers between devices  60.6 us (54%)
  Pallas kernels  22.4 us (20%)
  local copies, waits for them, and re-layouts  13.8 us (12%)
  waiting for transfers between devices  12.1 us (11%)
  other arithmetic  1.74 us (2%)
    all_to_all x1, starting transfers between devices, on_device(): home = lax.all_to_all(terms, band, 0, 0, tiled=True)  23.4 us
    all_to_all x1, starting transfers between devices, on_device(): arrived = lax.all_to_all(payload, band, 0, 0, tiled=True)  18.4 us
    unnamed x59, local copies, waits for them, and re-layouts  10.6 us
    all_to_all x1, waiting for transfers between devices, on_device(): arrived = lax.all_to_all(payload, band, 0, 0, tiled=True)  9.76 us
    pallas_call x1, Pallas kernels, on_device(): call(functools.partial(tracer_body, 0), (shape(flat.shape[1:]), shape((pe...  4.81 us
    pallas_call x1, Pallas kernels, on_device(): call(functools.partial(tracer_body, 1), shape(flat.shape[1:]), 'salinity'...  4.44 us
    ppermute x1, starting transfers between devices, on_device(): f_west = lax.ppermute(f_last, 'col', right)  4.12 us
    ppermute x1, starting transfers between devices, on_device(): before = lax.ppermute(z[ROWS - HALO:], rows_axis, up)  3.62 us
  transfers between devices with their start and end apart: 10, of which 3 were waited for; matrix products, arithmetic and copies ran while one was open for 5% of the time, Pallas kernels for 12%

profile of v2, /device:TPU:1, one launch (start us, length us, event | category | flops | bytes accessed | tf_op | source)
XLA Modules:
  0.0 111.7 jit_solution(8497846466002449534)
XLA Ops:
  0.6 0.0 copy-start.1
  0.6 0.7 copy-done.1
  1.3 1.1 copy-done.4
  2.4 0.8 copy-done.8
  3.1 0.7 copy-done.12
  3.8 3.0 %fluxes.1 = (bf16[2048,128]{1,0:T(8,128)(2,1)}, f32[4,8,512]{2,1,0:T(8,128)S(1)}) custom-call(s32[2,128]{1,0:T(2,128)S(1)} %bitcast.19, f32[4,72,512]{2,1,0:T(8,128)S(1)} %copy-done.4, f32[72,72]{1,0:T(8,128)S(1)} %copy-done.8, f32[1,512]{1,0:T(1,128)S(1)} %bitcast.25), custom_call_target="tpu_custom_call" | custom-call | flops 3000000000 | bytes 9000000 | tf_op jit(solution)/shard_map/fluxes/pallas_call | solution.py:561
  6.9 18.4 %all-to-all-start = ((bf16[128,16,128]{2,1,0:T(8,128)(2,1)}), bf16[128,16,128]{2,1,0:T(8,128)(2,1)S(1)}, u32[]{:S(2)}, u32[]{:S(2)}) async-start(bf16[128,16,128]{2,1,0:T(8,128)(2,1)} %bitcast.6), calls=%async_computation | async-start | bytes 1048576 | tf_op jit(solution)/shard_map/all_to_all | solution.py:575
  25.3 0.2 rows.1.z_ref
  25.6 1.1 fusion.3
  26.7 3.6 %collective-permute-start = (bf16[6,336,128]{2,1,0:T(8,128)(2,1)}, bf16[6,336,128]{2,1,0:T(8,128)(2,1)S(1)}, u32[]{:S(2)}, u32[]{:S(2)}) collective-permute-start(bf16[6,336,128]{2,1,0:T(8,128)(2,1)} %get-tuple-element.52), channel_id=1, source_target_pairs={{0,16},{16,32},{32,48},{48,64},{64,80},{80,96},{96,112},{112,128},... | collective-permute-start | bytes 1548296 | tf_op jit(solution)/shard_map/ppermute | solution.py:586
  30.4 1.9 %collective-permute-start.1 = (bf16[6,336,128]{2,1,0:T(8,128)(2,1)}, bf16[6,336,128]{2,1,0:T(8,128)(2,1)S(1)}, u32[]{:S(2)}, u32[]{:S(2)}) collective-permute-start(bf16[6,336,128]{2,1,0:T(8,128)(2,1)} %get-tuple-element.51), channel_id=1, source_target_pairs={{16,0},{32,16},{48,32},{64,48},{80,64},{96,80},{112,96},{128,112},... | collective-permute-start | bytes 1548296 | tf_op jit(solution)/shard_map/ppermute | solution.py:587
  32.3 0.5 broadcast.196
  32.8 0.7 reduce.3
  33.5 0.1 reshape_reshape.3
  33.5 0.1 copy.19
  33.6 0.1 reshape.220
  33.7 0.8 broadcast_in_dim.13
  34.5 1.0 reshape.221.table_ref
  35.5 0.1 pad_add_fusion.refs_13_
  35.6 1.1 cells.1.w_ref.refs_12_
  36.7 0.8 copy-done.18
  37.5 0.1 pad_maximum_fusion.1.mix_ref.refs_3_
  37.6 9.8 %all-to-all-done = bf16[128,16,128]{2,1,0:T(8,128)(2,1)S(1)} async-done(((bf16[128,16,128]{2,1,0:T(8,128)(2,1)}), bf16[128,16,128]{2,1,0:T(8,128)(2,1)S(1)}, u32[]{:S(2)}, u32[]{:S(2)}) %all-to-all-start) | async-done | bytes 524320 | tf_op jit(solution)/shard_map/all_to_all | solution.py:575
  47.4 1.0 copy-done.19
  48.4 1.5 %remap.1 = (f32[128,128]{1,0:T(8,128)S(1)}, bf16[5,16,128]{2,1,0:T(8,128)(2,1)S(1)}, bf16[5,16,128]{2,1,0:T(8,128)(2,1)S(1)}, f32[2,8,128]{2,1,0:T(8,128)}) custom-call(s32[1,64]{1,0:T(1,128)S(1)} %bitcast.26, bf16[2048,128]{1,0:T(8,128)(2,1)S(1)} %bitcast.15, bf16[1024,256]{1,0:T(8,128)(2,1)S(1)} %copy-done.19, f32[2,8,128]{2,1,0:T(8,128)S(1)} %copy-done.10, ...), custom_call_target="tpu_custom_call" | custom-call | flops 1000000000 | bytes 3000000 | tf_op jit(solution)/shard_map/remap/pallas_call | solution.py:611
  49.9 1.9 %collective-permute-start.4 = (bf16[5,16,128]{2,1,0:T(8,128)(2,1)S(1)}, bf16[5,16,128]{2,1,0:T(8,128)(2,1)S(1)}, u32[]{:S(2)}, u32[]{:S(2)}) collective-permute-start(bf16[5,16,128]{2,1,0:T(8,128)(2,1)S(1)} %get-tuple-element.33), channel_id=1, source_target_pairs={{0,16},{16,32},{32,48},{48,64},{64,80},{80,96},{96,112},{112,128},... | collective-permute-start | bytes 61448 | tf_op jit(solution)/shard_map/ppermute | solution.py:617
  51.8 2.4 %collective-permute-start.5 = (bf16[5,16,128]{2,1,0:T(8,128)(2,1)S(1)}, bf16[5,16,128]{2,1,0:T(8,128)(2,1)S(1)}, u32[]{:S(2)}, u32[]{:S(2)}) collective-permute-start(bf16[5,16,128]{2,1,0:T(8,128)(2,1)S(1)} %get-tuple-element.34), channel_id=1, source_target_pairs={{16,0},{32,16},{48,32},{64,48},{80,64},{96,80},{112,96},{128,112},... | collective-permute-start | bytes 61448 | tf_op jit(solution)/shard_map/ppermute | solution.py:618
  54.3 0.6 pack.1
  54.9 2.2 %collective-permute-start.2 = (bf16[336,128]{1,0:T(8,128)(2,1)S(1)}, bf16[336,128]{1,0:T(8,128)(2,1)S(1)}, u32[]{:S(2)}, u32[]{:S(2)}) collective-permute-start(bf16[336,128]{1,0:T(8,128)(2,1)S(1)} %get-tuple-element.29), channel_id=1, source_target_pairs={{0,1},{1,2},{2,3},{3,4},{4,5},{5,6},{6,7},{7,8},{8,9},{9,10},{10,1... | collective-permute-start | bytes 258056 | tf_op jit(solution)/shard_map/ppermute | solution.py:593
  57.1 1.3 %collective-permute-start.3 = (bf16[336,128]{1,0:T(8,128)(2,1)S(1)}, bf16[336,128]{1,0:T(8,128)(2,1)S(1)}, u32[]{:S(2)}, u32[]{:S(2)}) collective-permute-start(bf16[336,128]{1,0:T(8,128)(2,1)S(1)} %get-tuple-element.30), channel_id=1, source_target_pairs={{1,0},{2,1},{3,2},{4,3},{5,4},{6,5},{7,6},{8,7},{9,8},{10,9},{11,1... | collective-permute-start | bytes 258056 | tf_op jit(solution)/shard_map/ppermute | solution.py:592
  58.4 0.0 copy-start.15
  58.4 0.0 copy-start.16
  58.4 0.3 pack_forcing.1
  58.7 4.1 %collective-permute-start.6 = (bf16[16,128]{1,0:T(8,128)(2,1)S(1)}, bf16[16,128]{1,0:T(8,128)(2,1)S(1)}, u32[]{:S(2)}, u32[]{:S(2)}) collective-permute-start(bf16[16,128]{1,0:T(8,128)(2,1)S(1)} %get-tuple-element.41), channel_id=1, source_target_pairs={{0,1},{1,2},{2,3},{3,4},{4,5},{5,6},{6,7},{7,8},{8,9},{9,10},{10,1... | collective-permute-start | bytes 12296 | tf_op jit(solution)/shard_map/ppermute | solution.py:625
  62.9 1.3 %collective-permute-start.7 = (bf16[16,128]{1,0:T(8,128)(2,1)S(1)}, bf16[16,128]{1,0:T(8,128)(2,1)S(1)}, u32[]{:S(2)}, u32[]{:S(2)}) collective-permute-start(bf16[16,128]{1,0:T(8,128)(2,1)S(1)} %get-tuple-element.42), channel_id=1, source_target_pairs={{1,0},{2,1},{3,2},{4,3},{5,4},{6,5},{7,6},{8,7},{9,8},{10,9},{11,1... | collective-permute-start | bytes 12296 | tf_op jit(solution)/shard_map/ppermute | solution.py:624
  64.2 2.9 %coefficients.1 = (f32[5,27,80,128]{3,2,1,0:T(8,128)S(1)}, f32[27,80,128]{2,1,0:T(8,128)S(1)}, f32[27,80,128]{2,1,0:T(8,128)S(1)}, f32[27,8,128]{2,1,0:T(8,128)S(1)}) custom-call(bf16[6,336,128]{2,1,0:T(8,128)(2,1)S(1)} %collective-permute-done.before_ref, bf16[8,336,128]{2,1,0:T(8,128)(2,1)S(1)} %rows.1.z_ref, ...), custom_call_target="tpu_custom_call" | custom-call | flops 4000000000 | bytes 12000000 | tf_op jit(solution)/shard_map/coefficients/pallas_call | solution.py:627
  67.1 0.1 collective-permute-done.7.refs_8_
  67.2 4.8 %temperature.1 = (f32[640,128]{1,0:T(8,128)S(1)}, f32[512,128]{1,0:T(8,128)}) custom-call(f32[27,80,128]{2,1,0:T(8,128)S(1)} %get-tuple-element.38.refs_0_, f32[5,27,80,128]{3,2,1,0:T(8,128)S(1)} %get-tuple-element.39.refs_1_, f32[27,8,128]{2,1,0:T(8,128)S(1)} %get-tuple-element.40.refs_2_, bf16[80,240]{1,0:T(8,128)(2,1)S(1)} %pad_maximum_fusion.1.mix_ref.refs_3_, ...), custom_call_target="tpu_custom_call" | custom-call | flops 6000000000 | bytes 18000000 | tf_op jit(solution)/shard_map/temperature/pallas_call | solution.py:648
  72.0 23.4 %all-to-all-start.1 = ((f32[128,4,128]{2,1,0:T(4,128)}), f32[128,4,128]{2,1,0:T(4,128)S(1)}, u32[]{:S(2)}, u32[]{:S(2)}) async-start(f32[128,4,128]{2,1,0:T(4,128)} %bitcast.13), calls=%async_computation.1 | async-start | bytes 524288 | tf_op jit(solution)/shard_map/all_to_all | solution.py:657
  95.5 2.6 %copy-done.22 = f32[5,27,80,128]{3,2,1,0:T(8,128)S(1)} copy-done((f32[5,27,80,128]{3,2,1,0:T(8,128)S(1)}, f32[5,27,80,128]{3,2,1,0:T(8,128)}, u32[]{:S(2)}) %copy-start.22) | copy-done | bytes 5529624
  98.0 0.8 copy-done.24
  98.9 1.2 %copy-done.26 = f32[27,80,128]{2,1,0:T(8,128)S(1)} copy-done((f32[27,80,128]{2,1,0:T(8,128)S(1)}, f32[27,80,128]{2,1,0:T(8,128)}, u32[]{:S(2)}) %copy-start.26) | copy-done | bytes 1105944
  100.1 4.4 %salinity.1 = f32[640,128]{1,0:T(8,128)S(1)} custom-call(f32[27,80,128]{2,1,0:T(8,128)S(1)} %copy-done.26, f32[5,27,80,128]{3,2,1,0:T(8,128)S(1)} %copy-done.22, f32[27,8,128]{2,1,0:T(8,128)S(1)} %get-tuple-element.40.refs_2_, bf16[80,240]{1,0:T(8,128)(2,1)S(1)} %pad_maximum_fusion.1.mix_ref.refs_3_, f32[128,128]{1,0:T(8,128)S(1)} %copy-done.24, ...), custom_call_target="tpu_custom_call" | custom-call | flops 6000000000 | bytes 18000000 | tf_op jit(solution)/shard_map/salinity/pallas_call | solution.py:666
  104.6 0.9 pad_maximum_fusion
  105.5 0.4 copy-done.5
  105.9 2.6 %atmosphere.1 = f32[4,72,512]{2,1,0:T(8,128)} custom-call(f32[4,72,512]{2,1,0:T(8,128)S(1)} %copy-done.5, f32[4,8,512]{2,1,0:T(8,128)S(1)} %copy-done.28, f32[72,72]{1,0:T(8,128)S(1)} %copy-done.9), custom_call_target="tpu_custom_call" | custom-call | flops 3000000000 | bytes 9000000 | tf_op jit(solution)/shard_map/atmosphere/pallas_call | solution.py:659
  108.5 2.3 %all-to-all-done.1 = f32[128,4,128]{2,1,0:T(4,128)S(1)} async-done(((f32[128,4,128]{2,1,0:T(4,128)}), f32[128,4,128]{2,1,0:T(4,128)S(1)}, u32[]{:S(2)}, u32[]{:S(2)}) %all-to-all-start.1) | async-done | bytes 262176 | tf_op jit(solution)/shard_map/all_to_all | solution.py:657
  110.8 0.9 finish.1
  (55 shorter events, 0.1 us)
Async XLA Ops:
  0.6 0.7 copy-start.1
  1.3 1.1 copy-start.4
  2.4 0.8 copy-start.8
  3.1 0.7 copy-start.12
  3.8 21.5 %copy-start.3 = (f32[2,80,8,128]{3,2,1,0:T(8,128)S(1)}, f32[2,80,8,128]{3,2,1,0:T(8,128)}, u32[]{:S(2)}) copy-start(f32[2,80,8,128]{3,2,1,0:T(8,128)} %param.17) | copy-start | bytes 1966084
  3.8 21.5 %copy-start.7 = (bf16[2,80,8,128]{3,2,1,0:T(8,128)(2,1)S(1)}, bf16[2,80,8,128]{3,2,1,0:T(8,128)(2,1)}, u32[]{:S(2)}) copy-start(bf16[2,80,8,128]{3,2,1,0:T(8,128)(2,1)} %param.19) | copy-start | bytes 983044
  3.8 21.5 %copy-start.11 = (s32[8,128]{1,0:T(8,128)S(1)}, s32[8,128]{1,0:T(8,128)}, u32[]{:S(2)}) copy-start(s32[8,128]{1,0:T(8,128)} %wet_ref.2) | copy-start | bytes 12292
  6.8 18.5 %copy-start.27 = (f32[4,8,512]{2,1,0:T(8,128)}, f32[4,8,512]{2,1,0:T(8,128)S(1)}, u32[]{:S(2)}) copy-start(f32[4,8,512]{2,1,0:T(8,128)S(1)} %get-tuple-element.45.g_ref) | copy-start | bytes 196612
  6.9 40.5 %all-to-all-start = ((bf16[128,16,128]{2,1,0:T(8,128)(2,1)}), bf16[128,16,128]{2,1,0:T(8,128)(2,1)S(1)}, u32[]{:S(2)}, u32[]{:S(2)}) async-start(bf16[128,16,128]{2,1,0:T(8,128)(2,1)} %bitcast.6), calls=%async_computation | async-start | bytes 1048576 | tf_op jit(solution)/shard_map/all_to_all | solution.py:575
  25.6 7.2 %copy-start.13 = (s32[1,1,64]{2,1,0:T(1,128)S(1)}, s32[1,1,64]{2,1,0:T(1,128)}, u32[]{:S(2)}) copy-start(s32[1,1,64]{2,1,0:T(1,128)} %param.24) | copy-start | bytes 772
  25.6 8.1 %copy-start.2 = (s32[1,1,128,2]{2,3,1,0:T(2,128)S(1)}, s32[1,1,128,2]{2,3,1,0:T(2,128)}, u32[]{:S(2)}) copy-start(s32[1,1,128,2]{2,3,1,0:T(2,128)} %param.23) | copy-start | bytes 3076
  25.6 10.0 %copy-start.6 = (bf16[1,1,64,4096]{3,2,1,0:T(8,128)(2,1)S(1)}, bf16[1,1,64,4096]{3,2,1,0:T(8,128)(2,1)}, u32[]{:S(2)}) copy-start(bf16[1,1,64,4096]{3,2,1,0:T(8,128)(2,1)} %param.22) | copy-start | bytes 1572868
  26.7 27.5 %collective-permute-start = (bf16[6,336,128]{2,1,0:T(8,128)(2,1)}, bf16[6,336,128]{2,1,0:T(8,128)(2,1)S(1)}, u32[]{:S(2)}, u32[]{:S(2)}) collective-permute-start(bf16[6,336,128]{2,1,0:T(8,128)(2,1)} %get-tuple-element.52), channel_id=1, source_target_pairs={{0,16},{16,32},{32,48},{48,64},{64,80},{80,96},{96,112},{112,128},... | collective-permute-start | bytes 1548296 | tf_op jit(solution)/shard_map/ppermute | solution.py:586
  30.4 23.9 %collective-permute-start.1 = (bf16[6,336,128]{2,1,0:T(8,128)(2,1)}, bf16[6,336,128]{2,1,0:T(8,128)(2,1)S(1)}, u32[]{:S(2)}, u32[]{:S(2)}) collective-permute-start(bf16[6,336,128]{2,1,0:T(8,128)(2,1)} %get-tuple-element.51), channel_id=1, source_target_pairs={{16,0},{32,16},{48,32},{64,48},{80,64},{96,80},{112,96},{128,112},... | collective-permute-start | bytes 1548296 | tf_op jit(solution)/shard_map/ppermute | solution.py:587
  35.6 1.9 %copy-start = (f32[80,80]{1,0:T(8,128)S(1)}, f32[80,80]{1,0:T(8,128)}, u32[]{:S(2)}) copy-start(f32[80,80]{1,0:T(8,128)} %refs_11_.1) | copy-start | bytes 76804
  35.6 11.8 %copy-start.10 = (f32[2,8,128]{2,1,0:T(8,128)S(1)}, f32[2,8,128]{2,1,0:T(8,128)}, u32[]{:S(2)}) copy-start(f32[2,8,128]{2,1,0:T(8,128)} %u_ref.1) | copy-start | bytes 24580
  36.7 0.8 copy-start.18
  47.4 1.0 copy-start.19
  48.4 5.8 %copy-start.14 = (bf16[2560,256]{1,0:T(8,128)(2,1)S(1)}, bf16[2560,256]{1,0:T(8,128)(2,1)}, u32[]{:S(2)}) copy-start(bf16[2560,256]{1,0:T(8,128)(2,1)} %constant.43.clone.pack_ref) | copy-start | bytes 3932164
  49.9 17.3 %copy-start.23 = (f32[128,128]{1,0:T(8,128)}, f32[128,128]{1,0:T(8,128)S(1)}, u32[]{:S(2)}) copy-start(f32[128,128]{1,0:T(8,128)S(1)} %get-tuple-element.32.f_ref.refs_4_) | copy-start | bytes 196612
  49.9 8.5 %collective-permute-start.4 = (bf16[5,16,128]{2,1,0:T(8,128)(2,1)S(1)}, bf16[5,16,128]{2,1,0:T(8,128)(2,1)S(1)}, u32[]{:S(2)}, u32[]{:S(2)}) collective-permute-start(bf16[5,16,128]{2,1,0:T(8,128)(2,1)S(1)} %get-tuple-element.33), channel_id=1, source_target_pairs={{0,16},{16,32},{32,48},{48,64},{64,80},{80,96},{96,112},{112,128},... | collective-permute-start | bytes 61448 | tf_op jit(solution)/shard_map/ppermute | solution.py:617
  51.8 6.6 %collective-permute-start.5 = (bf16[5,16,128]{2,1,0:T(8,128)(2,1)S(1)}, bf16[5,16,128]{2,1,0:T(8,128)(2,1)S(1)}, u32[]{:S(2)}, u32[]{:S(2)}) collective-permute-start(bf16[5,16,128]{2,1,0:T(8,128)(2,1)S(1)} %get-tuple-element.34), channel_id=1, source_target_pairs={{16,0},{32,16},{48,32},{64,48},{80,64},{96,80},{112,96},{128,112},... | collective-permute-start | bytes 61448 | tf_op jit(solution)/shard_map/ppermute | solution.py:618
  54.9 9.3 %collective-permute-start.2 = (bf16[336,128]{1,0:T(8,128)(2,1)S(1)}, bf16[336,128]{1,0:T(8,128)(2,1)S(1)}, u32[]{:S(2)}, u32[]{:S(2)}) collective-permute-start(bf16[336,128]{1,0:T(8,128)(2,1)S(1)} %get-tuple-element.29), channel_id=1, source_target_pairs={{0,1},{1,2},{2,3},{3,4},{4,5},{5,6},{6,7},{7,8},{8,9},{9,10},{10,1... | collective-permute-start | bytes 258056 | tf_op jit(solution)/shard_map/ppermute | solution.py:593
  57.1 7.1 %collective-permute-start.3 = (bf16[336,128]{1,0:T(8,128)(2,1)S(1)}, bf16[336,128]{1,0:T(8,128)(2,1)S(1)}, u32[]{:S(2)}, u32[]{:S(2)}) collective-permute-start(bf16[336,128]{1,0:T(8,128)(2,1)S(1)} %get-tuple-element.30), channel_id=1, source_target_pairs={{1,0},{2,1},{3,2},{4,3},{5,4},{6,5},{7,6},{8,7},{9,8},{10,9},{11,1... | collective-permute-start | bytes 258056 | tf_op jit(solution)/shard_map/ppermute | solution.py:592
  58.4 5.8 %copy-start.15 = (bf16[256,896]{1,0:T(8,128)(2,1)S(1)}, bf16[256,896]{1,0:T(8,128)(2,1)}, u32[]{:S(2)}) copy-start(bf16[256,896]{1,0:T(8,128)(2,1)} %constant.44.clone.spread_ref.refs_9_) | copy-start | bytes 1376260
  58.4 5.8 %copy-start.16 = (bf16[384,128]{1,0:T(8,128)(2,1)S(1)}, bf16[384,128]{1,0:T(8,128)(2,1)}, u32[]{:S(2)}) copy-start(bf16[384,128]{1,0:T(8,128)(2,1)} %constant.45.clone.own_ref.refs_10_) | copy-start | bytes 294916
  58.7 8.5 %copy-start.17 = (f32[2,8,128]{2,1,0:T(8,128)S(1)}, f32[2,8,128]{2,1,0:T(8,128)}, u32[]{:S(2)}) copy-start(f32[2,8,128]{2,1,0:T(8,128)} %get-tuple-element.24.refs_14_) | copy-start | bytes 24580
  58.7 8.5 %copy-start.20 = (bf16[1024,256]{1,0:T(8,128)(2,1)S(1)}, bf16[1024,256]{1,0:T(8,128)(2,1)}, u32[]{:S(2)}) copy-start(bf16[1024,256]{1,0:T(8,128)(2,1)} %copy-done.18) | copy-start | bytes 1572868
  58.7 8.4 %collective-permute-start.6 = (bf16[16,128]{1,0:T(8,128)(2,1)S(1)}, bf16[16,128]{1,0:T(8,128)(2,1)S(1)}, u32[]{:S(2)}, u32[]{:S(2)}) collective-permute-start(bf16[16,128]{1,0:T(8,128)(2,1)S(1)} %get-tuple-element.41), channel_id=1, source_target_pairs={{0,1},{1,2},{2,3},{3,4},{4,5},{5,6},{6,7},{7,8},{8,9},{9,10},{10,1... | collective-permute-start | bytes 12296 | tf_op jit(solution)/shard_map/ppermute | solution.py:625
  62.9 4.4 %collective-permute-start.7 = (bf16[16,128]{1,0:T(8,128)(2,1)S(1)}, bf16[16,128]{1,0:T(8,128)(2,1)S(1)}, u32[]{:S(2)}, u32[]{:S(2)}) collective-permute-start(bf16[16,128]{1,0:T(8,128)(2,1)S(1)} %get-tuple-element.42), channel_id=1, source_target_pairs={{1,0},{2,1},{3,2},{4,3},{5,4},{6,5},{7,6},{8,7},{9,8},{10,9},{11,1... | collective-permute-start | bytes 12296 | tf_op jit(solution)/shard_map/ppermute | solution.py:624
  67.1 4.9 %copy-start.21 = (f32[5,27,80,128]{3,2,1,0:T(8,128)}, f32[5,27,80,128]{3,2,1,0:T(8,128)S(1)}, u32[]{:S(2)}) copy-start(f32[5,27,80,128]{3,2,1,0:T(8,128)S(1)} %get-tuple-element.39.refs_1_) | copy-start | bytes 16588804
  67.1 4.9 %copy-start.25 = (f32[27,80,128]{2,1,0:T(8,128)}, f32[27,80,128]{2,1,0:T(8,128)S(1)}, u32[]{:S(2)}) copy-start(f32[27,80,128]{2,1,0:T(8,128)S(1)} %get-tuple-element.47.refs_0_) | copy-start | bytes 3317764
  72.0 38.8 %all-to-all-start.1 = ((f32[128,4,128]{2,1,0:T(4,128)}), f32[128,4,128]{2,1,0:T(4,128)S(1)}, u32[]{:S(2)}, u32[]{:S(2)}) async-start(f32[128,4,128]{2,1,0:T(4,128)} %bitcast.13), calls=%async_computation.1 | async-start | bytes 524288 | tf_op jit(solution)/shard_map/all_to_all | solution.py:657
  95.5 2.6 %copy-start.22 = (f32[5,27,80,128]{3,2,1,0:T(8,128)S(1)}, f32[5,27,80,128]{3,2,1,0:T(8,128)}, u32[]{:S(2)}) copy-start(f32[5,27,80,128]{3,2,1,0:T(8,128)} %copy-done.21) | copy-start | bytes 16588804
  98.0 0.8 copy-start.24
  98.9 1.2 %copy-start.26 = (f32[27,80,128]{2,1,0:T(8,128)S(1)}, f32[27,80,128]{2,1,0:T(8,128)}, u32[]{:S(2)}) copy-start(f32[27,80,128]{2,1,0:T(8,128)} %copy-done.25) | copy-start | bytes 3317764
  104.6 1.3 %copy-start.5 = (f32[4,72,512]{2,1,0:T(8,128)S(1)}, f32[4,72,512]{2,1,0:T(8,128)}, u32[]{:S(2)}) copy-start(f32[4,72,512]{2,1,0:T(8,128)} %a_ref.3) | copy-start | bytes 1769476
  104.6 1.3 %copy-start.9 = (f32[72,72]{1,0:T(8,128)S(1)}, f32[72,72]{1,0:T(8,128)}, u32[]{:S(2)}) copy-start(f32[72,72]{1,0:T(8,128)} %m_ref.3) | copy-start | bytes 62212
  104.6 1.3 %copy-start.28 = (f32[4,8,512]{2,1,0:T(8,128)S(1)}, f32[4,8,512]{2,1,0:T(8,128)}, u32[]{:S(2)}) copy-start(f32[4,8,512]{2,1,0:T(8,128)} %copy-done.27) | copy-start | bytes 196612

commit v3 on v2

--- a/solution.py
+++ b/solution.py
@@ -120,7 +120,17 @@
     return power
 
 
-def flux_body(table_ref, a_ref, m_ref, sst_ref, pay_ref, g_hbm, block_ref, g_ref, sem):
+def flux_body(
+    table_ref, a_hbm, m_hbm, sst_hbm, pay_ref, g_hbm, block_ref, g_ref, a_ref, m_ref, sst_ref, sems, sem
+):
+    loads = [
+        pltpu.make_async_copy(m_hbm, m_ref, sems.at[0]),
+        pltpu.make_async_copy(sst_hbm, sst_ref, sems.at[1]),
+        pltpu.make_async_copy(a_hbm, a_ref, sems.at[2]),
+    ]
+    for load in loads:
+        load.start()
+    loads[0].wait()
     levels = m_ref.shape[0]
     bottom = levels - 1
     power = mixing_powers(m_ref)
@@ -129,6 +139,8 @@
     rows = jnp.concatenate(rows + [jnp.zeros((8 - STEPS, levels), f32)], axis=0)
     row_high, row_low = halves(rows)
     both = jnp.concatenate([row_high.astype(f32), row_low.astype(f32)], axis=0).astype(bf16)
+    loads[1].wait()
+    loads[2].wait()
     base = []
     for v in range(4):
         high, low = halves(a_ref[v])
@@ -462,10 +474,10 @@
     x_ref, coef_ref, wet_ref, mix_ref, f_ref, before_ref, after_ref, west_ref, east_ref = refs[:9]
     spread_ref, own_ref = refs[9:11]
     if t == 0:
-        column_ref, w_ref, place_ref, u_ref, out_ref, send_ref = refs[11:17]
-        one_ref, two_ref, force_ref, cat_ref, sst_ref = refs[17:]
+        column_ref, w_ref, place_ref, u_ref, out_hbm, send_ref = refs[11:17]
+        one_ref, two_ref, force_ref, cat_ref, out_ref, sem, sst_ref = refs[17:]
     else:
-        out_ref, one_ref, two_ref, force_ref, cat_ref = refs[11:]
+        _, out_hbm, one_ref, two_ref, force_ref, cat_ref, out_ref, sem = refs[11:]
     levels = mix_ref.shape[0]
     rows = forcing_rows(f_ref, before_ref, after_ref)
     sides = jnp.concatenate([east_ref[...], west_ref[...]], axis=1)
@@ -518,10 +530,13 @@
             out_ref[pl.ds(lo * ROWS + r, 16, stride=ROWS), :] = value
             if t == 0 and lo == 0:
                 sst_ref[r : r + 1, :] = value[0:1]
+    copy = pltpu.make_async_copy(out_ref, out_hbm.at[t], sem)
+    copy.start()
     if t == 0:
         fields = [sst_ref[...], u_ref[0], u_ref[1]]
         fields = [field.astype(bf16).astype(f32) for field in fields]
         send_ref[...] = returned_rows(fields, w_ref, place_ref[...], send_ref.shape[0])
+    copy.wait()
 
 
 def neighbours(size):
@@ -562,13 +577,18 @@
         flux_body,
         (shape((peers * 16, LANES), bf16), shape((4, 8, air_columns))),
         "fluxes",
-        [SMEM, VMEM, VMEM, VMEM],
+        [SMEM, HBM, HBM, HBM],
         (VMEM, HBM),
         scratch=[
             pltpu.VMEM((64, LANES), f32),
             pltpu.VMEM((4, 8, air_columns), f32),
+            pltpu.VMEM(atmosphere_level_state.shape, f32),
+            pltpu.VMEM(atmosphere_mixing_map.shape, f32),
+            pltpu.VMEM((1, air_columns), f32),
+            pltpu.SemaphoreType.DMA((3,)),
             pltpu.SemaphoreType.DMA,
         ],
+        limit=56,
         micros=3,
     )(table, atmosphere_level_state, atmosphere_mixing_map, sea_surface_temps[None])
     payload, wet_rows = lax.optimization_barrier((payload, ocean_cell_mask))
@@ -607,6 +627,8 @@
     mix = jnp.concatenate([upper, lower, upper], axis=1)
     wide = (TILES, levels, LANES)
     cat = pltpu.VMEM((2, 3 * levels, 4 * LANES), bf16)
+    arrived, east_in, west_in = lax.optimization_barrier((arrived, east_in, west_in))
+
     edge_rows = shape((HALO - 1, 16, LANES), bf16)
     forcing, send_up, send_down, ocean_currents = call(
         remap_body,
@@ -644,12 +666,15 @@
         pltpu.VMEM(wide, f32),
         pltpu.VMEM((TILES, 8, LANES), f32),
         cat,
+        pltpu.VMEM(flat.shape[1:], f32),
+        pltpu.SemaphoreType.DMA,
     ]
     warm, terms = call(
         functools.partial(tracer_body, 0),
-        (shape(flat.shape[1:]), shape((peers * 4, LANES))),
+        (shape(flat.shape), shape((peers * 4, LANES))),
         "temperature",
         [VMEM] * 15,
+        (HBM, VMEM),
         scratch=scratch + [pltpu.VMEM((ROWS, LANES), f32)],
         limit=24,
         micros=6,
@@ -663,20 +688,21 @@
         [VMEM] * 3,
         micros=3,
     )(atmosphere_level_state, gained, atmosphere_mixing_map)
-    cold = call(
+    both = call(
         functools.partial(tracer_body, 1),
-        shape(flat.shape[1:]),
+        shape(flat.shape),
         "salinity",
-        [VMEM] * 11,
+        [VMEM] * 11 + [HBM],
+        HBM,
         scratch=scratch,
+        aliases={11: 0},
         limit=24,
         micros=6,
-    )(salt, *shared)
+    )(salt, *shared, warm)
     returned = call(finish_body, shape((3, air_columns)), "finish", [VMEM, VMEM])(
         jnp.repeat(table, 4, axis=1), home
     )
-    ocean_tracers = jnp.stack([warm, cold]).reshape(tracers.shape)
-    return (atm_final, ocean_tracers, ocean_currents, returned)
+    return (atm_final, both.reshape(tracers.shape), ocean_currents, returned)
 
 
 def solution(mesh):

time: 113 us -> 135 us (1.19)
  waiting for transfers between devices: 12.1 us -> 24.9 us
  starting transfers between devices: 60.6 us -> 73 us
  local copies, waits for them, and re-layouts: 13.8 us -> 9.15 us
  Pallas kernels: 22.4 us -> 25.2 us
    all_to_all x1, starting transfers between devices: 23.4 us -> 34.4 us  [on_device(): home = lax.all_to_all(terms, band, 0, 0, tiled=True)]
    all_to_all x1, waiting for transfers between devices: 9.76 us -> 0.01 us  [on_device(): arrived = lax.all_to_all(payload, band, 0, 0, tiled=True)]
    ppermute x1, waiting for transfers between devices: 0.01 us -> 8.18 us  [on_device(): before = lax.ppermute(z[ROWS - HALO:], rows_axis, up)]
    ppermute x1, waiting for transfers between devices: 0.01 us -> 5.56 us  [on_device(): after = lax.ppermute(z[:HALO], rows_axis, down)]
    all_to_all x1, waiting for transfers between devices: 2.3 us -> 7.62 us  [on_device(): home = lax.all_to_all(terms, band, 0, 0, tiled=True)]
    ppermute x1, waiting for transfers between devices: 0.01 us -> 3.52 us  [on_device(): f_after = lax.ppermute(send_down, rows_axis, down)]
    unnamed x59 -> x47, local copies, waits for them, and re-layouts: 10.6 us -> 7.62 us
    ppermute x1, starting transfers between devices: 2.19 us -> 3.99 us  [on_device(): west_in = lax.ppermute(last, 'col', right)]
  transfers between devices with their start and end apart: 10 -> 10, of which waited for: 3 -> 4; matrix products, arithmetic and copies ran while one was open for 5% -> 2% of each run, Pallas kernels for 12% -> 7%
where the time goes in v3:
time: 135 us; the launch traced here: 134 us
  starting transfers between devices  73 us (54%)
  Pallas kernels  25.2 us (19%)
  waiting for transfers between devices  24.9 us (18%)
  local copies, waits for them, and re-layouts  9.15 us (7%)
    all_to_all x1, starting transfers between devices, on_device(): home = lax.all_to_all(terms, band, 0, 0, tiled=True)  34.4 us
    all_to_all x1, starting transfers between devices, on_device(): arrived = lax.all_to_all(payload, band, 0, 0, tiled=True)  18.4 us
    ppermute x1, waiting for transfers between devices, on_device(): before = lax.ppermute(z[ROWS - HALO:], rows_axis, up)  8.18 us
    all_to_all x1, waiting for transfers between devices, on_device(): home = lax.all_to_all(terms, band, 0, 0, tiled=True)  7.62 us
    unnamed x47, local copies, waits for them, and re-layouts  7.62 us
    ppermute x1, waiting for transfers between devices, on_device(): after = lax.ppermute(z[:HALO], rows_axis, down)  5.56 us
    pallas_call x1, Pallas kernels, on_device(): call(functools.partial(tracer_body, 0), (shape(flat.shape), shape((peers...  5.3 us
    pallas_call x1, Pallas kernels, on_device(): call(functools.partial(tracer_body, 1), shape(flat.shape), 'salinity', [V...  5.13 us
  transfers between devices with their start and end apart: 10, of which 4 were waited for; matrix products, arithmetic and copies ran while one was open for 2% of the time, Pallas kernels for 7%

profile of v3, /device:TPU:1, one launch (start us, length us, event | category | flops | bytes accessed | tf_op | source)
XLA Modules:
  0.0 134.2 jit_solution(13334301444947141830)
XLA Ops:
  0.7 4.6 %fluxes.1 = (bf16[2048,128]{1,0:T(8,128)(2,1)}, f32[4,8,512]{2,1,0:T(8,128)}) custom-call(s32[2,128]{1,0:T(2,128)} %bitcast.23, f32[4,72,512]{2,1,0:T(8,128)} %a_ref.1, f32[72,72]{1,0:T(8,128)} %m_ref.1, f32[1,512]{1,0:T(1,128)} %bitcast.25), custom_call_target="tpu_custom_call" | custom-call | flops 3000000000 | bytes 9000000 | tf_op jit(solution)/shard_map/fluxes/pallas_call | solution.py:576
  5.3 18.4 %all-to-all-start = ((bf16[128,16,128]{2,1,0:T(8,128)(2,1)}), bf16[128,16,128]{2,1,0:T(8,128)(2,1)S(1)}, u32[]{:S(2)}, u32[]{:S(2)}) async-start(bf16[128,16,128]{2,1,0:T(8,128)(2,1)} %bitcast.21), calls=%async_computation | async-start | bytes 1048576 | tf_op jit(solution)/shard_map/all_to_all | solution.py:595
  23.8 0.2 rows.1.z_ref
  24.0 0.0 copy-start.8
  24.0 0.0 copy-start
  24.0 1.1 fusion.3
  25.1 3.6 %collective-permute-start = (bf16[6,336,128]{2,1,0:T(8,128)(2,1)}, bf16[6,336,128]{2,1,0:T(8,128)(2,1)S(1)}, u32[]{:S(2)}, u32[]{:S(2)}) collective-permute-start(bf16[6,336,128]{2,1,0:T(8,128)(2,1)} %get-tuple-element.58), channel_id=1, source_target_pairs={{0,16},{16,32},{32,48},{48,64},{64,80},{80,96},{96,112},{112,128},... | collective-permute-start | bytes 1548296 | tf_op jit(solution)/shard_map/ppermute | solution.py:606
  28.7 1.9 %collective-permute-start.1 = (bf16[6,336,128]{2,1,0:T(8,128)(2,1)}, bf16[6,336,128]{2,1,0:T(8,128)(2,1)S(1)}, u32[]{:S(2)}, u32[]{:S(2)}) collective-permute-start(bf16[6,336,128]{2,1,0:T(8,128)(2,1)} %get-tuple-element.57), channel_id=1, source_target_pairs={{16,0},{32,16},{48,32},{64,48},{80,64},{96,80},{112,96},{128,112},... | collective-permute-start | bytes 1548296 | tf_op jit(solution)/shard_map/ppermute | solution.py:607
  30.7 0.5 broadcast.196
  31.2 0.7 reduce.3
  31.8 0.1 reshape_reshape.3
  31.9 0.1 copy.20
  32.0 0.1 reshape.218
  32.1 0.1 pad_maximum_fusion.mix_ref.refs_3_
  32.3 0.0 copy-start.3
  32.3 8.2 %collective-permute-done.before_ref = bf16[6,336,128]{2,1,0:T(8,128)(2,1)S(1)} collective-permute-done((bf16[6,336,128]{2,1,0:T(8,128)(2,1)}, bf16[6,336,128]{2,1,0:T(8,128)(2,1)S(1)}, u32[]{:S(2)}, u32[]{:S(2)}) %collective-permute-start) | collective-permute-done | bytes 516128 | tf_op jit(solution)/shard_map/ppermute | solution.py:606
  40.5 5.6 %collective-permute-done.1.after_ref = bf16[6,336,128]{2,1,0:T(8,128)(2,1)S(1)} collective-permute-done((bf16[6,336,128]{2,1,0:T(8,128)(2,1)}, bf16[6,336,128]{2,1,0:T(8,128)(2,1)S(1)}, u32[]{:S(2)}, u32[]{:S(2)}) %collective-permute-start.1) | collective-permute-done | bytes 516128 | tf_op jit(solution)/shard_map/ppermute | solution.py:607
  46.0 1.3 copy-done.9
  47.3 0.6 pack.1
  48.0 1.3 collective-permute-start.2
  49.3 4.0 %collective-permute-start.3 = (bf16[336,128]{1,0:T(8,128)(2,1)S(1)}, bf16[336,128]{1,0:T(8,128)(2,1)S(1)}, u32[]{:S(2)}, u32[]{:S(2)}) collective-permute-start(bf16[336,128]{1,0:T(8,128)(2,1)S(1)} %get-tuple-element.34), channel_id=1, source_target_pairs={{0,1},{1,2},{2,3},{3,4},{4,5},{5,6},{6,7},{7,8},{8,9},{9,10},{10,1... | collective-permute-start | bytes 258056 | tf_op jit(solution)/shard_map/ppermute | solution.py:613
  53.3 0.0 copy-start.6
  53.3 1.1 cells.1.w_ref.refs_12_
  54.4 0.0 copy-start.14
  54.4 0.8 copy-done.14
  55.2 0.0 all-to-all-done
  55.2 1.0 copy-done.15
  56.2 1.5 %remap.1 = (f32[128,128]{1,0:T(8,128)S(1)}, bf16[5,16,128]{2,1,0:T(8,128)(2,1)S(1)}, bf16[5,16,128]{2,1,0:T(8,128)(2,1)S(1)}, f32[2,8,128]{2,1,0:T(8,128)}) custom-call(s32[1,64]{1,0:T(1,128)S(1)} %bitcast.20, bf16[2048,128]{1,0:T(8,128)(2,1)S(1)} %bitcast.14, bf16[1024,256]{1,0:T(8,128)(2,1)S(1)} %copy-done.15, f32[2,8,128]{2,1,0:T(8,128)S(1)} %copy-done.6, ...), custom_call_target="tpu_custom_call" | custom-call | flops 1000000000 | bytes 3000000 | tf_op jit(solution)/shard_map/remap/pallas_call | solution.py:633
  57.7 2.4 %collective-permute-start.4 = (bf16[5,16,128]{2,1,0:T(8,128)(2,1)S(1)}, bf16[5,16,128]{2,1,0:T(8,128)(2,1)S(1)}, u32[]{:S(2)}, u32[]{:S(2)}) collective-permute-start(bf16[5,16,128]{2,1,0:T(8,128)(2,1)S(1)} %get-tuple-element.39), channel_id=1, source_target_pairs={{0,16},{16,32},{32,48},{48,64},{64,80},{80,96},{96,112},{112,128},... | collective-permute-start | bytes 61448 | tf_op jit(solution)/shard_map/ppermute | solution.py:639
  60.1 1.9 %collective-permute-start.5 = (bf16[5,16,128]{2,1,0:T(8,128)(2,1)S(1)}, bf16[5,16,128]{2,1,0:T(8,128)(2,1)S(1)}, u32[]{:S(2)}, u32[]{:S(2)}) collective-permute-start(bf16[5,16,128]{2,1,0:T(8,128)(2,1)S(1)} %get-tuple-element.40), channel_id=1, source_target_pairs={{16,0},{32,16},{48,32},{64,48},{80,64},{96,80},{112,96},{128,112},... | collective-permute-start | bytes 61448 | tf_op jit(solution)/shard_map/ppermute | solution.py:640
  62.0 0.1 pad_add_fusion.refs_13_
  62.1 0.1 broadcast_in_dim.13
  62.2 0.1 reshape.220.table_ref
  62.4 3.5 %collective-permute-done.5.after_ref.refs_6_ = bf16[5,16,128]{2,1,0:T(8,128)(2,1)S(1)} collective-permute-done((bf16[5,16,128]{2,1,0:T(8,128)(2,1)S(1)}, bf16[5,16,128]{2,1,0:T(8,128)(2,1)S(1)}, u32[]{:S(2)}, u32[]{:S(2)}) %collective-permute-start.5) | collective-permute-done | bytes 20512 | tf_op jit(solution)/shard_map/ppermute | solution.py:640
  65.9 1.3 copy-done.10
  67.2 0.3 pack_forcing.1
  67.5 3.5 %collective-permute-start.6 = (bf16[16,128]{1,0:T(8,128)(2,1)S(1)}, bf16[16,128]{1,0:T(8,128)(2,1)S(1)}, u32[]{:S(2)}, u32[]{:S(2)}) collective-permute-start(bf16[16,128]{1,0:T(8,128)(2,1)S(1)} %get-tuple-element.47), channel_id=1, source_target_pairs={{0,1},{1,2},{2,3},{3,4},{4,5},{5,6},{6,7},{7,8},{8,9},{9,10},{10,1... | collective-permute-start | bytes 12296 | tf_op jit(solution)/shard_map/ppermute | solution.py:647
  71.0 1.5 %collective-permute-start.7 = (bf16[16,128]{1,0:T(8,128)(2,1)S(1)}, bf16[16,128]{1,0:T(8,128)(2,1)S(1)}, u32[]{:S(2)}, u32[]{:S(2)}) collective-permute-start(bf16[16,128]{1,0:T(8,128)(2,1)S(1)} %get-tuple-element.48), channel_id=1, source_target_pairs={{1,0},{2,1},{3,2},{4,3},{5,4},{6,5},{7,6},{8,7},{9,8},{10,9},{11,1... | collective-permute-start | bytes 12296 | tf_op jit(solution)/shard_map/ppermute | solution.py:646
  72.5 2.9 %coefficients.1 = (f32[5,27,80,128]{3,2,1,0:T(8,128)S(1)}, f32[27,80,128]{2,1,0:T(8,128)S(1)}, f32[27,80,128]{2,1,0:T(8,128)S(1)}, f32[27,8,128]{2,1,0:T(8,128)S(1)}) custom-call(bf16[6,336,128]{2,1,0:T(8,128)(2,1)S(1)} %collective-permute-done.before_ref, bf16[8,336,128]{2,1,0:T(8,128)(2,1)S(1)} %rows.1.z_ref, ...), custom_call_target="tpu_custom_call" | custom-call | flops 4000000000 | bytes 12000000 | tf_op jit(solution)/shard_map/coefficients/pallas_call | solution.py:649
  75.5 0.0 copy-start.2
  75.5 0.0 copy-start.5
  75.5 5.3 %temperature.1 = (f32[2,640,128]{2,1,0:T(8,128)}, f32[512,128]{1,0:T(8,128)}) custom-call(f32[27,80,128]{2,1,0:T(8,128)S(1)} %get-tuple-element.44.refs_0_, f32[5,27,80,128]{3,2,1,0:T(8,128)S(1)} %get-tuple-element.45.refs_1_, f32[27,8,128]{2,1,0:T(8,128)S(1)} %get-tuple-element.46.refs_2_, bf16[80,240]{1,0:T(8,128)(2,1)S(1)} %pad_maximum_fusion.mix_ref.refs_3_, ...), custom_call_target="tpu_custom_call" | custom-call | flops 6000000000 | bytes 18000000 | tf_op jit(solution)/shard_map/temperature/pallas_call | solution.py:672
  80.8 2.6 %atmosphere.1 = f32[4,72,512]{2,1,0:T(8,128)} custom-call(f32[4,72,512]{2,1,0:T(8,128)S(1)} %copy-done.2, f32[4,8,512]{2,1,0:T(8,128)S(1)} %copy-done.21, f32[72,72]{1,0:T(8,128)S(1)} %copy-done.5), custom_call_target="tpu_custom_call" | custom-call | flops 3000000000 | bytes 9000000 | tf_op jit(solution)/shard_map/atmosphere/pallas_call | solution.py:684
  83.5 34.4 %all-to-all-start.1 = ((f32[128,4,128]{2,1,0:T(4,128)}), f32[128,4,128]{2,1,0:T(4,128)S(1)}, u32[]{:S(2)}, u32[]{:S(2)}) async-start(f32[128,4,128]{2,1,0:T(4,128)} %bitcast.12), calls=%async_computation.1 | async-start | bytes 524288 | tf_op jit(solution)/shard_map/all_to_all | solution.py:682
  117.9 2.6 %copy-done.18 = f32[5,27,80,128]{3,2,1,0:T(8,128)S(1)} copy-done((f32[5,27,80,128]{3,2,1,0:T(8,128)S(1)}, f32[5,27,80,128]{3,2,1,0:T(8,128)}, u32[]{:S(2)}) %copy-start.18) | copy-done | bytes 5529624
  120.5 5.1 %salinity.1 = f32[2,640,128]{2,1,0:T(8,128)} custom-call(f32[27,80,128]{2,1,0:T(8,128)S(1)} %copy-done.20, f32[5,27,80,128]{3,2,1,0:T(8,128)S(1)} %copy-done.18, f32[27,8,128]{2,1,0:T(8,128)S(1)} %get-tuple-element.46.refs_2_, bf16[80,240]{1,0:T(8,128)(2,1)S(1)} %pad_maximum_fusion.mix_ref.refs_3_, ...), custom_call_target="tpu_custom_call", output_to_operand_aliasing={{}: (11, {})} | custom-call | flops 6000000000 | bytes 18000000 | tf_op jit(solution)/shard_map/salinity/pallas_call | solution.py:691
  125.6 7.6 %all-to-all-done.1 = f32[128,4,128]{2,1,0:T(4,128)S(1)} async-done(((f32[128,4,128]{2,1,0:T(4,128)}), f32[128,4,128]{2,1,0:T(4,128)S(1)}, u32[]{:S(2)}, u32[]{:S(2)}) %all-to-all-start.1) | async-done | bytes 262176 | tf_op jit(solution)/shard_map/all_to_all | solution.py:682
  133.3 0.9 finish.1
  (42 shorter events, 0.1 us)
Async XLA Ops:
  0.6 23.1 %copy-start.1 = (f32[2,80,8,128]{3,2,1,0:T(8,128)S(1)}, f32[2,80,8,128]{3,2,1,0:T(8,128)}, u32[]{:S(2)}) copy-start(f32[2,80,8,128]{3,2,1,0:T(8,128)} %param.17) | copy-start | bytes 1966084
  0.6 23.1 %copy-start.4 = (bf16[2,80,8,128]{3,2,1,0:T(8,128)(2,1)S(1)}, bf16[2,80,8,128]{3,2,1,0:T(8,128)(2,1)}, u32[]{:S(2)}) copy-start(bf16[2,80,8,128]{3,2,1,0:T(8,128)(2,1)} %param.19) | copy-start | bytes 983044
  0.7 23.1 %copy-start.7 = (s32[8,128]{1,0:T(8,128)S(1)}, s32[8,128]{1,0:T(8,128)}, u32[]{:S(2)}) copy-start(s32[8,128]{1,0:T(8,128)} %wet_ref.2) | copy-start | bytes 12292
  5.3 49.9 %all-to-all-start = ((bf16[128,16,128]{2,1,0:T(8,128)(2,1)}), bf16[128,16,128]{2,1,0:T(8,128)(2,1)S(1)}, u32[]{:S(2)}, u32[]{:S(2)}) async-start(bf16[128,16,128]{2,1,0:T(8,128)(2,1)} %bitcast.21), calls=%async_computation | async-start | bytes 1048576 | tf_op jit(solution)/shard_map/all_to_all | solution.py:595
  24.0 7.2 %copy-start.8 = (s32[1,1,64]{2,1,0:T(1,128)S(1)}, s32[1,1,64]{2,1,0:T(1,128)}, u32[]{:S(2)}) copy-start(s32[1,1,64]{2,1,0:T(1,128)} %param.24) | copy-start | bytes 772
  24.0 8.1 %copy-start = (f32[80,80]{1,0:T(8,128)S(1)}, f32[80,80]{1,0:T(8,128)}, u32[]{:S(2)}) copy-start(f32[80,80]{1,0:T(8,128)} %refs_11_.1) | copy-start | bytes 76804
  25.1 15.3 %collective-permute-start = (bf16[6,336,128]{2,1,0:T(8,128)(2,1)}, bf16[6,336,128]{2,1,0:T(8,128)(2,1)S(1)}, u32[]{:S(2)}, u32[]{:S(2)}) collective-permute-start(bf16[6,336,128]{2,1,0:T(8,128)(2,1)} %get-tuple-element.58), channel_id=1, source_target_pairs={{0,16},{16,32},{32,48},{48,64},{64,80},{80,96},{96,112},{112,128},... | collective-permute-start | bytes 1548296 | tf_op jit(solution)/shard_map/ppermute | solution.py:606
  28.7 17.3 %collective-permute-start.1 = (bf16[6,336,128]{2,1,0:T(8,128)(2,1)}, bf16[6,336,128]{2,1,0:T(8,128)(2,1)S(1)}, u32[]{:S(2)}, u32[]{:S(2)}) collective-permute-start(bf16[6,336,128]{2,1,0:T(8,128)(2,1)} %get-tuple-element.57), channel_id=1, source_target_pairs={{16,0},{32,16},{48,32},{64,48},{80,64},{96,80},{112,96},{128,112},... | collective-permute-start | bytes 1548296 | tf_op jit(solution)/shard_map/ppermute | solution.py:607
  32.3 21.0 %copy-start.3 = (bf16[1,1,64,4096]{3,2,1,0:T(8,128)(2,1)S(1)}, bf16[1,1,64,4096]{3,2,1,0:T(8,128)(2,1)}, u32[]{:S(2)}) copy-start(bf16[1,1,64,4096]{3,2,1,0:T(8,128)(2,1)} %param.22) | copy-start | bytes 1572868
  46.0 1.3 copy-start.9
  48.0 7.2 %collective-permute-start.2 = (bf16[336,128]{1,0:T(8,128)(2,1)S(1)}, bf16[336,128]{1,0:T(8,128)(2,1)S(1)}, u32[]{:S(2)}, u32[]{:S(2)}) collective-permute-start(bf16[336,128]{1,0:T(8,128)(2,1)S(1)} %get-tuple-element.33), channel_id=1, source_target_pairs={{1,0},{2,1},{3,2},{4,3},{5,4},{6,5},{7,6},{8,7},{9,8},{10,9},{11,1... | collective-permute-start | bytes 258056 | tf_op jit(solution)/shard_map/ppermute | solution.py:612
  49.3 5.9 %collective-permute-start.3 = (bf16[336,128]{1,0:T(8,128)(2,1)S(1)}, bf16[336,128]{1,0:T(8,128)(2,1)S(1)}, u32[]{:S(2)}, u32[]{:S(2)}) collective-permute-start(bf16[336,128]{1,0:T(8,128)(2,1)S(1)} %get-tuple-element.34), channel_id=1, source_target_pairs={{0,1},{1,2},{2,3},{3,4},{4,5},{5,6},{6,7},{7,8},{8,9},{9,10},{10,1... | collective-permute-start | bytes 258056 | tf_op jit(solution)/shard_map/ppermute | solution.py:613
  53.3 1.9 %copy-start.6 = (f32[2,8,128]{2,1,0:T(8,128)S(1)}, f32[2,8,128]{2,1,0:T(8,128)}, u32[]{:S(2)}) copy-start(f32[2,8,128]{2,1,0:T(8,128)} %u_ref.1) | copy-start | bytes 24580
  54.4 0.8 copy-start.14
  55.2 1.0 copy-start.15
  56.2 5.9 %copy-start.22 = (s32[1,1,128,2]{2,3,1,0:T(2,128)S(1)}, s32[1,1,128,2]{2,3,1,0:T(2,128)}, u32[]{:S(2)}) copy-start(s32[1,1,128,2]{2,3,1,0:T(2,128)} %param.23) | copy-start | bytes 3076
  57.7 4.7 %collective-permute-start.4 = (bf16[5,16,128]{2,1,0:T(8,128)(2,1)S(1)}, bf16[5,16,128]{2,1,0:T(8,128)(2,1)S(1)}, u32[]{:S(2)}, u32[]{:S(2)}) collective-permute-start(bf16[5,16,128]{2,1,0:T(8,128)(2,1)S(1)} %get-tuple-element.39), channel_id=1, source_target_pairs={{0,16},{16,32},{32,48},{48,64},{64,80},{80,96},{96,112},{112,128},... | collective-permute-start | bytes 61448 | tf_op jit(solution)/shard_map/ppermute | solution.py:639
  60.1 5.8 %collective-permute-start.5 = (bf16[5,16,128]{2,1,0:T(8,128)(2,1)S(1)}, bf16[5,16,128]{2,1,0:T(8,128)(2,1)S(1)}, u32[]{:S(2)}, u32[]{:S(2)}) collective-permute-start(bf16[5,16,128]{2,1,0:T(8,128)(2,1)S(1)} %get-tuple-element.40), channel_id=1, source_target_pairs={{16,0},{32,16},{48,32},{64,48},{80,64},{96,80},{112,96},{128,112},... | collective-permute-start | bytes 61448 | tf_op jit(solution)/shard_map/ppermute | solution.py:640
  65.9 1.3 copy-start.10
  67.2 5.3 %copy-start.11 = (bf16[256,896]{1,0:T(8,128)(2,1)S(1)}, bf16[256,896]{1,0:T(8,128)(2,1)}, u32[]{:S(2)}) copy-start(bf16[256,896]{1,0:T(8,128)(2,1)} %constant.44.clone.spread_ref.refs_9_) | copy-start | bytes 1376260
  67.2 5.3 %copy-start.12 = (bf16[384,128]{1,0:T(8,128)(2,1)S(1)}, bf16[384,128]{1,0:T(8,128)(2,1)}, u32[]{:S(2)}) copy-start(bf16[384,128]{1,0:T(8,128)(2,1)} %constant.45.clone.own_ref.refs_10_) | copy-start | bytes 294916
  67.5 7.9 %copy-start.13 = (f32[2,8,128]{2,1,0:T(8,128)S(1)}, f32[2,8,128]{2,1,0:T(8,128)}, u32[]{:S(2)}) copy-start(f32[2,8,128]{2,1,0:T(8,128)} %get-tuple-element.27.refs_14_) | copy-start | bytes 24580
  67.5 8.0 %copy-start.16 = (bf16[1024,256]{1,0:T(8,128)(2,1)S(1)}, bf16[1024,256]{1,0:T(8,128)(2,1)}, u32[]{:S(2)}) copy-start(bf16[1024,256]{1,0:T(8,128)(2,1)} %copy-done.14) | copy-start | bytes 1572868
  67.5 7.9 %collective-permute-start.6 = (bf16[16,128]{1,0:T(8,128)(2,1)S(1)}, bf16[16,128]{1,0:T(8,128)(2,1)S(1)}, u32[]{:S(2)}, u32[]{:S(2)}) collective-permute-start(bf16[16,128]{1,0:T(8,128)(2,1)S(1)} %get-tuple-element.47), channel_id=1, source_target_pairs={{0,1},{1,2},{2,3},{3,4},{4,5},{5,6},{6,7},{7,8},{8,9},{9,10},{10,1... | collective-permute-start | bytes 12296 | tf_op jit(solution)/shard_map/ppermute | solution.py:647
  71.0 4.4 %collective-permute-start.7 = (bf16[16,128]{1,0:T(8,128)(2,1)S(1)}, bf16[16,128]{1,0:T(8,128)(2,1)S(1)}, u32[]{:S(2)}, u32[]{:S(2)}) collective-permute-start(bf16[16,128]{1,0:T(8,128)(2,1)S(1)} %get-tuple-element.48), channel_id=1, source_target_pairs={{1,0},{2,1},{3,2},{4,3},{5,4},{6,5},{7,6},{8,7},{9,8},{10,9},{11,1... | collective-permute-start | bytes 12296 | tf_op jit(solution)/shard_map/ppermute | solution.py:646
  75.4 5.4 %copy-start.17 = (f32[5,27,80,128]{3,2,1,0:T(8,128)}, f32[5,27,80,128]{3,2,1,0:T(8,128)S(1)}, u32[]{:S(2)}) copy-start(f32[5,27,80,128]{3,2,1,0:T(8,128)S(1)} %get-tuple-element.45.refs_1_) | copy-start | bytes 16588804
  75.4 5.4 %copy-start.19 = (f32[27,80,128]{2,1,0:T(8,128)}, f32[27,80,128]{2,1,0:T(8,128)S(1)}, u32[]{:S(2)}) copy-start(f32[27,80,128]{2,1,0:T(8,128)S(1)} %get-tuple-element.52.refs_0_) | copy-start | bytes 3317764
  75.5 5.4 %copy-start.2 = (f32[4,72,512]{2,1,0:T(8,128)S(1)}, f32[4,72,512]{2,1,0:T(8,128)}, u32[]{:S(2)}) copy-start(f32[4,72,512]{2,1,0:T(8,128)} %a_ref.1) | copy-start | bytes 1769476
  75.5 5.4 %copy-start.5 = (f32[72,72]{1,0:T(8,128)S(1)}, f32[72,72]{1,0:T(8,128)}, u32[]{:S(2)}) copy-start(f32[72,72]{1,0:T(8,128)} %m_ref.1) | copy-start | bytes 62212
  75.5 5.4 %copy-start.21 = (f32[4,8,512]{2,1,0:T(8,128)S(1)}, f32[4,8,512]{2,1,0:T(8,128)}, u32[]{:S(2)}) copy-start(f32[4,8,512]{2,1,0:T(8,128)} %get-tuple-element.51.g_ref) | copy-start | bytes 196612
  80.8 37.1 %copy-start.20 = (f32[27,80,128]{2,1,0:T(8,128)S(1)}, f32[27,80,128]{2,1,0:T(8,128)}, u32[]{:S(2)}) copy-start(f32[27,80,128]{2,1,0:T(8,128)} %copy-done.19) | copy-start | bytes 3317764
  83.5 49.8 %all-to-all-start.1 = ((f32[128,4,128]{2,1,0:T(4,128)}), f32[128,4,128]{2,1,0:T(4,128)S(1)}, u32[]{:S(2)}, u32[]{:S(2)}) async-start(f32[128,4,128]{2,1,0:T(4,128)} %bitcast.12), calls=%async_computation.1 | async-start | bytes 524288 | tf_op jit(solution)/shard_map/all_to_all | solution.py:682
  117.9 2.6 %copy-start.18 = (f32[5,27,80,128]{3,2,1,0:T(8,128)S(1)}, f32[5,27,80,128]{3,2,1,0:T(8,128)}, u32[]{:S(2)}) copy-start(f32[5,27,80,128]{3,2,1,0:T(8,128)} %copy-done.17) | copy-start | bytes 16588804

commit v4 on v3

--- a/solution.py
+++ b/solution.py
@@ -199,7 +199,8 @@
     copy.wait()
 
 
-def atmosphere_body(a_ref, g_ref, m_ref, out_ref):
+def atmosphere_body(a_ref, g_ref, m_ref, out_ref, token_ref):
+    token_ref[...] = jnp.zeros_like(token_ref)
     levels = m_ref.shape[0]
     power = mixing_powers(m_ref)
     lane = iota((levels, 8), 1)
@@ -271,13 +272,6 @@
     return rows + [after_ref[r] for r in range(HALO)]
 
 
-def pack_body(before_ref, z_ref, after_ref, pack_ref, first_ref, last_ref):
-    rows = widened(before_ref, z_ref, after_ref)
-    packed = times(jnp.concatenate(rows, axis=1), pack_ref[...]).astype(bf16)
-    first_ref[...] = packed[:, :LANES]
-    last_ref[...] = packed[:, LANES:]
-
-
 def forcing_rows(f_ref, before_ref, after_ref):
     blank = [jnp.zeros((16, LANES), bf16)]
     rows = blank + [before_ref[r] for r in range(HALO - 1)]
@@ -285,9 +279,10 @@
     return rows + [after_ref[r] for r in range(HALO - 1)] + blank
 
 
-def pack_forcing_body(f_ref, before_ref, after_ref, pack_ref, first_ref, last_ref):
-    rows = forcing_rows(f_ref, before_ref, after_ref)
-    packed = times(jnp.concatenate(rows, axis=1), pack_ref[...]).astype(bf16)
+def pack_body(before_ref, z_ref, after_ref, f_ref, f_before_ref, f_after_ref, pack_ref, first_ref, last_ref):
+    rows = jnp.concatenate(widened(before_ref, z_ref, after_ref), axis=1)
+    forcing = jnp.concatenate(forcing_rows(f_ref, f_before_ref, f_after_ref), axis=1)
+    packed = times(jnp.concatenate([rows, forcing], axis=0), pack_ref[...]).astype(bf16)
     first_ref[...] = packed[:, :LANES]
     last_ref[...] = packed[:, LANES:]
 
@@ -309,22 +304,19 @@
     return here, pltpu.roll(here, LANES - 1, 1), pltpu.roll(here, 1, 1), north, south
 
 
-def ocean_step(n, x_ref, coef_ref, mix_ref, cat_ref, store, force=None):
+def ocean_step(tiles, x, coef, mix_ref, cat_ref, store, force=None):
     levels = mix_ref.shape[0]
-    tiles = list(range(n + 1, EXT - 1 - n)) + list(range(EXT, TILES))
     first = iota((8, LANES), 0) == 0
     for lo in range(0, len(tiles), 4):
         some = tiles[lo : lo + 4]
         slot = (lo // 4) % 2
         for at in range(0, levels, 16):
             for i, idx in enumerate(some):
-                here, east, west, north, south = around(idx, lambda j: x_ref[j, at : at + 16, :])
+                here, east, west, north, south = around(idx, lambda j: x(j, at))
                 stepped = (
-                    coef_ref[0, idx, at : at + 16, :] * here
-                    + (coef_ref[1, idx, at : at + 16, :] * east
-                       + coef_ref[2, idx, at : at + 16, :] * west)
-                    + (coef_ref[3, idx, at : at + 16, :] * north
-                       + coef_ref[4, idx, at : at + 16, :] * south)
+                    coef(0, idx, at) * here
+                    + (coef(1, idx, at) * east + coef(2, idx, at) * west)
+                    + (coef(3, idx, at) * north + coef(4, idx, at) * south)
                 )
                 if force is not None and at == 0:
                     top = stepped[:8] + jnp.where(first, force(idx), 0.0)
@@ -339,33 +331,33 @@
             store(idx, mixed[:, i * LANES : (i + 1) * LANES])
 
 
-def coefficient_body(
-    before_ref, z_ref, after_ref, west_ref, east_ref, x_ref, mix_ref, spread_ref, own_ref,
-    coef_ref, x1_ref, salt_ref, wet_ref, x0_ref, near_ref, edge_ref, cat_ref,
-):
-    levels = mix_ref.shape[0]
-    rows = widened(before_ref, z_ref, after_ref)
-    sides = jnp.concatenate([east_ref[...], west_ref[...]], axis=1)
-    for g in range(EDGES):
-        edge_ref[g] = edge_tile(g, rows, sides, spread_ref, own_ref).astype(bf16)
-
-    def of(idx, at):
-        if idx >= EXT:
-            return edge_ref[idx - EXT, at, :].astype(f32)
-        if idx < HALO:
-            return before_ref[idx, at, :].astype(f32)
-        if idx < HALO + ROWS:
-            return z_ref[idx - HALO, at, :].astype(f32)
-        return after_ref[idx - HALO - ROWS, at, :].astype(f32)
-
-    wets = [of(idx, pl.ds(4 * levels, 16))[:8] for idx in range(TILES)]
-    for idx in range(TILES):
-        wet_ref[idx] = wets[idx]
-    inner = list(range(1, EXT - 1)) + list(range(EXT, TILES))
+def step_tiles(n):
+    return list(range(n + 1, EXT - 1 - n)), list(range(EXT, TILES))
+
+
+def two_refs(main_ref, edge_ref):
+    def get(idx, at):
+        if idx < EXT:
+            return main_ref[idx, at : at + 16, :]
+        return edge_ref[idx - EXT, at : at + 16, :]
+
+    return get
+
+
+def two_coefs(main_ref, edge_ref):
+    def get(s, idx, at):
+        if idx < EXT:
+            return main_ref[s, idx, at : at + 16, :]
+        return edge_ref[s, idx - EXT, at : at + 16, :]
+
+    return get
+
+
+def coefficients(inner, base, of, wets, levels, near_ref, coef_ref):
     for idx in inner:
         here, *near = around(idx, lambda j: wets[j])
         for s in range(4):
-            near_ref[s, idx] = here * near[s]
+            near_ref[s, idx - base] = here * near[s]
 
     def part(c, carry):
         at = pl.multiple_of(c * 16, 16)
@@ -375,35 +367,86 @@
             across = 0.5 * of(idx, pl.ds(3 * levels + at, 16))
             near = []
             for s in range(4):
-                one = near_ref[s, idx]
+                one = near_ref[s, idx - base]
                 near.append(jnp.concatenate([one, one], axis=0))
             c_east = near[0] * (diffusion - along)
             c_west = near[1] * (diffusion + along)
             c_north = near[2] * (diffusion - across)
             c_south = near[3] * (diffusion + across)
-            coef_ref[0, idx, here_at, :] = 1.0 - ((c_east + c_west) + (c_north + c_south))
-            coef_ref[1, idx, here_at, :] = c_east
-            coef_ref[2, idx, here_at, :] = c_west
-            coef_ref[3, idx, here_at, :] = c_north
-            coef_ref[4, idx, here_at, :] = c_south
-        for t, to_ref in enumerate((x0_ref, salt_ref)):
-            for idx in range(TILES):
-                if not HALO <= idx < HALO + ROWS:
-                    to_ref[idx, here_at, :] = of(idx, pl.ds(t * levels + at, 16))
+            coef_ref[0, idx - base, here_at, :] = 1.0 - ((c_east + c_west) + (c_north + c_south))
+            coef_ref[1, idx - base, here_at, :] = c_east
+            coef_ref[2, idx - base, here_at, :] = c_west
+            coef_ref[3, idx - base, here_at, :] = c_north
+            coef_ref[4, idx - base, here_at, :] = c_south
         return carry
 
     lax.fori_loop(0, levels // 16, part, 0)
+
+
+def rows_step_body(
+    before_ref, z_ref, after_ref, x_ref, mix_ref,
+    coef_ref, x1_ref, salt_ref, wet_ref, x0_ref, near_ref, cat_ref,
+):
+    levels = mix_ref.shape[0]
+
+    def of(idx, at):
+        if idx < HALO:
+            return before_ref[idx, at, :].astype(f32)
+        if idx < HALO + ROWS:
+            return z_ref[idx - HALO, at, :].astype(f32)
+        return after_ref[idx - HALO - ROWS, at, :].astype(f32)
+
+    wets = [of(idx, pl.ds(4 * levels, 16))[:8] for idx in range(EXT)]
+    for idx in range(EXT):
+        wet_ref[idx] = wets[idx]
+    inner = step_tiles(0)[0]
+    coefficients(inner, 0, of, wets, levels, near_ref, coef_ref)
     for t, to_ref in enumerate((x0_ref, salt_ref)):
-        for r in range(ROWS):
-            to_ref[HALO + r] = x_ref[t, pl.ds(r, levels, stride=ROWS), :]
+        for idx in range(EXT):
+            if HALO <= idx < HALO + ROWS:
+                to_ref[idx] = x_ref[t, pl.ds(idx - HALO, levels, stride=ROWS), :]
+            else:
+                to_ref[idx] = of(idx, pl.ds(t * levels, levels))
 
     def store(idx, value):
         x1_ref[idx] = value
 
-    ocean_step(0, x0_ref, coef_ref, mix_ref, cat_ref, store)
-
-
-def remap_body(arrival_ref, in_ref, w_ref, u_ref, wet_ref, f_ref, up_ref, down_ref, u_out_ref):
+    ocean_step(inner, two_refs(x0_ref, None), two_coefs(coef_ref, None), mix_ref, cat_ref, store)
+
+
+def edges_step_body(
+    before_ref, z_ref, after_ref, west_ref, east_ref, f_ref, f_before_ref, f_after_ref,
+    mix_ref, spread_ref, own_ref,
+    coef_ref, x1_ref, salt_ref, wet_ref, force_ref, x0_ref, near_ref, edge_ref, cat_ref,
+):
+    levels = mix_ref.shape[0]
+    depth = z_ref.shape[1]
+    rows = widened(before_ref, z_ref, after_ref)
+    forcing = forcing_rows(f_ref, f_before_ref, f_after_ref)
+    rows = [jnp.concatenate(pair, axis=0) for pair in zip(rows, forcing)]
+    sides = jnp.concatenate([east_ref[...], west_ref[...]], axis=1)
+    for g in range(EDGES):
+        tile = edge_tile(g, rows, sides, spread_ref, own_ref)
+        edge_ref[g] = tile[:depth].astype(bf16)
+        force_ref[g] = tile[depth:]
+        x0_ref[g] = tile[:levels]
+        salt_ref[g] = tile[levels : 2 * levels]
+        wet_ref[g] = tile[4 * levels : 4 * levels + 8]
+
+    def of(idx, at):
+        return edge_ref[idx - EXT, at, :].astype(f32)
+
+    inner = step_tiles(0)[1]
+    wets = {idx: wet_ref[idx - EXT] for idx in inner}
+    coefficients(inner, EXT, of, wets, levels, near_ref, coef_ref)
+
+    def store(idx, value):
+        x1_ref[idx - EXT] = value
+
+    ocean_step(inner, two_refs(None, x0_ref), two_coefs(None, coef_ref), mix_ref, cat_ref, store)
+
+
+def remap_body(arrival_ref, in_ref, w_ref, u_ref, wet_ref, _, f_ref, up_ref, down_ref, u_out_ref):
     def pick(j):
         t = arrival_ref[0, j]
         at = pl.multiple_of((t >> 1) * 16, 16)
@@ -471,35 +514,37 @@
 
 
 def tracer_body(t, *refs):
-    x_ref, coef_ref, wet_ref, mix_ref, f_ref, before_ref, after_ref, west_ref, east_ref = refs[:9]
-    spread_ref, own_ref = refs[9:11]
+    x_ref, edge_x_ref, coef_ref, edge_coef_ref, wet_ref, edge_wet_ref = refs[:6]
+    mix_ref, f_ref, before_ref, after_ref, edge_force_ref = refs[6:11]
     if t == 0:
         column_ref, w_ref, place_ref, u_ref, out_hbm, send_ref = refs[11:17]
         one_ref, two_ref, force_ref, cat_ref, out_ref, sem, sst_ref = refs[17:]
     else:
         _, out_hbm, one_ref, two_ref, force_ref, cat_ref, out_ref, sem = refs[11:]
     levels = mix_ref.shape[0]
-    rows = forcing_rows(f_ref, before_ref, after_ref)
-    sides = jnp.concatenate([east_ref[...], west_ref[...]], axis=1)
     for idx in range(1, TILES):
         if idx == EXT - 1:
             continue
-        if HALO <= idx < HALO + ROWS:
-            row = 16 * (idx - HALO)
-            forcing = f_ref[row : row + 16, :]
-        elif idx < EXT:
-            forcing = rows[idx].astype(f32)
+        if idx >= EXT:
+            wet, forcing = edge_wet_ref[idx - EXT], edge_force_ref[idx - EXT]
         else:
-            forcing = edge_tile(idx - EXT, rows, sides, spread_ref, own_ref)
-        force_ref[idx] = surface_gain[t] * wet_ref[idx] * forcing[8 * t : 8 * t + 8]
+            wet = wet_ref[idx]
+            if idx < HALO:
+                forcing = before_ref[idx - 1].astype(f32)
+            elif idx < HALO + ROWS:
+                forcing = f_ref[16 * (idx - HALO) : 16 * (idx - HALO) + 16, :]
+            else:
+                forcing = after_ref[idx - HALO - ROWS].astype(f32)
+        force_ref[idx] = surface_gain[t] * wet * forcing[8 * t : 8 * t + 8]
     if t == 0:
         column = jnp.broadcast_to(column_ref[:, 0:1], (levels, LANES))
         for idx in range(1, TILES):
             if idx != EXT - 1:
-                one_ref[idx] = x_ref[idx] + column * force_ref[idx, 0:1, :]
+                first = x_ref[idx] if idx < EXT else edge_x_ref[idx - EXT]
+                one_ref[idx] = first + column * force_ref[idx, 0:1, :]
         old, new = one_ref, two_ref
     else:
-        old, new = x_ref, one_ref
+        old, new = None, one_ref
     for n in range(1 if t == 0 else 0, STEPS):
 
         def store(idx, value, new=new):
@@ -508,7 +553,16 @@
         def force(idx, n=n):
             return force_ref[idx, n : n + 1, :]
 
-        ocean_step(n, old, coef_ref, mix_ref, cat_ref, store, force)
+        if old is None:
+            x = two_refs(x_ref, edge_x_ref)
+        else:
+
+            def x(idx, at, old=old):
+                return old[idx, at : at + 16, :]
+
+        main, edges = step_tiles(n)
+        coef = two_coefs(coef_ref, edge_coef_ref)
+        ocean_step(main + edges, x, coef, mix_ref, cat_ref, store, force)
         if t == 1 and n == 0:
             old, new = one_ref, two_ref
         else:
@@ -605,12 +659,14 @@
     )(flat, ocean_advect_velocity.reshape(flat.shape), wet_rows)
     before = lax.ppermute(z[ROWS - HALO :], rows_axis, up)
     after = lax.ppermute(z[:HALO], rows_axis, down)
-    edge_shape = shape((depth, LANES), bf16)
-    first, last = call(pack_body, (edge_shape, edge_shape), "pack", [VMEM] * 4)(
-        before, z, after, pack_moves
-    )
-    east_in = lax.ppermute(first, "col", leftward)
-    west_in = lax.ppermute(last, "col", right)
+    gained, wet_rows = lax.optimization_barrier((gained, wet_rows))
+    atm_final, token = call(
+        atmosphere_body,
+        (shape(atmosphere_level_state.shape), shape((8, LANES))),
+        "atmosphere",
+        [VMEM] * 3,
+        micros=3,
+    )(atmosphere_level_state, gained, atmosphere_mixing_map)
     cells = call(
         cells_body,
         shape((ROWS * LANES, WIDE), bf16),
@@ -625,42 +681,60 @@
     rounded = lax.reduce_precision(ocean_mixing_map, 8, 7)
     upper, lower = rounded.astype(bf16), (ocean_mixing_map - rounded).astype(bf16)
     mix = jnp.concatenate([upper, lower, upper], axis=1)
-    wide = (TILES, levels, LANES)
     cat = pltpu.VMEM((2, 3 * levels, 4 * LANES), bf16)
-    arrived, east_in, west_in = lax.optimization_barrier((arrived, east_in, west_in))
 
     edge_rows = shape((HALO - 1, 16, LANES), bf16)
     forcing, send_up, send_down, ocean_currents = call(
         remap_body,
         (shape((ROWS * 16, LANES)), edge_rows, edge_rows, shape(currents.shape)),
         "remap",
-        [SMEM] + [VMEM] * 4,
-    )(arrival, arrived, cells, currents, ocean_cell_mask)
+        [SMEM] + [VMEM] * 4 + [HBM],
+    )(arrival, arrived, cells, currents, ocean_cell_mask, token)
     f_before = lax.ppermute(send_up, rows_axis, up)
     f_after = lax.ppermute(send_down, rows_axis, down)
-    strip = shape((16, LANES), bf16)
-    f_first, f_last = call(pack_forcing_body, (strip, strip), "pack_forcing", [VMEM] * 4)(
-        forcing, f_before, f_after, pack_moves
-    )
-    f_first, f_last, mix = lax.optimization_barrier((f_first, f_last, mix))
-    f_east = lax.ppermute(f_first, "col", leftward)
-    f_west = lax.ppermute(f_last, "col", right)
-
+    strip = shape((depth + 16, LANES), bf16)
+    first, last = call(pack_body, (strip, strip), "pack", [VMEM] * 7)(
+        before, z, after, forcing, f_before, f_after, pack_moves
+    )
+    first, last, mix = lax.optimization_barrier((first, last, mix))
+    east_in = lax.ppermute(first, "col", leftward)
+    west_in = lax.ppermute(last, "col", right)
+    main, side = (EXT, levels, LANES), (EDGES, levels, LANES)
     coef, x1, salt, wet = call(
-        coefficient_body,
-        (shape((5, *wide)), shape(wide), shape(wide), shape((TILES, 8, LANES))),
-        "coefficients",
-        [VMEM] * 9,
+        rows_step_body,
+        (shape((5, *main)), shape(main), shape(main), shape((EXT, 8, LANES))),
+        "rows_step",
+        [VMEM] * 5,
+        scratch=[pltpu.VMEM(main, f32), pltpu.VMEM((4, EXT, 8, LANES), f32), cat],
+        limit=24,
+        micros=2,
+    )(before, z, after, flat, mix)
+    side_coef, side_x1, side_salt, side_wet, side_force = call(
+        edges_step_body,
+        (
+            shape((5, *side)),
+            shape(side),
+            shape(side),
+            shape((EDGES, 8, LANES)),
+            shape((EDGES, 16, LANES)),
+        ),
+        "edges_step",
+        [VMEM] * 11,
         scratch=[
-            pltpu.VMEM(wide, f32),
-            pltpu.VMEM((4, TILES, 8, LANES), f32),
+            pltpu.VMEM(side, f32),
+            pltpu.VMEM((4, EDGES, 8, LANES), f32),
             pltpu.VMEM((EDGES, depth, LANES), bf16),
             cat,
         ],
-        limit=24,
-        micros=4,
-    )(before, z, after, west_in, east_in, flat, mix, spread_moves, own_moves)
-    shared = (coef, wet, mix, forcing, f_before, f_after, f_west, f_east, spread_moves, own_moves)
+        limit=16,
+        micros=1,
+    )(
+        before, z, after, west_in, east_in, forcing, f_before, f_after,
+        mix, spread_moves, own_moves,
+    )
+
+    shared = (coef, side_coef, wet, side_wet, mix, forcing, f_before, f_after, side_force)
+    wide = (TILES, levels, LANES)
     scratch = [
         pltpu.VMEM(wide, f32),
         pltpu.VMEM(wide, f32),
@@ -678,16 +752,8 @@
         scratch=scratch + [pltpu.VMEM((ROWS, LANES), f32)],
         limit=24,
         micros=6,
-    )(x1, *shared, ocean_mixing_map, cells, place, ocean_currents)
+    )(x1, side_x1, *shared, ocean_mixing_map, cells, place, ocean_currents)
     home = lax.all_to_all(terms, band, 0, 0, tiled=True)
-    gained, terms = lax.optimization_barrier((gained, terms))
-    atm_final = call(
-        atmosphere_body,
-        shape(atmosphere_level_state.shape),
-        "atmosphere",
-        [VMEM] * 3,
-        micros=3,
-    )(atmosphere_level_state, gained, atmosphere_mixing_map)
     both = call(
         functools.partial(tracer_body, 1),
         shape(flat.shape),
@@ -698,7 +764,7 @@
         aliases={11: 0},
         limit=24,
         micros=6,
-    )(salt, *shared, warm)
+    )(salt, side_salt, *shared, warm)
     returned = call(finish_body, shape((3, air_columns)), "finish", [VMEM, VMEM])(
         jnp.repeat(table, 4, axis=1), home
     )

time: 135 us -> 109 us (0.81)
  starting transfers between devices: 73 us -> 50.1 us
  waiting for transfers between devices: 24.9 us -> 17.7 us
  local copies, waits for them, and re-layouts: 9.15 us -> 13.1 us
    all_to_all x1, starting transfers between devices: 34.4 us -> 18 us  [on_device(): home = lax.all_to_all(terms, band, 0, 0, tiled=True)]
    ppermute x1, waiting for transfers between devices: 8.18 us -> 0.01 us  [on_device(): before = lax.ppermute(z[ROWS - HALO:], rows_axis, up)]
    all_to_all x1, waiting for transfers between devices: 0.01 us -> 7.75 us  [on_device(): arrived = lax.all_to_all(payload, band, 0, 0, tiled=True)]
    ppermute x1, waiting for transfers between devices: 5.56 us -> 0.01 us  [on_device(): after = lax.ppermute(z[:HALO], rows_axis, down)]
    ppermute x2 -> x0, starting transfers between devices: 4.95 us -> none  [the longest x1 3.48 us: on_device(): f_west = lax.ppermute(f_last, 'col', right)]
    unnamed x47 -> x53, local copies, waits for them, and re-layouts: 7.62 us -> 11 us
    ppermute x1, waiting for transfers between devices: 0.01 us -> 1.79 us  [on_device(): east_in = lax.ppermute(first, 'col', leftward)]
    all_to_all x1, waiting for transfers between devices: 7.62 us -> 5.83 us  [on_device(): home = lax.all_to_all(terms, band, 0, 0, tiled=True)]
  transfers between devices with their start and end apart: 10 -> 8, of which waited for: 4 -> 4; matrix products, arithmetic and copies ran while one was open for 2% -> 4% of each run, Pallas kernels for 7% -> 11%
where the time goes in v4:
time: 109 us; the launch traced here: 108 us
  starting transfers between devices  50.1 us (46%)
  Pallas kernels  24.8 us (23%)
  waiting for transfers between devices  17.7 us (16%)
  local copies, waits for them, and re-layouts  13.1 us (12%)
  other arithmetic  1.52 us (1%)
    all_to_all x1, starting transfers between devices, on_device(): arrived = lax.all_to_all(payload, band, 0, 0, tiled=True)  18.4 us
    all_to_all x1, starting transfers between devices, on_device(): home = lax.all_to_all(terms, band, 0, 0, tiled=True)  18 us
    unnamed x53, local copies, waits for them, and re-layouts  11 us
    all_to_all x1, waiting for transfers between devices, on_device(): arrived = lax.all_to_all(payload, band, 0, 0, tiled=True)  7.75 us
    all_to_all x1, waiting for transfers between devices, on_device(): home = lax.all_to_all(terms, band, 0, 0, tiled=True)  5.83 us
    pallas_call x1, Pallas kernels, on_device(): call(functools.partial(tracer_body, 0), (shape(flat.shape), shape((peers...  5.15 us
    pallas_call x1, Pallas kernels, on_device(): call(functools.partial(tracer_body, 1), shape(flat.shape), 'salinity', [V...  5.08 us
    pallas_call x1, Pallas kernels, on_device(): call(flux_body, (shape((peers * 16, LANES), bf16), shape((4, 8, air_colum...  4.61 us
  transfers between devices with their start and end apart: 8, of which 4 were waited for; matrix products, arithmetic and copies ran while one was open for 4% of the time, Pallas kernels for 11%

profile of v4, /device:TPU:1, one launch (start us, length us, event | category | flops | bytes accessed | tf_op | source)
XLA Modules:
  0.0 108.3 jit_solution(12619594808049000808)
XLA Ops:
  0.7 4.6 %fluxes.1 = (bf16[2048,128]{1,0:T(8,128)(2,1)}, f32[4,8,512]{2,1,0:T(8,128)}) custom-call(s32[2,128]{1,0:T(2,128)} %bitcast.23, f32[4,72,512]{2,1,0:T(8,128)} %a_ref.1, f32[72,72]{1,0:T(8,128)} %m_ref.1, f32[1,512]{1,0:T(1,128)} %bitcast.25), custom_call_target="tpu_custom_call" | custom-call | flops 3000000000 | bytes 9000000 | tf_op jit(solution)/shard_map/fluxes/pallas_call | solution.py:630
  5.3 18.4 %all-to-all-start = ((bf16[128,16,128]{2,1,0:T(8,128)(2,1)}), bf16[128,16,128]{2,1,0:T(8,128)(2,1)S(1)}, u32[]{:S(2)}, u32[]{:S(2)}) async-start(bf16[128,16,128]{2,1,0:T(8,128)(2,1)} %bitcast.21), calls=%async_computation | async-start | bytes 1048576 | tf_op jit(solution)/shard_map/all_to_all | solution.py:649
  23.8 0.2 rows.1.z_ref
  24.0 0.0 copy-start
  24.0 0.0 copy-start.8
  24.1 1.1 %fusion.3 = (bf16[6,336,128]{2,1,0:T(8,128)(2,1)}, bf16[6,336,128]{2,1,0:T(8,128)(2,1)}) fusion(bf16[8,336,128]{2,1,0:T(8,128)(2,1)S(1)} %rows.1.z_ref), kind=kLoop, calls=%fused_computation.13 | loop fusion | bytes 2064384 | tf_op jit(solution)/shard_map/slice | solution.py:661
  25.2 3.6 %collective-permute-start = (bf16[6,336,128]{2,1,0:T(8,128)(2,1)}, bf16[6,336,128]{2,1,0:T(8,128)(2,1)S(1)}, u32[]{:S(2)}, u32[]{:S(2)}) collective-permute-start(bf16[6,336,128]{2,1,0:T(8,128)(2,1)} %get-tuple-element.62), channel_id=1, source_target_pairs={{0,16},{16,32},{32,48},{48,64},{64,80},{80,96},{96,112},{112,128},... | collective-permute-start | bytes 1548296 | tf_op jit(solution)/shard_map/ppermute | solution.py:660
  28.8 1.9 %collective-permute-start.1 = (bf16[6,336,128]{2,1,0:T(8,128)(2,1)}, bf16[6,336,128]{2,1,0:T(8,128)(2,1)S(1)}, u32[]{:S(2)}, u32[]{:S(2)}) collective-permute-start(bf16[6,336,128]{2,1,0:T(8,128)(2,1)} %get-tuple-element.61), channel_id=1, source_target_pairs={{16,0},{32,16},{48,32},{64,48},{80,64},{96,80},{112,96},{128,112},... | collective-permute-start | bytes 1548296 | tf_op jit(solution)/shard_map/ppermute | solution.py:661
  30.8 0.5 broadcast.196
  31.3 0.7 reduce.3
  31.9 0.1 reshape_reshape.3
  32.0 0.1 copy.20
  32.1 0.6 reshape.218
  32.7 0.1 pad_maximum_fusion.mix_ref.refs_6_
  32.8 0.7 compare_select_fusion.1
  33.5 0.0 copy-start.2
  33.5 0.0 copy-start.5
  33.5 1.1 %cells.1.w_ref.refs_12_ = bf16[1024,256]{1,0:T(8,128)(2,1)S(1)} custom-call(bf16[64,4096]{1,0:T(8,128)(2,1)S(1)} %bitcast.18), custom_call_target="tpu_custom_call" | custom-call | flops 1000000000 | bytes 3000000 | tf_op jit(solution)/shard_map/cells/pallas_call | solution.py:670
  34.6 0.8 copy-done.17
  35.4 2.6 %atmosphere.1 = (f32[4,72,512]{2,1,0:T(8,128)}, f32[8,128]{1,0:T(8,128)S(1)}) custom-call(f32[4,72,512]{2,1,0:T(8,128)S(1)} %copy-done.2, f32[4,8,512]{2,1,0:T(8,128)S(1)} %copy-done.24, f32[72,72]{1,0:T(8,128)S(1)} %copy-done.5), custom_call_target="tpu_custom_call" | custom-call | flops 3000000000 | bytes 9000000 | tf_op jit(solution)/shard_map/atmosphere/pallas_call | solution.py:663
  38.1 7.8 %all-to-all-done = bf16[128,16,128]{2,1,0:T(8,128)(2,1)S(1)} async-done(((bf16[128,16,128]{2,1,0:T(8,128)(2,1)}), bf16[128,16,128]{2,1,0:T(8,128)(2,1)S(1)}, u32[]{:S(2)}, u32[]{:S(2)}) %all-to-all-start) | async-done | bytes 524320 | tf_op jit(solution)/shard_map/all_to_all | solution.py:649
  45.8 1.0 copy-done.18
  46.9 1.5 %remap.1 = (f32[128,128]{1,0:T(8,128)S(1)}, bf16[5,16,128]{2,1,0:T(8,128)(2,1)S(1)}, bf16[5,16,128]{2,1,0:T(8,128)(2,1)S(1)}, f32[2,8,128]{2,1,0:T(8,128)}) custom-call(s32[1,64]{1,0:T(1,128)S(1)} %bitcast.20, bf16[2048,128]{1,0:T(8,128)(2,1)S(1)} %bitcast.14, bf16[1024,256]{1,0:T(8,128)(2,1)S(1)} %copy-done.18, f32[2,8,128]{2,1,0:T(8,128)S(1)} %copy-done.6, ...), custom_call_target="tpu_custom_call" | custom-call | flops 1000000000 | bytes 3000000 | tf_op jit(solution)/shard_map/remap/pallas_call | solution.py:687
  48.3 1.9 %collective-permute-start.2 = (bf16[5,16,128]{2,1,0:T(8,128)(2,1)S(1)}, bf16[5,16,128]{2,1,0:T(8,128)(2,1)S(1)}, u32[]{:S(2)}, u32[]{:S(2)}) collective-permute-start(bf16[5,16,128]{2,1,0:T(8,128)(2,1)S(1)} %get-tuple-element.39), channel_id=1, source_target_pairs={{0,16},{16,32},{32,48},{48,64},{64,80},{80,96},{96,112},{112,128},... | collective-permute-start | bytes 61448 | tf_op jit(solution)/shard_map/ppermute | solution.py:693
  50.3 2.4 %collective-permute-start.3 = (bf16[5,16,128]{2,1,0:T(8,128)(2,1)S(1)}, bf16[5,16,128]{2,1,0:T(8,128)(2,1)S(1)}, u32[]{:S(2)}, u32[]{:S(2)}) collective-permute-start(bf16[5,16,128]{2,1,0:T(8,128)(2,1)S(1)} %get-tuple-element.40), channel_id=1, source_target_pairs={{16,0},{32,16},{48,32},{64,48},{80,64},{96,80},{112,96},{128,112},... | collective-permute-start | bytes 61448 | tf_op jit(solution)/shard_map/ppermute | solution.py:694
  52.7 0.1 pad_add_fusion.refs_13_
  52.7 0.1 broadcast_in_dim.13
  52.8 0.1 reshape.220.table_ref
  53.0 2.4 %collective-permute-done.3.f_after_ref.refs_9_ = bf16[5,16,128]{2,1,0:T(8,128)(2,1)S(1)} collective-permute-done((bf16[5,16,128]{2,1,0:T(8,128)(2,1)S(1)}, bf16[5,16,128]{2,1,0:T(8,128)(2,1)S(1)}, u32[]{:S(2)}, u32[]{:S(2)}) %collective-permute-start.3) | collective-permute-done | bytes 20512 | tf_op jit(solution)/shard_map/ppermute | solution.py:694
  55.4 1.3 %copy-done.9 = bf16[2560,256]{1,0:T(8,128)(2,1)S(1)} copy-done((bf16[2560,256]{1,0:T(8,128)(2,1)S(1)}, bf16[2560,256]{1,0:T(8,128)(2,1)}, u32[]{:S(2)}) %copy-start.9) | copy-done | bytes 1310744
  56.7 0.6 pack.1
  57.3 0.0 copy-start.10
  57.3 0.0 copy-start.11
  57.4 2.3 %collective-permute-start.4 = (bf16[352,128]{1,0:T(8,128)(2,1)S(1)}, bf16[352,128]{1,0:T(8,128)(2,1)S(1)}, u32[]{:S(2)}, u32[]{:S(2)}) collective-permute-start(bf16[352,128]{1,0:T(8,128)(2,1)S(1)} %get-tuple-element.45), channel_id=1, source_target_pairs={{0,1},{1,2},{2,3},{3,4},{4,5},{5,6},{6,7},{7,8},{8,9},{9,10},{10,1... | collective-permute-start | bytes 270344 | tf_op jit(solution)/shard_map/ppermute | solution.py:701
  59.7 1.5 %collective-permute-start.5 = (bf16[352,128]{1,0:T(8,128)(2,1)S(1)}, bf16[352,128]{1,0:T(8,128)(2,1)S(1)}, u32[]{:S(2)}, u32[]{:S(2)}) collective-permute-start(bf16[352,128]{1,0:T(8,128)(2,1)S(1)} %get-tuple-element.46), channel_id=1, source_target_pairs={{1,0},{2,1},{3,2},{4,3},{5,4},{6,5},{7,6},{8,7},{9,8},{10,9},{11,1... | collective-permute-start | bytes 270344 | tf_op jit(solution)/shard_map/ppermute | solution.py:700
  61.2 1.3 %rows_step.1 = (f32[5,20,80,128]{3,2,1,0:T(8,128)S(1)}, f32[20,80,128]{2,1,0:T(8,128)S(1)}, f32[20,80,128]{2,1,0:T(8,128)S(1)}, f32[20,8,128]{2,1,0:T(8,128)S(1)}) custom-call(bf16[6,336,128]{2,1,0:T(8,128)(2,1)S(1)} %collective-permute-done.before_ref, bf16[8,336,128]{2,1,0:T(8,128)(2,1)S(1)} %rows.1.z_ref, ...), custom_call_target="tpu_custom_call" | custom-call | flops 2000000000 | bytes 6000000 | tf_op jit(solution)/shard_map/rows_step/pallas_call | solution.py:703
  62.4 0.9 copy-done.20
  63.4 1.8 %collective-permute-done.5.east_ref = bf16[352,128]{1,0:T(8,128)(2,1)S(1)} collective-permute-done((bf16[352,128]{1,0:T(8,128)(2,1)S(1)}, bf16[352,128]{1,0:T(8,128)(2,1)S(1)}, u32[]{:S(2)}, u32[]{:S(2)}) %collective-permute-start.5) | collective-permute-done | bytes 90144 | tf_op jit(solution)/shard_map/ppermute | solution.py:700
  65.2 1.7 %edges_step.1 = (f32[5,7,80,128]{3,2,1,0:T(8,128)S(1)}, f32[7,80,128]{2,1,0:T(8,128)S(1)}, f32[7,80,128]{2,1,0:T(8,128)S(1)}, f32[7,8,128]{2,1,0:T(8,128)S(1)}, f32[7,16,128]{2,1,0:T(8,128)S(1)}) custom-call(bf16[6,336,128]{2,1,0:T(8,128)(2,1)S(1)} %collective-permute-done.before_ref, bf16[8,336,128]{2,1,0:T(8,128)(2,1)S(1)} %rows.1.z_ref, ...), custom_call_target="tpu_custom_call" | custom-call | flops 1000000000 | bytes 3000000 | tf_op jit(solution)/shard_map/edges_step/pallas_call | solution.py:712
  66.9 5.1 %temperature.1 = (f32[2,640,128]{2,1,0:T(8,128)}, f32[512,128]{1,0:T(8,128)}) custom-call(f32[20,80,128]{2,1,0:T(8,128)S(1)} %get-tuple-element.53.refs_0_, f32[7,80,128]{2,1,0:T(8,128)S(1)} %get-tuple-element.54.refs_1_, f32[5,20,80,128]{3,2,1,0:T(8,128)S(1)} %get-tuple-element.48.refs_2_, f32[5,7,80,128]{3,2,1,0:T(8,128)S(1)} %get-tuple-element.49.refs_3_, ...), custom_call_target="tpu_custom_call" | custom-call | flops 6000000000 | bytes 18000000 | tf_op jit(solution)/shard_map/temperature/pallas_call | solution.py:746
  72.1 1.9 %copy-done.15 = f32[5,20,80,128]{3,2,1,0:T(8,128)} copy-done((f32[5,20,80,128]{3,2,1,0:T(8,128)}, f32[5,20,80,128]{3,2,1,0:T(8,128)S(1)}, u32[]{:S(2)}) %copy-start.15) | copy-done | bytes 4096024
  74.0 18.0 %all-to-all-start.1 = ((f32[128,4,128]{2,1,0:T(4,128)}), f32[128,4,128]{2,1,0:T(4,128)S(1)}, u32[]{:S(2)}, u32[]{:S(2)}) async-start(f32[128,4,128]{2,1,0:T(4,128)} %bitcast.12), calls=%async_computation.1 | async-start | bytes 524288 | tf_op jit(solution)/shard_map/all_to_all | solution.py:756
  92.1 1.4 %copy-done.14 = f32[5,7,80,128]{3,2,1,0:T(8,128)S(1)} copy-done((f32[5,7,80,128]{3,2,1,0:T(8,128)S(1)}, f32[5,7,80,128]{3,2,1,0:T(8,128)}, u32[]{:S(2)}) %copy-start.14) | copy-done | bytes 1433624
  93.4 2.2 %copy-done.16 = f32[5,20,80,128]{3,2,1,0:T(8,128)S(1)} copy-done((f32[5,20,80,128]{3,2,1,0:T(8,128)S(1)}, f32[5,20,80,128]{3,2,1,0:T(8,128)}, u32[]{:S(2)}) %copy-start.16) | copy-done | bytes 4096024
  95.6 0.9 copy-done.23
  96.5 5.1 %salinity.1 = f32[2,640,128]{2,1,0:T(8,128)} custom-call(f32[20,80,128]{2,1,0:T(8,128)S(1)} %copy-done.21, f32[7,80,128]{2,1,0:T(8,128)S(1)} %get-tuple-element.47.refs_1_, f32[5,20,80,128]{3,2,1,0:T(8,128)S(1)} %copy-done.16, f32[5,7,80,128]{3,2,1,0:T(8,128)S(1)} %copy-done.14, f32[20,8,128]{2,1,0:T(8,128)S(1)} %copy-done.23, ...), custom_call_target="tpu_custom_call", output_to_operand_aliasing={{}: (11, {})} | custom-call | flops 6000000000 | bytes 18000000 | tf_op jit(solution)/shard_map/salinity/pallas_call | solution.py:757
  101.6 5.8 %all-to-all-done.1 = f32[128,4,128]{2,1,0:T(4,128)S(1)} async-done(((f32[128,4,128]{2,1,0:T(4,128)}), f32[128,4,128]{2,1,0:T(4,128)S(1)}, u32[]{:S(2)}, u32[]{:S(2)}) %all-to-all-start.1) | async-done | bytes 262176 | tf_op jit(solution)/shard_map/all_to_all | solution.py:756
  107.4 0.9 finish.1
  (44 shorter events, 0.1 us)
Async XLA Ops:
  0.6 23.1 %copy-start.1 = (f32[2,80,8,128]{3,2,1,0:T(8,128)S(1)}, f32[2,80,8,128]{3,2,1,0:T(8,128)}, u32[]{:S(2)}) copy-start(f32[2,80,8,128]{3,2,1,0:T(8,128)} %param.17) | copy-start | bytes 1966084
  0.6 23.1 %copy-start.4 = (bf16[2,80,8,128]{3,2,1,0:T(8,128)(2,1)S(1)}, bf16[2,80,8,128]{3,2,1,0:T(8,128)(2,1)}, u32[]{:S(2)}) copy-start(bf16[2,80,8,128]{3,2,1,0:T(8,128)(2,1)} %param.19) | copy-start | bytes 983044
  0.7 23.1 %copy-start.7 = (s32[8,128]{1,0:T(8,128)S(1)}, s32[8,128]{1,0:T(8,128)}, u32[]{:S(2)}) copy-start(s32[8,128]{1,0:T(8,128)} %wet_ref.2) | copy-start | bytes 12292
  5.3 40.5 %all-to-all-start = ((bf16[128,16,128]{2,1,0:T(8,128)(2,1)}), bf16[128,16,128]{2,1,0:T(8,128)(2,1)S(1)}, u32[]{:S(2)}, u32[]{:S(2)}) async-start(bf16[128,16,128]{2,1,0:T(8,128)(2,1)} %bitcast.21), calls=%async_computation | async-start | bytes 1048576 | tf_op jit(solution)/shard_map/all_to_all | solution.py:649
  24.0 6.7 %copy-start = (f32[80,80]{1,0:T(8,128)S(1)}, f32[80,80]{1,0:T(8,128)}, u32[]{:S(2)}) copy-start(f32[80,80]{1,0:T(8,128)} %refs_11_.1) | copy-start | bytes 76804
  24.0 7.2 %copy-start.8 = (s32[1,1,64]{2,1,0:T(1,128)S(1)}, s32[1,1,64]{2,1,0:T(1,128)}, u32[]{:S(2)}) copy-start(s32[1,1,64]{2,1,0:T(1,128)} %param.24) | copy-start | bytes 772
  24.0 9.4 %copy-start.3 = (bf16[1,1,64,4096]{3,2,1,0:T(8,128)(2,1)S(1)}, bf16[1,1,64,4096]{3,2,1,0:T(8,128)(2,1)}, u32[]{:S(2)}) copy-start(bf16[1,1,64,4096]{3,2,1,0:T(8,128)(2,1)} %param.22) | copy-start | bytes 1572868
  25.2 27.8 %collective-permute-start = (bf16[6,336,128]{2,1,0:T(8,128)(2,1)}, bf16[6,336,128]{2,1,0:T(8,128)(2,1)S(1)}, u32[]{:S(2)}, u32[]{:S(2)}) collective-permute-start(bf16[6,336,128]{2,1,0:T(8,128)(2,1)} %get-tuple-element.62), channel_id=1, source_target_pairs={{0,16},{16,32},{32,48},{48,64},{64,80},{80,96},{96,112},{112,128},... | collective-permute-start | bytes 1548296 | tf_op jit(solution)/shard_map/ppermute | solution.py:660
  28.8 24.2 %collective-permute-start.1 = (bf16[6,336,128]{2,1,0:T(8,128)(2,1)}, bf16[6,336,128]{2,1,0:T(8,128)(2,1)S(1)}, u32[]{:S(2)}, u32[]{:S(2)}) collective-permute-start(bf16[6,336,128]{2,1,0:T(8,128)(2,1)} %get-tuple-element.61), channel_id=1, source_target_pairs={{16,0},{32,16},{48,32},{64,48},{80,64},{96,80},{112,96},{128,112},... | collective-permute-start | bytes 1548296 | tf_op jit(solution)/shard_map/ppermute | solution.py:661
  33.5 1.9 %copy-start.2 = (f32[4,72,512]{2,1,0:T(8,128)S(1)}, f32[4,72,512]{2,1,0:T(8,128)}, u32[]{:S(2)}) copy-start(f32[4,72,512]{2,1,0:T(8,128)} %a_ref.1) | copy-start | bytes 1769476
  33.5 1.9 %copy-start.5 = (f32[72,72]{1,0:T(8,128)S(1)}, f32[72,72]{1,0:T(8,128)}, u32[]{:S(2)}) copy-start(f32[72,72]{1,0:T(8,128)} %m_ref.1) | copy-start | bytes 62212
  33.5 1.9 %copy-start.24 = (f32[4,8,512]{2,1,0:T(8,128)S(1)}, f32[4,8,512]{2,1,0:T(8,128)}, u32[]{:S(2)}) copy-start(f32[4,8,512]{2,1,0:T(8,128)} %get-tuple-element.34.g_ref) | copy-start | bytes 196612
  34.6 0.8 copy-start.17
  35.4 10.4 %copy-start.6 = (f32[2,8,128]{2,1,0:T(8,128)S(1)}, f32[2,8,128]{2,1,0:T(8,128)}, u32[]{:S(2)}) copy-start(f32[2,8,128]{2,1,0:T(8,128)} %u_ref.1) | copy-start | bytes 24580
  45.8 1.0 copy-start.18
  46.9 5.9 %copy-start.25 = (s32[1,1,128,2]{2,3,1,0:T(2,128)S(1)}, s32[1,1,128,2]{2,3,1,0:T(2,128)}, u32[]{:S(2)}) copy-start(s32[1,1,128,2]{2,3,1,0:T(2,128)} %param.23) | copy-start | bytes 3076
  48.3 4.7 %collective-permute-start.2 = (bf16[5,16,128]{2,1,0:T(8,128)(2,1)S(1)}, bf16[5,16,128]{2,1,0:T(8,128)(2,1)S(1)}, u32[]{:S(2)}, u32[]{:S(2)}) collective-permute-start(bf16[5,16,128]{2,1,0:T(8,128)(2,1)S(1)} %get-tuple-element.39), channel_id=1, source_target_pairs={{0,16},{16,32},{32,48},{48,64},{64,80},{80,96},{96,112},{112,128},... | collective-permute-start | bytes 61448 | tf_op jit(solution)/shard_map/ppermute | solution.py:693
  50.3 5.1 %collective-permute-start.3 = (bf16[5,16,128]{2,1,0:T(8,128)(2,1)S(1)}, bf16[5,16,128]{2,1,0:T(8,128)(2,1)S(1)}, u32[]{:S(2)}, u32[]{:S(2)}) collective-permute-start(bf16[5,16,128]{2,1,0:T(8,128)(2,1)S(1)} %get-tuple-element.40), channel_id=1, source_target_pairs={{16,0},{32,16},{48,32},{64,48},{80,64},{96,80},{112,96},{128,112},... | collective-permute-start | bytes 61448 | tf_op jit(solution)/shard_map/ppermute | solution.py:694
  55.4 1.3 %copy-start.9 = (bf16[2560,256]{1,0:T(8,128)(2,1)S(1)}, bf16[2560,256]{1,0:T(8,128)(2,1)}, u32[]{:S(2)}) copy-start(bf16[2560,256]{1,0:T(8,128)(2,1)} %constant.43.clone.pack_ref) | copy-start | bytes 3932164
  57.3 7.8 %copy-start.10 = (bf16[256,896]{1,0:T(8,128)(2,1)S(1)}, bf16[256,896]{1,0:T(8,128)(2,1)}, u32[]{:S(2)}) copy-start(bf16[256,896]{1,0:T(8,128)(2,1)} %constant.44.clone.spread_ref) | copy-start | bytes 1376260
  57.3 7.8 %copy-start.11 = (bf16[384,128]{1,0:T(8,128)(2,1)S(1)}, bf16[384,128]{1,0:T(8,128)(2,1)}, u32[]{:S(2)}) copy-start(bf16[384,128]{1,0:T(8,128)(2,1)} %constant.45.clone.own_ref) | copy-start | bytes 294916
  57.4 6.0 %collective-permute-start.4 = (bf16[352,128]{1,0:T(8,128)(2,1)S(1)}, bf16[352,128]{1,0:T(8,128)(2,1)S(1)}, u32[]{:S(2)}, u32[]{:S(2)}) collective-permute-start(bf16[352,128]{1,0:T(8,128)(2,1)S(1)} %get-tuple-element.45), channel_id=1, source_target_pairs={{0,1},{1,2},{2,3},{3,4},{4,5},{5,6},{6,7},{7,8},{8,9},{9,10},{10,1... | collective-permute-start | bytes 270344 | tf_op jit(solution)/shard_map/ppermute | solution.py:701
  59.7 5.5 %collective-permute-start.5 = (bf16[352,128]{1,0:T(8,128)(2,1)S(1)}, bf16[352,128]{1,0:T(8,128)(2,1)S(1)}, u32[]{:S(2)}, u32[]{:S(2)}) collective-permute-start(bf16[352,128]{1,0:T(8,128)(2,1)S(1)} %get-tuple-element.46), channel_id=1, source_target_pairs={{1,0},{2,1},{3,2},{4,3},{5,4},{6,5},{7,6},{8,7},{9,8},{10,9},{11,1... | collective-permute-start | bytes 270344 | tf_op jit(solution)/shard_map/ppermute | solution.py:700
  62.4 0.9 copy-start.20
  63.3 3.5 %copy-start.22 = (f32[20,8,128]{2,1,0:T(8,128)}, f32[20,8,128]{2,1,0:T(8,128)S(1)}, u32[]{:S(2)}) copy-start(f32[20,8,128]{2,1,0:T(8,128)S(1)} %get-tuple-element.50.refs_4_) | copy-start | bytes 245764
  63.3 3.5 %copy-start.12 = (f32[2,8,128]{2,1,0:T(8,128)S(1)}, f32[2,8,128]{2,1,0:T(8,128)}, u32[]{:S(2)}) copy-start(f32[2,8,128]{2,1,0:T(8,128)} %get-tuple-element.29.refs_14_) | copy-start | bytes 24580
  63.3 3.5 %copy-start.19 = (bf16[1024,256]{1,0:T(8,128)(2,1)S(1)}, bf16[1024,256]{1,0:T(8,128)(2,1)}, u32[]{:S(2)}) copy-start(bf16[1024,256]{1,0:T(8,128)(2,1)} %copy-done.17) | copy-start | bytes 1572868
  66.9 5.2 %copy-start.13 = (f32[5,7,80,128]{3,2,1,0:T(8,128)}, f32[5,7,80,128]{3,2,1,0:T(8,128)S(1)}, u32[]{:S(2)}) copy-start(f32[5,7,80,128]{3,2,1,0:T(8,128)S(1)} %get-tuple-element.49.refs_3_) | copy-start | bytes 4300804
  66.9 25.2 %copy-start.21 = (f32[20,80,128]{2,1,0:T(8,128)S(1)}, f32[20,80,128]{2,1,0:T(8,128)}, u32[]{:S(2)}) copy-start(f32[20,80,128]{2,1,0:T(8,128)} %copy-done.20) | copy-start | bytes 2457604
  72.1 1.9 %copy-start.15 = (f32[5,20,80,128]{3,2,1,0:T(8,128)}, f32[5,20,80,128]{3,2,1,0:T(8,128)S(1)}, u32[]{:S(2)}) copy-start(f32[5,20,80,128]{3,2,1,0:T(8,128)S(1)} %get-tuple-element.48.refs_2_) | copy-start | bytes 12288004
  74.0 33.4 %all-to-all-start.1 = ((f32[128,4,128]{2,1,0:T(4,128)}), f32[128,4,128]{2,1,0:T(4,128)S(1)}, u32[]{:S(2)}, u32[]{:S(2)}) async-start(f32[128,4,128]{2,1,0:T(4,128)} %bitcast.12), calls=%async_computation.1 | async-start | bytes 524288 | tf_op jit(solution)/shard_map/all_to_all | solution.py:756
  92.1 1.4 %copy-start.14 = (f32[5,7,80,128]{3,2,1,0:T(8,128)S(1)}, f32[5,7,80,128]{3,2,1,0:T(8,128)}, u32[]{:S(2)}) copy-start(f32[5,7,80,128]{3,2,1,0:T(8,128)} %copy-done.13) | copy-start | bytes 4300804
  93.4 2.2 %copy-start.16 = (f32[5,20,80,128]{3,2,1,0:T(8,128)S(1)}, f32[5,20,80,128]{3,2,1,0:T(8,128)}, u32[]{:S(2)}) copy-start(f32[5,20,80,128]{3,2,1,0:T(8,128)} %copy-done.15) | copy-start | bytes 12288004
  95.6 0.9 copy-start.23

commit v5 on v4

--- a/solution.py
+++ b/solution.py
@@ -89,14 +89,11 @@
 
 
 def moves():
-    pack = np.zeros((EXT, LANES, 2, LANES), np.float32)
     spread = np.zeros((2, LANES, EDGES, LANES), np.float32)
     own = np.zeros((GROUP, LANES, LANES), np.float32)
     for r in range(EXT):
         at = SIDE * (r // EDGES)
         for c in range(HALO):
-            pack[r, c, 0, HALO * r + c] = 1
-            pack[r, LANES - HALO + c, 1, HALO * r + c] = 1
             spread[0, HALO * r + c, r % EDGES, at + SIDE - HALO + c] = 1
             spread[1, HALO * r + c, r % EDGES, at + c] = 1
     for k in range(GROUP):
@@ -104,7 +101,6 @@
             own[k, c, SIDE * k + HALO + c] = 1
             own[k, LANES - REACH + c, SIDE * k + HALO + REACH + c] = 1
     return (
-        jnp.asarray(pack.reshape(EXT * LANES, 2 * LANES), bf16),
         jnp.asarray(spread.reshape(2 * LANES, EDGES * LANES), bf16),
         jnp.asarray(own.reshape(GROUP * LANES, LANES), bf16),
     )
@@ -279,12 +275,32 @@
     return rows + [after_ref[r] for r in range(HALO - 1)] + blank
 
 
-def pack_body(before_ref, z_ref, after_ref, f_ref, f_before_ref, f_after_ref, pack_ref, first_ref, last_ref):
+def pack_matrix():
+    row, lane = iota((LANES, LANES), 0), iota((LANES, LANES), 1)
+    first = jnp.where(row < HALO, lane - row, -LANES)
+    last = jnp.where(row >= LANES - HALO, lane - row + LANES - HALO, -LANES)
+    both = [
+        jnp.concatenate([one_hot(first == HALO * r), one_hot(last == HALO * r)], axis=1)
+        for r in range(EXT)
+    ]
+    return jnp.concatenate(both, axis=0)
+
+
+def pack_body(
+    odd_ref, before_ref, z_ref, after_ref, f_ref, one_ref, two_ref,
+    send_one_ref, send_two_ref, f_before_ref, f_after_ref,
+):
+    odd_row, odd_col = odd_ref[0, 0] == 1, odd_ref[0, 1] == 1
+    for i in range(HALO - 1):
+        one, two = one_ref[i].astype(f32), two_ref[i].astype(f32)
+        f_before_ref[i] = jnp.where(odd_row, two, one).astype(bf16)
+        f_after_ref[i] = jnp.where(odd_row, one, two).astype(bf16)
     rows = jnp.concatenate(widened(before_ref, z_ref, after_ref), axis=1)
     forcing = jnp.concatenate(forcing_rows(f_ref, f_before_ref, f_after_ref), axis=1)
-    packed = times(jnp.concatenate([rows, forcing], axis=0), pack_ref[...]).astype(bf16)
-    first_ref[...] = packed[:, :LANES]
-    last_ref[...] = packed[:, LANES:]
+    packed = times(jnp.concatenate([rows, forcing], axis=0), pack_matrix())
+    first, last = packed[:, :LANES], packed[:, LANES:]
+    send_one_ref[...] = jnp.where(odd_col, last, first).astype(bf16)
+    send_two_ref[...] = jnp.where(odd_col, first, last).astype(bf16)
 
 
 def edge_tile(g, rows, sides, spread_ref, own_ref):
@@ -385,7 +401,7 @@
 
 def rows_step_body(
     before_ref, z_ref, after_ref, x_ref, mix_ref,
-    coef_ref, x1_ref, salt_ref, wet_ref, x0_ref, near_ref, cat_ref,
+    coef_ref, x1_ref, wet_ref, coef_hbm, salt_hbm, x0_ref, near_ref, cat_ref, salt_ref, sems,
 ):
     levels = mix_ref.shape[0]
 
@@ -401,21 +417,29 @@
         wet_ref[idx] = wets[idx]
     inner = step_tiles(0)[0]
     coefficients(inner, 0, of, wets, levels, near_ref, coef_ref)
+    stores = [
+        pltpu.make_async_copy(coef_ref, coef_hbm, sems.at[0]),
+        pltpu.make_async_copy(salt_ref, salt_hbm, sems.at[1]),
+    ]
+    stores[0].start()
     for t, to_ref in enumerate((x0_ref, salt_ref)):
         for idx in range(EXT):
             if HALO <= idx < HALO + ROWS:
                 to_ref[idx] = x_ref[t, pl.ds(idx - HALO, levels, stride=ROWS), :]
             else:
                 to_ref[idx] = of(idx, pl.ds(t * levels, levels))
+    stores[1].start()
 
     def store(idx, value):
         x1_ref[idx] = value
 
     ocean_step(inner, two_refs(x0_ref, None), two_coefs(coef_ref, None), mix_ref, cat_ref, store)
+    for copy in stores:
+        copy.wait()
 
 
 def edges_step_body(
-    before_ref, z_ref, after_ref, west_ref, east_ref, f_ref, f_before_ref, f_after_ref,
+    odd_ref, before_ref, z_ref, after_ref, one_ref, two_ref, f_ref, f_before_ref, f_after_ref,
     mix_ref, spread_ref, own_ref,
     coef_ref, x1_ref, salt_ref, wet_ref, force_ref, x0_ref, near_ref, edge_ref, cat_ref,
 ):
@@ -424,7 +448,10 @@
     rows = widened(before_ref, z_ref, after_ref)
     forcing = forcing_rows(f_ref, f_before_ref, f_after_ref)
     rows = [jnp.concatenate(pair, axis=0) for pair in zip(rows, forcing)]
-    sides = jnp.concatenate([east_ref[...], west_ref[...]], axis=1)
+    odd = odd_ref[0, 1] == 1
+    one, two = one_ref[...].astype(f32), two_ref[...].astype(f32)
+    sides = jnp.concatenate([jnp.where(odd, one, two), jnp.where(odd, two, one)], axis=1)
+    sides = sides.astype(bf16)
     for g in range(EDGES):
         tile = edge_tile(g, rows, sides, spread_ref, own_ref)
         edge_ref[g] = tile[:depth].astype(bf16)
@@ -446,7 +473,7 @@
     ocean_step(inner, two_refs(None, x0_ref), two_coefs(None, coef_ref), mix_ref, cat_ref, store)
 
 
-def remap_body(arrival_ref, in_ref, w_ref, u_ref, wet_ref, _, f_ref, up_ref, down_ref, u_out_ref):
+def remap_body(arrival_ref, odd_ref, in_ref, w_ref, u_ref, wet_ref, _, f_ref, one_ref, two_ref, u_out_ref):
     def pick(j):
         t = arrival_ref[0, j]
         at = pl.multiple_of((t >> 1) * 16, 16)
@@ -470,10 +497,12 @@
         product = times_rows(sources, w_ref[r * LANES : (r + 1) * LANES, :])
         forcing = jnp.where(left_two, product[:16], product[16:])
         f_ref[16 * r : 16 * r + 16, :] = forcing
-        if r < HALO - 1:
-            down_ref[r] = forcing.astype(bf16)
-        if r >= ROWS - HALO + 1:
-            up_ref[r - (ROWS - HALO + 1)] = forcing.astype(bf16)
+    odd = odd_ref[0, 0] == 1
+    for i in range(HALO - 1):
+        up = f_ref[16 * (ROWS - HALO + 1 + i) : 16 * (ROWS - HALO + 2 + i), :]
+        down = f_ref[16 * i : 16 * i + 16, :]
+        one_ref[i] = jnp.where(odd, up, down).astype(bf16)
+        two_ref[i] = jnp.where(odd, down, up).astype(bf16)
     whole = np.linalg.matrix_power(turn, STEPS)
     wet = wet_ref[...].astype(f32)
     push = [surface_push * f_ref[pl.ds(6 + 8 * v, ROWS, stride=16), :] for v in range(2)]
@@ -520,7 +549,15 @@
         column_ref, w_ref, place_ref, u_ref, out_hbm, send_ref = refs[11:17]
         one_ref, two_ref, force_ref, cat_ref, out_ref, sem, sst_ref = refs[17:]
     else:
-        _, out_hbm, one_ref, two_ref, force_ref, cat_ref, out_ref, sem = refs[11:]
+        _, out_hbm, one_ref, two_ref, force_ref, cat_ref, out_ref, sem = refs[11:19]
+        x_hbm, coef_hbm = x_ref, coef_ref
+        x_ref, coef_ref, sems = refs[19:]
+        loads = [
+            pltpu.make_async_copy(x_hbm, x_ref, sems.at[0]),
+            pltpu.make_async_copy(coef_hbm, coef_ref, sems.at[1]),
+        ]
+        for copy in loads:
+            copy.start()
     levels = mix_ref.shape[0]
     for idx in range(1, TILES):
         if idx == EXT - 1:
@@ -544,6 +581,8 @@
                 one_ref[idx] = first + column * force_ref[idx, 0:1, :]
         old, new = one_ref, two_ref
     else:
+        for copy in loads:
+            copy.wait()
         old, new = None, one_ref
     for n in range(1 if t == 0 else 0, STEPS):
 
@@ -593,6 +632,14 @@
     copy.wait()
 
 
+def swaps(size):
+    rounds = []
+    for start in (1, 0):
+        pairs = [(i, i + 1) for i in range(start, size - 1, 2)]
+        rounds.append(pairs + [(j, i) for i, j in pairs])
+    return rounds
+
+
 def neighbours(size):
     up = [(i, i + 1) for i in range(size - 1)]
     return up, [(j, i) for i, j in up]
@@ -617,8 +664,11 @@
     air_levels, air_columns = atmosphere_level_state.shape[1:]
     rows_axis = ("comp", "row")
     up, down = neighbours(lax.axis_size(rows_axis))
-    right, leftward = neighbours(lax.axis_size("col"))
-    pack_moves, spread_moves, own_moves = moves()
+    row_rounds = swaps(lax.axis_size(rows_axis))
+    col_rounds = swaps(lax.axis_size("col"))
+    odd = jnp.stack([lax.axis_index(rows_axis) % 2, lax.axis_index("col") % 2])
+    odd = odd.astype(jnp.int32).reshape(1, 2)
+    spread_moves, own_moves = moves()
 
     table = outgoing_block_table.reshape(peers, 2).T
     arrival = arrival_slot_table.reshape(1, 64)
@@ -684,28 +734,41 @@
     cat = pltpu.VMEM((2, 3 * levels, 4 * LANES), bf16)
 
     edge_rows = shape((HALO - 1, 16, LANES), bf16)
-    forcing, send_up, send_down, ocean_currents = call(
+    forcing, send_one, send_two, ocean_currents = call(
         remap_body,
         (shape((ROWS * 16, LANES)), edge_rows, edge_rows, shape(currents.shape)),
         "remap",
-        [SMEM] + [VMEM] * 4 + [HBM],
-    )(arrival, arrived, cells, currents, ocean_cell_mask, token)
-    f_before = lax.ppermute(send_up, rows_axis, up)
-    f_after = lax.ppermute(send_down, rows_axis, down)
+        [SMEM, SMEM] + [VMEM] * 4 + [HBM],
+    )(arrival, odd, arrived, cells, currents, ocean_cell_mask, token)
+    f_one = lax.ppermute(send_one, rows_axis, row_rounds[0])
+    f_two = lax.ppermute(send_two, rows_axis, row_rounds[1])
     strip = shape((depth + 16, LANES), bf16)
-    first, last = call(pack_body, (strip, strip), "pack", [VMEM] * 7)(
-        before, z, after, forcing, f_before, f_after, pack_moves
-    )
-    first, last, mix = lax.optimization_barrier((first, last, mix))
-    east_in = lax.ppermute(first, "col", leftward)
-    west_in = lax.ppermute(last, "col", right)
+    send_one, send_two, f_before, f_after = call(
+        pack_body, (strip, strip, edge_rows, edge_rows), "pack", [SMEM] + [VMEM] * 6
+    )(odd, before, z, after, forcing, f_one, f_two)
+    send_one, send_two, mix = lax.optimization_barrier((send_one, send_two, mix))
+    one_in = lax.ppermute(send_one, "col", col_rounds[0])
+    two_in = lax.ppermute(send_two, "col", col_rounds[1])
     main, side = (EXT, levels, LANES), (EDGES, levels, LANES)
-    coef, x1, salt, wet = call(
+    coef, x1, wet, coef_late, salt = call(
         rows_step_body,
-        (shape((5, *main)), shape(main), shape(main), shape((EXT, 8, LANES))),
+        (
+            shape((5, *main)),
+            shape(main),
+            shape((EXT, 8, LANES)),
+            shape((5, *main)),
+            shape(main),
+        ),
         "rows_step",
         [VMEM] * 5,
-        scratch=[pltpu.VMEM(main, f32), pltpu.VMEM((4, EXT, 8, LANES), f32), cat],
+        (VMEM, VMEM, VMEM, HBM, HBM),
+        scratch=[
+            pltpu.VMEM(main, f32),
+            pltpu.VMEM((4, EXT, 8, LANES), f32),
+            cat,
+            pltpu.VMEM(main, f32),
+            pltpu.SemaphoreType.DMA((2,)),
+        ],
         limit=24,
         micros=2,
     )(before, z, after, flat, mix)
@@ -719,7 +782,7 @@
             shape((EDGES, 16, LANES)),
         ),
         "edges_step",
-        [VMEM] * 11,
+        [SMEM] + [VMEM] * 11,
         scratch=[
             pltpu.VMEM(side, f32),
             pltpu.VMEM((4, EDGES, 8, LANES), f32),
@@ -729,11 +792,11 @@
         limit=16,
         micros=1,
     )(
-        before, z, after, west_in, east_in, forcing, f_before, f_after,
+        odd, before, z, after, one_in, two_in, forcing, f_before, f_after,
         mix, spread_moves, own_moves,
     )
 
-    shared = (coef, side_coef, wet, side_wet, mix, forcing, f_before, f_after, side_force)
+    shared = (side_coef, wet, side_wet, mix, forcing, f_before, f_after, side_force)
     wide = (TILES, levels, LANES)
     scratch = [
         pltpu.VMEM(wide, f32),
@@ -752,19 +815,20 @@
         scratch=scratch + [pltpu.VMEM((ROWS, LANES), f32)],
         limit=24,
         micros=6,
-    )(x1, side_x1, *shared, ocean_mixing_map, cells, place, ocean_currents)
+    )(x1, side_x1, coef, *shared, ocean_mixing_map, cells, place, ocean_currents)
     home = lax.all_to_all(terms, band, 0, 0, tiled=True)
     both = call(
         functools.partial(tracer_body, 1),
         shape(flat.shape),
         "salinity",
-        [VMEM] * 11 + [HBM],
+        [HBM, VMEM, HBM] + [VMEM] * 8 + [HBM],
         HBM,
-        scratch=scratch,
+        scratch=scratch
+        + [pltpu.VMEM(main, f32), pltpu.VMEM((5, *main), f32), pltpu.SemaphoreType.DMA((2,))],
         aliases={11: 0},
-        limit=24,
+        limit=56,
         micros=6,
-    )(salt, side_salt, *shared, warm)
+    )(salt, side_salt, coef_late, *shared, warm)
     returned = call(finish_body, shape((3, air_columns)), "finish", [VMEM, VMEM])(
         jnp.repeat(table, 4, axis=1), home
     )

time: 109 us -> 102 us (0.936)
  Pallas kernels: 24.8 us -> 33 us
  starting transfers between devices: 50.1 us -> 43 us
  local copies, waits for them, and re-layouts: 13.1 us -> 6.67 us
  waiting for transfers between devices: 17.7 us -> 16.5 us
    all_to_all x1, starting transfers between devices: 18 us -> 10.3 us  [on_device(): home = lax.all_to_all(terms, band, 0, 0, tiled=True)]
    pallas_call x3, Pallas kernels: 6.99 us -> 13.7 us  [the longest x1 8.66 us: on_device(): call(functools.partial(tracer_body, 1), shape(flat.shape), 'salinity', [H...]
    unnamed x53 -> x57, local copies, waits for them, and re-layouts: 11 us -> 5.1 us
    ppermute x4, waiting for transfers between devices: 4.15 us -> 0.93 us  [the longest x1 0.92 us: on_device(): f_one = lax.ppermute(send_one, rows_axis, row_rounds[0])]
    pallas_call x1, Pallas kernels: 1.7 us -> 3.19 us  [on_device(): call(edges_step_body, (shape((5, *side)), shape(side), shape(side), shape...]
    all_to_all x1, waiting for transfers between devices: 7.75 us -> 8.86 us  [on_device(): arrived = lax.all_to_all(payload, band, 0, 0, tiled=True)]
  transfers between devices with their start and end apart: 8 -> 8, of which waited for: 4 -> 3; matrix products, arithmetic and copies ran while one was open for 4% -> 3% of each run, Pallas kernels for 11% -> 17%
where the time goes in v5:
time: 102 us; the launch traced here: 101 us
  starting transfers between devices  43 us (42%)
  Pallas kernels  33 us (32%)
  waiting for transfers between devices  16.5 us (16%)
  local copies, waits for them, and re-layouts  6.67 us (7%)
  between operations  1.15 us (1%)
    all_to_all x1, starting transfers between devices, on_device(): arrived = lax.all_to_all(payload, band, 0, 0, tiled=True)  18.6 us
    all_to_all x1, starting transfers between devices, on_device(): home = lax.all_to_all(terms, band, 0, 0, tiled=True)  10.3 us
    all_to_all x1, waiting for transfers between devices, on_device(): arrived = lax.all_to_all(payload, band, 0, 0, tiled=True)  8.86 us
    pallas_call x1, Pallas kernels, on_device(): call(functools.partial(tracer_body, 1), shape(flat.shape), 'salinity', [H...  8.66 us
    all_to_all x1, waiting for transfers between devices, on_device(): home = lax.all_to_all(terms, band, 0, 0, tiled=True)  6.66 us
    unnamed x57, local copies, waits for them, and re-layouts  5.1 us
    pallas_call x1, Pallas kernels, on_device(): call(functools.partial(tracer_body, 0), (shape(flat.shape), shape((peers...  5.07 us
    pallas_call x1, Pallas kernels, on_device(): call(flux_body, (shape((peers * 16, LANES), bf16), shape((4, 8, air_colum...  4.61 us
  transfers between devices with their start and end apart: 8, of which 3 were waited for; matrix products, arithmetic and copies ran while one was open for 3% of the time, Pallas kernels for 17%

profile of v5, /device:TPU:1, one launch (start us, length us, event | category | flops | bytes accessed | tf_op | source)
XLA Modules:
  0.0 101.2 jit_solution(13277617187209550625)
XLA Ops:
  0.7 4.6 %fluxes.1 = (bf16[2048,128]{1,0:T(8,128)(2,1)}, f32[4,8,512]{2,1,0:T(8,128)}) custom-call(s32[2,128]{1,0:T(2,128)} %bitcast.27, f32[4,72,512]{2,1,0:T(8,128)} %a_ref.1, f32[72,72]{1,0:T(8,128)} %m_ref.1, f32[1,512]{1,0:T(1,128)} %bitcast.29), custom_call_target="tpu_custom_call" | custom-call | flops 3000000000 | bytes 9000000 | tf_op jit(solution)/shard_map/fluxes/pallas_call | solution.py:680
  5.3 0.0 copy-start
  5.3 0.0 copy-start.9
  5.3 0.0 copy-start.4
  5.3 18.6 %all-to-all-start = ((bf16[128,16,128]{2,1,0:T(8,128)(2,1)}), bf16[128,16,128]{2,1,0:T(8,128)(2,1)S(1)}, u32[]{:S(2)}, u32[]{:S(2)}) async-start(bf16[128,16,128]{2,1,0:T(8,128)(2,1)} %bitcast.25), calls=%async_computation | async-start | bytes 1048576 | tf_op jit(solution)/shard_map/all_to_all | solution.py:699
  23.9 0.0 copy-start.3
  23.9 0.0 copy-start.6
  24.0 0.0 copy-start.26
  24.0 0.2 rows.1.z_ref
  24.2 1.1 %fusion.3 = (bf16[6,336,128]{2,1,0:T(8,128)(2,1)}, bf16[6,336,128]{2,1,0:T(8,128)(2,1)}) fusion(bf16[8,336,128]{2,1,0:T(8,128)(2,1)S(1)} %rows.1.z_ref), kind=kLoop, calls=%fused_computation.14 | loop fusion | bytes 2064384 | tf_op jit(solution)/shard_map/slice | solution.py:711
  25.3 3.6 %collective-permute-start = (bf16[6,336,128]{2,1,0:T(8,128)(2,1)}, bf16[6,336,128]{2,1,0:T(8,128)(2,1)}, u32[]{:S(2)}, u32[]{:S(2)}) collective-permute-start(bf16[6,336,128]{2,1,0:T(8,128)(2,1)} %get-tuple-element.68), channel_id=1, source_target_pairs={{0,16},{16,32},{32,48},{48,64},{64,80},{80,96},{96,112},{112,128},... | collective-permute-start | bytes 1548296 | tf_op jit(solution)/shard_map/ppermute | solution.py:710
  29.0 1.9 %collective-permute-start.1 = (bf16[6,336,128]{2,1,0:T(8,128)(2,1)}, bf16[6,336,128]{2,1,0:T(8,128)(2,1)}, u32[]{:S(2)}, u32[]{:S(2)}) collective-permute-start(bf16[6,336,128]{2,1,0:T(8,128)(2,1)} %get-tuple-element.67), channel_id=1, source_target_pairs={{16,0},{32,16},{48,32},{64,48},{80,64},{96,80},{112,96},{128,112},... | collective-permute-start | bytes 1548296 | tf_op jit(solution)/shard_map/ppermute | solution.py:711
  30.9 0.5 broadcast.198
  31.4 0.7 reduce.3
  32.1 0.1 reshape_reshape.3
  32.2 0.1 copy.19
  32.3 0.1 reshape.222
  32.4 0.1 add_bitcast_fusion.odd_ref
  32.4 0.1 pad_maximum_fusion.mix_ref.refs_6_
  32.6 1.1 %cells.1.w_ref.refs_12_ = bf16[1024,256]{1,0:T(8,128)(2,1)S(1)} custom-call(bf16[64,4096]{1,0:T(8,128)(2,1)S(1)} %bitcast.22), custom_call_target="tpu_custom_call" | custom-call | flops 1000000000 | bytes 3000000 | tf_op jit(solution)/shard_map/cells/pallas_call | solution.py:720
  33.7 0.8 copy-done.16
  34.5 0.0 copy-start.27
  34.5 2.6 %atmosphere.1 = (f32[4,72,512]{2,1,0:T(8,128)}, f32[8,128]{1,0:T(8,128)S(1)}) custom-call(f32[4,72,512]{2,1,0:T(8,128)S(1)} %copy-done.3, f32[4,8,512]{2,1,0:T(8,128)S(1)} %copy-done.26, f32[72,72]{1,0:T(8,128)S(1)} %copy-done.6), custom_call_target="tpu_custom_call" | custom-call | flops 3000000000 | bytes 9000000 | tf_op jit(solution)/shard_map/atmosphere/pallas_call | solution.py:713
  37.1 8.9 %all-to-all-done = bf16[128,16,128]{2,1,0:T(8,128)(2,1)S(1)} async-done(((bf16[128,16,128]{2,1,0:T(8,128)(2,1)}), bf16[128,16,128]{2,1,0:T(8,128)(2,1)S(1)}, u32[]{:S(2)}, u32[]{:S(2)}) %all-to-all-start) | async-done | bytes 524320 | tf_op jit(solution)/shard_map/all_to_all | solution.py:699
  46.0 1.0 %copy-done.17 = bf16[1024,256]{1,0:T(8,128)(2,1)S(1)} copy-done((bf16[1024,256]{1,0:T(8,128)(2,1)S(1)}, bf16[1024,256]{1,0:T(8,128)(2,1)}, u32[]{:S(2)}) %copy-start.17) | copy-done | bytes 524312
  47.0 1.5 %remap.1 = (f32[128,128]{1,0:T(8,128)S(1)}, bf16[5,16,128]{2,1,0:T(8,128)(2,1)S(1)}, bf16[5,16,128]{2,1,0:T(8,128)(2,1)S(1)}, f32[2,8,128]{2,1,0:T(8,128)}) custom-call(s32[1,64]{1,0:T(1,128)S(1)} %bitcast.24, s32[1,2]{1,0:T(1,128)S(1)} %add_bitcast_fusion.odd_ref, bf16[2048,128]{1,0:T(8,128)(2,1)S(1)} %bitcast.18, bf16[1024,256]{1,0:T(8,128)(2,1)S(1)} %copy-done.17, ...), custom_call_target="tpu_custom_call" | custom-call | flops 1000000000 | bytes 3000000 | tf_op jit(solution)/shard_map/remap/pallas_call | solution.py:737
  48.5 1.9 %collective-permute-start.2 = (bf16[5,16,128]{2,1,0:T(8,128)(2,1)S(1)}, bf16[5,16,128]{2,1,0:T(8,128)(2,1)S(1)}, u32[]{:S(2)}, u32[]{:S(2)}) collective-permute-start(bf16[5,16,128]{2,1,0:T(8,128)(2,1)S(1)} %get-tuple-element.42), channel_id=1, source_target_pairs={{16,32},{48,64},{80,96},{112,128},{144,160},{176,192},{208,224},{2... | collective-permute-start | bytes 61448 | tf_op jit(solution)/shard_map/ppermute | solution.py:743
  50.4 1.9 %collective-permute-start.3 = (bf16[5,16,128]{2,1,0:T(8,128)(2,1)S(1)}, bf16[5,16,128]{2,1,0:T(8,128)(2,1)S(1)}, u32[]{:S(2)}, u32[]{:S(2)}) collective-permute-start(bf16[5,16,128]{2,1,0:T(8,128)(2,1)S(1)} %get-tuple-element.43), channel_id=1, source_target_pairs={{0,16},{32,48},{64,80},{96,112},{128,144},{160,176},{192,208},{224... | collective-permute-start | bytes 61448 | tf_op jit(solution)/shard_map/ppermute | solution.py:744
  52.4 0.1 pad_add_fusion.refs_13_
  52.4 0.1 broadcast_in_dim.13
  52.5 0.1 reshape.224.table_ref
  52.7 0.0 collective-permute-done.1.after_ref
  52.7 0.9 collective-permute-done.2.one_ref
  53.6 1.8 %pack.1 = (bf16[352,128]{1,0:T(8,128)(2,1)S(1)}, bf16[352,128]{1,0:T(8,128)(2,1)S(1)}, bf16[5,16,128]{2,1,0:T(8,128)(2,1)S(1)}, bf16[5,16,128]{2,1,0:T(8,128)(2,1)S(1)}) custom-call(s32[1,2]{1,0:T(1,128)S(1)} %add_bitcast_fusion.odd_ref, bf16[6,336,128]{2,1,0:T(8,128)(2,1)} %collective-permute-done.before_ref, bf16[8,336,128]{2,1,0:T(8,128)(2,1)S(1)} %rows.1.z_ref, ...), custom_call_target="tpu_custom_call" | custom-call | flops 1000000000 | bytes 3000000 | tf_op jit(solution)/shard_map/pack/pallas_call | solution.py:746
  55.5 0.0 copy-start.10
  55.5 0.0 copy-start.11
  55.5 0.0 copy-start.12
  55.5 0.8 collective-permute-start.4
  56.3 4.0 %collective-permute-start.5 = (bf16[352,128]{1,0:T(8,128)(2,1)S(1)}, bf16[352,128]{1,0:T(8,128)(2,1)S(1)}, u32[]{:S(2)}, u32[]{:S(2)}) collective-permute-start(bf16[352,128]{1,0:T(8,128)(2,1)S(1)} %get-tuple-element.49), channel_id=1, source_target_pairs={{0,1},{2,3},{4,5},{6,7},{8,9},{10,11},{12,13},{14,15},{1,0},{3,2},... | collective-permute-start | bytes 270344 | tf_op jit(solution)/shard_map/ppermute | solution.py:751
  60.3 3.2 %rows_step.1 = (f32[5,20,80,128]{3,2,1,0:T(8,128)S(1)}, f32[20,80,128]{2,1,0:T(8,128)S(1)}, f32[20,8,128]{2,1,0:T(8,128)S(1)}, f32[5,20,80,128]{3,2,1,0:T(8,128)S(1)}, f32[20,80,128]{2,1,0:T(8,128)S(1)}) custom-call(bf16[6,336,128]{2,1,0:T(8,128)(2,1)} %collective-permute-done.before_ref, bf16[8,336,128]{2,1,0:T(8,128)(2,1)S(1)} %rows.1.z_ref, ...), custom_call_target="tpu_custom_call" | custom-call | flops 2000000000 | bytes 6000000 | tf_op jit(solution)/shard_map/rows_step/pallas_call | solution.py:753
  63.5 1.9 %copy-done.15 = f32[5,20,80,128]{3,2,1,0:T(8,128)} copy-done((f32[5,20,80,128]{3,2,1,0:T(8,128)}, f32[5,20,80,128]{3,2,1,0:T(8,128)S(1)}, u32[]{:S(2)}) %copy-start.15) | copy-done | bytes 4096024
  65.5 3.2 %edges_step.1 = (f32[5,7,80,128]{3,2,1,0:T(8,128)S(1)}, f32[7,80,128]{2,1,0:T(8,128)S(1)}, f32[7,80,128]{2,1,0:T(8,128)S(1)}, f32[7,8,128]{2,1,0:T(8,128)S(1)}, f32[7,16,128]{2,1,0:T(8,128)S(1)}) custom-call(s32[1,2]{1,0:T(1,128)S(1)} %add_bitcast_fusion.odd_ref, bf16[6,336,128]{2,1,0:T(8,128)(2,1)} %collective-permute-done.before_ref, ...), custom_call_target="tpu_custom_call" | custom-call | flops 1000000000 | bytes 3000000 | tf_op jit(solution)/shard_map/edges_step/pallas_call | solution.py:775
  68.7 0.7 copy-done.14
  69.5 5.1 %temperature.1 = (f32[2,640,128]{2,1,0:T(8,128)}, f32[512,128]{1,0:T(8,128)}) custom-call(f32[20,80,128]{2,1,0:T(8,128)S(1)} %get-tuple-element.58.refs_0_, f32[7,80,128]{2,1,0:T(8,128)S(1)} %get-tuple-element.59.refs_1_, f32[5,20,80,128]{3,2,1,0:T(8,128)S(1)} %get-tuple-element.60.refs_2_, f32[5,7,80,128]{3,2,1,0:T(8,128)S(1)} %get-tuple-element.54.refs_3_, ...), custom_call_target="tpu_custom_call" | custom-call | flops 6000000000 | bytes 18000000 | tf_op jit(solution)/shard_map/temperature/pallas_call | solution.py:809
  74.6 10.3 %all-to-all-start.1 = ((f32[128,4,128]{2,1,0:T(4,128)}), f32[128,4,128]{2,1,0:T(4,128)S(1)}, u32[]{:S(2)}, u32[]{:S(2)}) async-start(f32[128,4,128]{2,1,0:T(4,128)} %bitcast.15), calls=%async_computation.1 | async-start | bytes 524288 | tf_op jit(solution)/shard_map/all_to_all | solution.py:819
  84.9 8.7 %salinity.1 = f32[2,640,128]{2,1,0:T(8,128)} custom-call(f32[20,80,128]{2,1,0:T(8,128)} %copy-done.21, f32[7,80,128]{2,1,0:T(8,128)} %copy-done.14, f32[5,20,80,128]{3,2,1,0:T(8,128)} %copy-done.15, f32[5,7,80,128]{3,2,1,0:T(8,128)} %copy-done.13, f32[20,8,128]{2,1,0:T(8,128)} %copy-done.25, ...), custom_call_target="tpu_custom_call", output_to_operand_aliasing={{}: (11, {})} | custom-call | flops 6000000000 | bytes 18000000 | tf_op jit(solution)/shard_map/salinity/pallas_call | solution.py:820
  93.6 6.7 %all-to-all-done.1 = f32[128,4,128]{2,1,0:T(4,128)S(1)} async-done(((f32[128,4,128]{2,1,0:T(4,128)}), f32[128,4,128]{2,1,0:T(4,128)S(1)}, u32[]{:S(2)}, u32[]{:S(2)}) %all-to-all-start.1) | async-done | bytes 262176 | tf_op jit(solution)/shard_map/all_to_all | solution.py:819
  100.2 0.9 finish.1
  (49 shorter events, 0.1 us)
Async XLA Ops:
  0.6 23.3 %copy-start.2 = (f32[2,80,8,128]{3,2,1,0:T(8,128)S(1)}, f32[2,80,8,128]{3,2,1,0:T(8,128)}, u32[]{:S(2)}) copy-start(f32[2,80,8,128]{3,2,1,0:T(8,128)} %param.16) | copy-start | bytes 1966084
  0.6 23.3 %copy-start.5 = (bf16[2,80,8,128]{3,2,1,0:T(8,128)(2,1)S(1)}, bf16[2,80,8,128]{3,2,1,0:T(8,128)(2,1)}, u32[]{:S(2)}) copy-start(bf16[2,80,8,128]{3,2,1,0:T(8,128)(2,1)} %param.18) | copy-start | bytes 983044
  0.7 23.3 %copy-start.8 = (s32[8,128]{1,0:T(8,128)S(1)}, s32[8,128]{1,0:T(8,128)}, u32[]{:S(2)}) copy-start(s32[8,128]{1,0:T(8,128)} %wet_ref.2) | copy-start | bytes 12292
  5.3 25.6 %copy-start = (f32[80,80]{1,0:T(8,128)S(1)}, f32[80,80]{1,0:T(8,128)}, u32[]{:S(2)}) copy-start(f32[80,80]{1,0:T(8,128)} %refs_11_.1) | copy-start | bytes 76804
  5.3 26.1 %copy-start.9 = (s32[1,1,64]{2,1,0:T(1,128)S(1)}, s32[1,1,64]{2,1,0:T(1,128)}, u32[]{:S(2)}) copy-start(s32[1,1,64]{2,1,0:T(1,128)} %param.23) | copy-start | bytes 772
  5.3 27.3 %copy-start.4 = (bf16[1,1,64,4096]{3,2,1,0:T(8,128)(2,1)S(1)}, bf16[1,1,64,4096]{3,2,1,0:T(8,128)(2,1)}, u32[]{:S(2)}) copy-start(bf16[1,1,64,4096]{3,2,1,0:T(8,128)(2,1)} %param.21) | copy-start | bytes 1572868
  5.3 40.7 %all-to-all-start = ((bf16[128,16,128]{2,1,0:T(8,128)(2,1)}), bf16[128,16,128]{2,1,0:T(8,128)(2,1)S(1)}, u32[]{:S(2)}, u32[]{:S(2)}) async-start(bf16[128,16,128]{2,1,0:T(8,128)(2,1)} %bitcast.25), calls=%async_computation | async-start | bytes 1048576 | tf_op jit(solution)/shard_map/all_to_all | solution.py:699
  23.9 10.5 %copy-start.3 = (f32[4,72,512]{2,1,0:T(8,128)S(1)}, f32[4,72,512]{2,1,0:T(8,128)}, u32[]{:S(2)}) copy-start(f32[4,72,512]{2,1,0:T(8,128)} %a_ref.1) | copy-start | bytes 1769476
  23.9 10.5 %copy-start.6 = (f32[72,72]{1,0:T(8,128)S(1)}, f32[72,72]{1,0:T(8,128)}, u32[]{:S(2)}) copy-start(f32[72,72]{1,0:T(8,128)} %m_ref.1) | copy-start | bytes 62212
  24.0 10.5 %copy-start.26 = (f32[4,8,512]{2,1,0:T(8,128)S(1)}, f32[4,8,512]{2,1,0:T(8,128)}, u32[]{:S(2)}) copy-start(f32[4,8,512]{2,1,0:T(8,128)} %get-tuple-element.37.g_ref) | copy-start | bytes 196612
  25.3 27.3 %collective-permute-start = (bf16[6,336,128]{2,1,0:T(8,128)(2,1)}, bf16[6,336,128]{2,1,0:T(8,128)(2,1)}, u32[]{:S(2)}, u32[]{:S(2)}) collective-permute-start(bf16[6,336,128]{2,1,0:T(8,128)(2,1)} %get-tuple-element.68), channel_id=1, source_target_pairs={{0,16},{16,32},{32,48},{48,64},{64,80},{80,96},{96,112},{112,128},... | collective-permute-start | bytes 1548296 | tf_op jit(solution)/shard_map/ppermute | solution.py:710
  29.0 23.7 %collective-permute-start.1 = (bf16[6,336,128]{2,1,0:T(8,128)(2,1)}, bf16[6,336,128]{2,1,0:T(8,128)(2,1)}, u32[]{:S(2)}, u32[]{:S(2)}) collective-permute-start(bf16[6,336,128]{2,1,0:T(8,128)(2,1)} %get-tuple-element.67), channel_id=1, source_target_pairs={{16,0},{32,16},{48,32},{64,48},{80,64},{96,80},{112,96},{128,112},... | collective-permute-start | bytes 1548296 | tf_op jit(solution)/shard_map/ppermute | solution.py:711
  32.5 36.9 %copy-start.1 = (bf16[80,240]{1,0:T(8,128)(2,1)}, bf16[80,240]{1,0:T(8,128)(2,1)S(1)}, u32[]{:S(2)}) copy-start(bf16[80,240]{1,0:T(8,128)(2,1)S(1)} %pad_maximum_fusion.mix_ref.refs_6_) | copy-start | bytes 115204
  33.7 0.8 copy-start.16
  34.5 11.5 %copy-start.7 = (f32[2,8,128]{2,1,0:T(8,128)S(1)}, f32[2,8,128]{2,1,0:T(8,128)}, u32[]{:S(2)}) copy-start(f32[2,8,128]{2,1,0:T(8,128)} %u_ref.1) | copy-start | bytes 24580
  34.5 17.9 %copy-start.27 = (s32[1,1,128,2]{2,3,1,0:T(2,128)S(1)}, s32[1,1,128,2]{2,3,1,0:T(2,128)}, u32[]{:S(2)}) copy-start(s32[1,1,128,2]{2,3,1,0:T(2,128)} %param.22) | copy-start | bytes 3076
  46.0 1.0 %copy-start.17 = (bf16[1024,256]{1,0:T(8,128)(2,1)S(1)}, bf16[1024,256]{1,0:T(8,128)(2,1)}, u32[]{:S(2)}) copy-start(bf16[1024,256]{1,0:T(8,128)(2,1)} %copy-done.16) | copy-start | bytes 1572868
  48.5 20.9 %copy-start.19 = (f32[128,128]{1,0:T(8,128)}, f32[128,128]{1,0:T(8,128)S(1)}, u32[]{:S(2)}) copy-start(f32[128,128]{1,0:T(8,128)S(1)} %get-tuple-element.41.f_ref.refs_7_) | copy-start | bytes 196612
  48.5 5.1 %collective-permute-start.2 = (bf16[5,16,128]{2,1,0:T(8,128)(2,1)S(1)}, bf16[5,16,128]{2,1,0:T(8,128)(2,1)S(1)}, u32[]{:S(2)}, u32[]{:S(2)}) collective-permute-start(bf16[5,16,128]{2,1,0:T(8,128)(2,1)S(1)} %get-tuple-element.42), channel_id=1, source_target_pairs={{16,32},{48,64},{80,96},{112,128},{144,160},{176,192},{208,224},{2... | collective-permute-start | bytes 61448 | tf_op jit(solution)/shard_map/ppermute | solution.py:743
  50.4 3.2 %collective-permute-start.3 = (bf16[5,16,128]{2,1,0:T(8,128)(2,1)S(1)}, bf16[5,16,128]{2,1,0:T(8,128)(2,1)S(1)}, u32[]{:S(2)}, u32[]{:S(2)}) collective-permute-start(bf16[5,16,128]{2,1,0:T(8,128)(2,1)S(1)} %get-tuple-element.43), channel_id=1, source_target_pairs={{0,16},{32,48},{64,80},{96,112},{128,144},{160,176},{192,208},{224... | collective-permute-start | bytes 61448 | tf_op jit(solution)/shard_map/ppermute | solution.py:744
  55.5 14.0 %copy-start.23 = (bf16[5,16,128]{2,1,0:T(8,128)(2,1)}, bf16[5,16,128]{2,1,0:T(8,128)(2,1)S(1)}, u32[]{:S(2)}) copy-start(bf16[5,16,128]{2,1,0:T(8,128)(2,1)S(1)} %get-tuple-element.50.f_before_ref.refs_8_) | copy-start | bytes 61444
  55.5 14.0 %copy-start.24 = (bf16[5,16,128]{2,1,0:T(8,128)(2,1)}, bf16[5,16,128]{2,1,0:T(8,128)(2,1)S(1)}, u32[]{:S(2)}) copy-start(bf16[5,16,128]{2,1,0:T(8,128)(2,1)S(1)} %get-tuple-element.51.f_after_ref.refs_9_) | copy-start | bytes 61444
  55.5 10.0 %copy-start.10 = (bf16[256,896]{1,0:T(8,128)(2,1)S(1)}, bf16[256,896]{1,0:T(8,128)(2,1)}, u32[]{:S(2)}) copy-start(bf16[256,896]{1,0:T(8,128)(2,1)} %constant.67.clone.spread_ref) | copy-start | bytes 1376260
  55.5 10.0 %copy-start.11 = (bf16[384,128]{1,0:T(8,128)(2,1)S(1)}, bf16[384,128]{1,0:T(8,128)(2,1)}, u32[]{:S(2)}) copy-start(bf16[384,128]{1,0:T(8,128)(2,1)} %constant.68.clone.own_ref) | copy-start | bytes 294916
  55.5 14.0 %copy-start.12 = (f32[2,8,128]{2,1,0:T(8,128)S(1)}, f32[2,8,128]{2,1,0:T(8,128)}, u32[]{:S(2)}) copy-start(f32[2,8,128]{2,1,0:T(8,128)} %get-tuple-element.32.refs_14_) | copy-start | bytes 24580
  55.5 14.0 %copy-start.18 = (bf16[1024,256]{1,0:T(8,128)(2,1)S(1)}, bf16[1024,256]{1,0:T(8,128)(2,1)}, u32[]{:S(2)}) copy-start(bf16[1024,256]{1,0:T(8,128)(2,1)} %copy-done.16) | copy-start | bytes 1572868
  55.5 9.9 %collective-permute-start.4 = (bf16[352,128]{1,0:T(8,128)(2,1)S(1)}, bf16[352,128]{1,0:T(8,128)(2,1)S(1)}, u32[]{:S(2)}, u32[]{:S(2)}) collective-permute-start(bf16[352,128]{1,0:T(8,128)(2,1)S(1)} %get-tuple-element.48), channel_id=1, source_target_pairs={{1,2},{3,4},{5,6},{7,8},{9,10},{11,12},{13,14},{2,1},{4,3},{6,5},{... | collective-permute-start | bytes 270344 | tf_op jit(solution)/shard_map/ppermute | solution.py:750
  56.3 9.1 %collective-permute-start.5 = (bf16[352,128]{1,0:T(8,128)(2,1)S(1)}, bf16[352,128]{1,0:T(8,128)(2,1)S(1)}, u32[]{:S(2)}, u32[]{:S(2)}) collective-permute-start(bf16[352,128]{1,0:T(8,128)(2,1)S(1)} %get-tuple-element.49), channel_id=1, source_target_pairs={{0,1},{2,3},{4,5},{6,7},{8,9},{10,11},{12,13},{14,15},{1,0},{3,2},... | collective-permute-start | bytes 270344 | tf_op jit(solution)/shard_map/ppermute | solution.py:751
  63.5 1.9 %copy-start.15 = (f32[5,20,80,128]{3,2,1,0:T(8,128)}, f32[5,20,80,128]{3,2,1,0:T(8,128)S(1)}, u32[]{:S(2)}) copy-start(f32[5,20,80,128]{3,2,1,0:T(8,128)S(1)} %get-tuple-element.53.refs_2_) | copy-start | bytes 12288004
  65.5 9.1 %copy-start.21 = (f32[20,80,128]{2,1,0:T(8,128)}, f32[20,80,128]{2,1,0:T(8,128)S(1)}, u32[]{:S(2)}) copy-start(f32[20,80,128]{2,1,0:T(8,128)S(1)} %get-tuple-element.47.refs_0_) | copy-start | bytes 2457604
  65.5 9.1 %copy-start.25 = (f32[20,8,128]{2,1,0:T(8,128)}, f32[20,8,128]{2,1,0:T(8,128)S(1)}, u32[]{:S(2)}) copy-start(f32[20,8,128]{2,1,0:T(8,128)S(1)} %get-tuple-element.55.refs_4_) | copy-start | bytes 245764
  68.7 0.7 copy-start.14
  69.4 5.2 %copy-start.13 = (f32[5,7,80,128]{3,2,1,0:T(8,128)}, f32[5,7,80,128]{3,2,1,0:T(8,128)S(1)}, u32[]{:S(2)}) copy-start(f32[5,7,80,128]{3,2,1,0:T(8,128)S(1)} %get-tuple-element.54.refs_3_) | copy-start | bytes 4300804
  69.4 5.2 %copy-start.20 = (f32[7,16,128]{2,1,0:T(8,128)}, f32[7,16,128]{2,1,0:T(8,128)S(1)}, u32[]{:S(2)}) copy-start(f32[7,16,128]{2,1,0:T(8,128)S(1)} %get-tuple-element.57.refs_10_) | copy-start | bytes 172036
  69.4 5.2 %copy-start.22 = (f32[7,8,128]{2,1,0:T(8,128)}, f32[7,8,128]{2,1,0:T(8,128)S(1)}, u32[]{:S(2)}) copy-start(f32[7,8,128]{2,1,0:T(8,128)S(1)} %get-tuple-element.56.refs_5_) | copy-start | bytes 86020
  74.6 25.6 %all-to-all-start.1 = ((f32[128,4,128]{2,1,0:T(4,128)}), f32[128,4,128]{2,1,0:T(4,128)S(1)}, u32[]{:S(2)}, u32[]{:S(2)}) async-start(f32[128,4,128]{2,1,0:T(4,128)} %bitcast.15), calls=%async_computation.1 | async-start | bytes 524288 | tf_op jit(solution)/shard_map/all_to_all | solution.py:819

commit v6 on v5

--- a/solution.py
+++ b/solution.py
@@ -399,12 +399,7 @@
     lax.fori_loop(0, levels // 16, part, 0)
 
 
-def rows_step_body(
-    before_ref, z_ref, after_ref, x_ref, mix_ref,
-    coef_ref, x1_ref, wet_ref, coef_hbm, salt_hbm, x0_ref, near_ref, cat_ref, salt_ref, sems,
-):
-    levels = mix_ref.shape[0]
-
+def row_reader(before_ref, z_ref, after_ref):
     def of(idx, at):
         if idx < HALO:
             return before_ref[idx, at, :].astype(f32)
@@ -412,30 +407,32 @@
             return z_ref[idx - HALO, at, :].astype(f32)
         return after_ref[idx - HALO - ROWS, at, :].astype(f32)
 
+    return of
+
+
+def row_start(t, of, x_ref, levels, near_ref, coef_ref, wet_ref, x0_ref):
     wets = [of(idx, pl.ds(4 * levels, 16))[:8] for idx in range(EXT)]
     for idx in range(EXT):
         wet_ref[idx] = wets[idx]
-    inner = step_tiles(0)[0]
-    coefficients(inner, 0, of, wets, levels, near_ref, coef_ref)
-    stores = [
-        pltpu.make_async_copy(coef_ref, coef_hbm, sems.at[0]),
-        pltpu.make_async_copy(salt_ref, salt_hbm, sems.at[1]),
-    ]
-    stores[0].start()
-    for t, to_ref in enumerate((x0_ref, salt_ref)):
-        for idx in range(EXT):
-            if HALO <= idx < HALO + ROWS:
-                to_ref[idx] = x_ref[t, pl.ds(idx - HALO, levels, stride=ROWS), :]
-            else:
-                to_ref[idx] = of(idx, pl.ds(t * levels, levels))
-    stores[1].start()
+    coefficients(step_tiles(0)[0], 0, of, wets, levels, near_ref, coef_ref)
+    for idx in range(EXT):
+        if HALO <= idx < HALO + ROWS:
+            x0_ref[idx] = x_ref[t, pl.ds(idx - HALO, levels, stride=ROWS), :]
+        else:
+            x0_ref[idx] = of(idx, pl.ds(t * levels, levels))
+
+
+def rows_step_body(
+    before_ref, z_ref, after_ref, x_ref, mix_ref, coef_ref, x1_ref, wet_ref, x0_ref, near_ref, cat_ref
+):
+    of = row_reader(before_ref, z_ref, after_ref)
+    row_start(0, of, x_ref, mix_ref.shape[0], near_ref, coef_ref, wet_ref, x0_ref)
 
     def store(idx, value):
         x1_ref[idx] = value
 
+    inner = step_tiles(0)[0]
     ocean_step(inner, two_refs(x0_ref, None), two_coefs(coef_ref, None), mix_ref, cat_ref, store)
-    for copy in stores:
-        copy.wait()
 
 
 def edges_step_body(
@@ -543,21 +540,15 @@
 
 
 def tracer_body(t, *refs):
-    x_ref, edge_x_ref, coef_ref, edge_coef_ref, wet_ref, edge_wet_ref = refs[:6]
-    mix_ref, f_ref, before_ref, after_ref, edge_force_ref = refs[6:11]
+    edge_x_ref, edge_coef_ref, edge_wet_ref, mix_ref, f_ref, before_ref, after_ref, edge_force_ref = refs[:8]
     if t == 0:
-        column_ref, w_ref, place_ref, u_ref, out_hbm, send_ref = refs[11:17]
+        x_ref, coef_ref, wet_ref, column_ref, w_ref, place_ref, u_ref, out_hbm, send_ref = refs[8:17]
         one_ref, two_ref, force_ref, cat_ref, out_ref, sem, sst_ref = refs[17:]
     else:
-        _, out_hbm, one_ref, two_ref, force_ref, cat_ref, out_ref, sem = refs[11:19]
-        x_hbm, coef_hbm = x_ref, coef_ref
-        x_ref, coef_ref, sems = refs[19:]
-        loads = [
-            pltpu.make_async_copy(x_hbm, x_ref, sems.at[0]),
-            pltpu.make_async_copy(coef_hbm, coef_ref, sems.at[1]),
-        ]
-        for copy in loads:
-            copy.start()
+        z_before_ref, z_ref, z_after_ref, start_ref, _, out_hbm = refs[8:14]
+        one_ref, two_ref, force_ref, cat_ref, out_ref, sem, x_ref, coef_ref, wet_ref, near_ref = refs[14:]
+        of = row_reader(z_before_ref, z_ref, z_after_ref)
+        row_start(1, of, start_ref, mix_ref.shape[0], near_ref, coef_ref, wet_ref, x_ref)
     levels = mix_ref.shape[0]
     for idx in range(1, TILES):
         if idx == EXT - 1:
@@ -581,8 +572,6 @@
                 one_ref[idx] = first + column * force_ref[idx, 0:1, :]
         old, new = one_ref, two_ref
     else:
-        for copy in loads:
-            copy.wait()
         old, new = None, one_ref
     for n in range(1 if t == 0 else 0, STEPS):
 
@@ -750,25 +739,12 @@
     one_in = lax.ppermute(send_one, "col", col_rounds[0])
     two_in = lax.ppermute(send_two, "col", col_rounds[1])
     main, side = (EXT, levels, LANES), (EDGES, levels, LANES)
-    coef, x1, wet, coef_late, salt = call(
+    coef, x1, wet = call(
         rows_step_body,
-        (
-            shape((5, *main)),
-            shape(main),
-            shape((EXT, 8, LANES)),
-            shape((5, *main)),
-            shape(main),
-        ),
+        (shape((5, *main)), shape(main), shape((EXT, 8, LANES))),
         "rows_step",
         [VMEM] * 5,
-        (VMEM, VMEM, VMEM, HBM, HBM),
-        scratch=[
-            pltpu.VMEM(main, f32),
-            pltpu.VMEM((4, EXT, 8, LANES), f32),
-            cat,
-            pltpu.VMEM(main, f32),
-            pltpu.SemaphoreType.DMA((2,)),
-        ],
+        scratch=[pltpu.VMEM(main, f32), pltpu.VMEM((4, EXT, 8, LANES), f32), cat],
         limit=24,
         micros=2,
     )(before, z, after, flat, mix)
@@ -796,7 +772,7 @@
         mix, spread_moves, own_moves,
     )
 
-    shared = (side_coef, wet, side_wet, mix, forcing, f_before, f_after, side_force)
+    shared = (side_coef, side_wet, mix, forcing, f_before, f_after, side_force)
     wide = (TILES, levels, LANES)
     scratch = [
         pltpu.VMEM(wide, f32),
@@ -815,20 +791,25 @@
         scratch=scratch + [pltpu.VMEM((ROWS, LANES), f32)],
         limit=24,
         micros=6,
-    )(x1, side_x1, coef, *shared, ocean_mixing_map, cells, place, ocean_currents)
+    )(side_x1, *shared, x1, coef, wet, ocean_mixing_map, cells, place, ocean_currents)
     home = lax.all_to_all(terms, band, 0, 0, tiled=True)
     both = call(
         functools.partial(tracer_body, 1),
         shape(flat.shape),
         "salinity",
-        [HBM, VMEM, HBM] + [VMEM] * 8 + [HBM],
+        [VMEM] * 12 + [HBM],
         HBM,
         scratch=scratch
-        + [pltpu.VMEM(main, f32), pltpu.VMEM((5, *main), f32), pltpu.SemaphoreType.DMA((2,))],
-        aliases={11: 0},
+        + [
+            pltpu.VMEM(main, f32),
+            pltpu.VMEM((5, *main), f32),
+            pltpu.VMEM((EXT, 8, LANES), f32),
+            pltpu.VMEM((4, EXT, 8, LANES), f32),
+        ],
+        aliases={12: 0},
         limit=56,
         micros=6,
-    )(salt, side_salt, coef_late, *shared, warm)
+    )(side_salt, *shared, before, z, after, flat, warm)
     returned = call(finish_body, shape((3, air_columns)), "finish", [VMEM, VMEM])(
         jnp.repeat(table, 4, axis=1), home
     )

time: 102 us -> 109 us (1.069)
  waiting for transfers between devices: 16.5 us -> 23.3 us
  starting transfers between devices: 43 us -> 47.7 us
  Pallas kernels: 33 us -> 30.6 us
  local copies, waits for them, and re-layouts: 6.67 us -> 4.75 us
    all_to_all x1, starting transfers between devices: 18.6 us -> 12.6 us  [on_device(): arrived = lax.all_to_all(payload, band, 0, 0, tiled=True)]
    all_to_all x1, waiting for transfers between devices: 8.86 us -> 14.6 us  [on_device(): arrived = lax.all_to_all(payload, band, 0, 0, tiled=True)]
    ppermute x1, starting transfers between devices: 1.92 us -> 6.29 us  [on_device(): after = lax.ppermute(z[:HALO], rows_axis, down)]
    all_to_all x1, starting transfers between devices: 10.3 us -> 14.4 us  [on_device(): home = lax.all_to_all(terms, band, 0, 0, tiled=True)]
    unnamed x57 -> x53, local copies, waits for them, and re-layouts: 5.1 us -> 3.19 us
    all_to_all x1, waiting for transfers between devices: 6.66 us -> 7.85 us  [on_device(): home = lax.all_to_all(terms, band, 0, 0, tiled=True)]
    pallas_call x1, Pallas kernels: 8.66 us -> 7.47 us  [on_device(): call(functools.partial(tracer_body, 1), shape(flat.shape), 'salinity', [V...]
  transfers between devices with their start and end apart: 8 -> 8, of which waited for: 3 -> 4; matrix products, arithmetic and copies ran while one was open for 3% -> 2% of each run, Pallas kernels for 17% -> 14%
where the time goes in v6:
time: 109 us; the launch traced here: 108 us
  starting transfers between devices  47.7 us (44%)
  Pallas kernels  30.6 us (28%)
  waiting for transfers between devices  23.3 us (21%)
  local copies, waits for them, and re-layouts  4.75 us (4%)
  between operations  1.15 us (1%)
    all_to_all x1, waiting for transfers between devices, on_device(): arrived = lax.all_to_all(payload, band, 0, 0, tiled=True)  14.6 us
    all_to_all x1, starting transfers between devices, on_device(): home = lax.all_to_all(terms, band, 0, 0, tiled=True)  14.4 us
    all_to_all x1, starting transfers between devices, on_device(): arrived = lax.all_to_all(payload, band, 0, 0, tiled=True)  12.6 us
    all_to_all x1, waiting for transfers between devices, on_device(): home = lax.all_to_all(terms, band, 0, 0, tiled=True)  7.85 us
    pallas_call x1, Pallas kernels, on_device(): call(functools.partial(tracer_body, 1), shape(flat.shape), 'salinity', [V...  7.47 us
    ppermute x1, starting transfers between devices, on_device(): after = lax.ppermute(z[:HALO], rows_axis, down)  6.29 us
    pallas_call x1, Pallas kernels, on_device(): call(functools.partial(tracer_body, 0), (shape(flat.shape), shape((peers...  5.05 us
    ppermute x1, starting transfers between devices, on_device(): two_in = lax.ppermute(send_two, 'col', col_rounds[1])  4.68 us
  transfers between devices with their start and end apart: 8, of which 4 were waited for; matrix products, arithmetic and copies ran while one was open for 2% of the time, Pallas kernels for 14%

profile of v6, /device:TPU:1, one launch (start us, length us, event | category | flops | bytes accessed | tf_op | source)
XLA Modules:
  0.0 108.4 jit_solution(13503663081378514479)
XLA Ops:
  0.6 0.0 copy-start.3
  0.7 4.6 %fluxes.1 = (bf16[2048,128]{1,0:T(8,128)(2,1)}, f32[4,8,512]{2,1,0:T(8,128)}) custom-call(s32[2,128]{1,0:T(2,128)} %bitcast.28, f32[4,72,512]{2,1,0:T(8,128)} %a_ref.1, f32[72,72]{1,0:T(8,128)} %m_ref.1, f32[1,512]{1,0:T(1,128)} %bitcast.30), custom_call_target="tpu_custom_call" | custom-call | flops 3000000000 | bytes 9000000 | tf_op jit(solution)/shard_map/fluxes/pallas_call | solution.py:669
  5.3 0.0 copy-start.1
  5.3 0.0 copy-start.10
  5.3 0.0 copy-start.5
  5.4 0.2 rows.1.z_ref.refs_9_
  5.6 0.0 copy-start.4
  5.6 0.0 copy-start.7
  5.6 0.0 copy-start.24
  5.7 1.1 %fusion.3 = (bf16[6,336,128]{2,1,0:T(8,128)(2,1)}, bf16[6,336,128]{2,1,0:T(8,128)(2,1)}) fusion(bf16[8,336,128]{2,1,0:T(8,128)(2,1)S(1)} %rows.1.z_ref.refs_9_), kind=kLoop, calls=%fused_computation.14 | loop fusion | bytes 2064384 | tf_op jit(solution)/shard_map/slice | solution.py:700
  6.8 4.6 %collective-permute-start = (bf16[6,336,128]{2,1,0:T(8,128)(2,1)}, bf16[6,336,128]{2,1,0:T(8,128)(2,1)}, u32[]{:S(2)}, u32[]{:S(2)}) collective-permute-start(bf16[6,336,128]{2,1,0:T(8,128)(2,1)} %get-tuple-element.64), channel_id=1, source_target_pairs={{0,16},{16,32},{32,48},{48,64},{64,80},{80,96},{96,112},{112,128},... | collective-permute-start | bytes 1548296 | tf_op jit(solution)/shard_map/ppermute | solution.py:699
  11.3 6.3 %collective-permute-start.1 = (bf16[6,336,128]{2,1,0:T(8,128)(2,1)}, bf16[6,336,128]{2,1,0:T(8,128)(2,1)}, u32[]{:S(2)}, u32[]{:S(2)}) collective-permute-start(bf16[6,336,128]{2,1,0:T(8,128)(2,1)} %get-tuple-element.63), channel_id=1, source_target_pairs={{16,0},{32,16},{48,32},{64,48},{80,64},{96,80},{112,96},{128,112},... | collective-permute-start | bytes 1548296 | tf_op jit(solution)/shard_map/ppermute | solution.py:700
  17.6 12.6 %all-to-all-start = ((bf16[128,16,128]{2,1,0:T(8,128)(2,1)}), bf16[128,16,128]{2,1,0:T(8,128)(2,1)S(1)}, u32[]{:S(2)}, u32[]{:S(2)}) async-start(bf16[128,16,128]{2,1,0:T(8,128)(2,1)} %bitcast.26), calls=%async_computation | async-start | bytes 1048576 | tf_op jit(solution)/shard_map/all_to_all | solution.py:688
  30.3 0.5 broadcast.198
  30.8 0.7 reduce.3
  31.5 0.1 reshape_reshape.3
  31.5 0.1 copy.19
  31.6 0.1 reshape.222
  31.7 0.1 add_bitcast_fusion.odd_ref
  31.8 0.1 pad_maximum_fusion.mix_ref.refs_3_
  32.0 1.1 cells.1.w_ref.refs_12_
  33.1 0.8 copy-done.16
  33.9 0.0 copy-start.25
  33.9 2.6 %atmosphere.1 = (f32[4,72,512]{2,1,0:T(8,128)}, f32[8,128]{1,0:T(8,128)S(1)}) custom-call(f32[4,72,512]{2,1,0:T(8,128)S(1)} %copy-done.4, f32[4,8,512]{2,1,0:T(8,128)S(1)} %copy-done.24, f32[72,72]{1,0:T(8,128)S(1)} %copy-done.7), custom_call_target="tpu_custom_call" | custom-call | flops 3000000000 | bytes 9000000 | tf_op jit(solution)/shard_map/atmosphere/pallas_call | solution.py:702
  36.5 14.6 %all-to-all-done = bf16[128,16,128]{2,1,0:T(8,128)(2,1)S(1)} async-done(((bf16[128,16,128]{2,1,0:T(8,128)(2,1)}), bf16[128,16,128]{2,1,0:T(8,128)(2,1)S(1)}, u32[]{:S(2)}, u32[]{:S(2)}) %all-to-all-start) | async-done | bytes 524320 | tf_op jit(solution)/shard_map/all_to_all | solution.py:688
  51.1 1.0 copy-done.17
  52.1 1.5 %remap.1 = (f32[128,128]{1,0:T(8,128)S(1)}, bf16[5,16,128]{2,1,0:T(8,128)(2,1)S(1)}, bf16[5,16,128]{2,1,0:T(8,128)(2,1)S(1)}, f32[2,8,128]{2,1,0:T(8,128)}) custom-call(s32[1,64]{1,0:T(1,128)S(1)} %bitcast.25, s32[1,2]{1,0:T(1,128)S(1)} %add_bitcast_fusion.odd_ref, bf16[2048,128]{1,0:T(8,128)(2,1)S(1)} %bitcast.18, bf16[1024,256]{1,0:T(8,128)(2,1)S(1)} %copy-done.17, ...), custom_call_target="tpu_custom_call" | custom-call | flops 1000000000 | bytes 3000000 | tf_op jit(solution)/shard_map/remap/pallas_call | solution.py:726
  53.6 2.4 %collective-permute-start.2 = (bf16[5,16,128]{2,1,0:T(8,128)(2,1)S(1)}, bf16[5,16,128]{2,1,0:T(8,128)(2,1)S(1)}, u32[]{:S(2)}, u32[]{:S(2)}) collective-permute-start(bf16[5,16,128]{2,1,0:T(8,128)(2,1)S(1)} %get-tuple-element.40), channel_id=1, source_target_pairs={{16,32},{48,64},{80,96},{112,128},{144,160},{176,192},{208,224},{2... | collective-permute-start | bytes 61448 | tf_op jit(solution)/shard_map/ppermute | solution.py:732
  56.0 1.9 %collective-permute-start.3 = (bf16[5,16,128]{2,1,0:T(8,128)(2,1)S(1)}, bf16[5,16,128]{2,1,0:T(8,128)(2,1)S(1)}, u32[]{:S(2)}, u32[]{:S(2)}) collective-permute-start(bf16[5,16,128]{2,1,0:T(8,128)(2,1)S(1)} %get-tuple-element.41), channel_id=1, source_target_pairs={{0,16},{32,48},{64,80},{96,112},{128,144},{160,176},{192,208},{224... | collective-permute-start | bytes 61448 | tf_op jit(solution)/shard_map/ppermute | solution.py:733
  58.0 0.1 pad_add_fusion.refs_13_
  58.1 0.1 broadcast_in_dim.13
  58.1 0.1 reshape.224.table_ref
  58.3 0.4 collective-permute-done.2.one_ref
  58.7 0.4 collective-permute-done.3.two_ref
  59.1 1.8 %pack.1 = (bf16[352,128]{1,0:T(8,128)(2,1)S(1)}, bf16[352,128]{1,0:T(8,128)(2,1)S(1)}, bf16[5,16,128]{2,1,0:T(8,128)(2,1)S(1)}, bf16[5,16,128]{2,1,0:T(8,128)(2,1)S(1)}) custom-call(s32[1,2]{1,0:T(1,128)S(1)} %add_bitcast_fusion.odd_ref, bf16[6,336,128]{2,1,0:T(8,128)(2,1)} %collective-permute-done.before_ref.refs_8_, ...), custom_call_target="tpu_custom_call" | custom-call | flops 1000000000 | bytes 3000000 | tf_op jit(solution)/shard_map/pack/pallas_call | solution.py:735
  61.0 0.0 copy-start.11
  61.0 0.0 copy-start.12
  61.0 0.0 copy-start.13
  61.1 0.8 collective-permute-start.4
  61.9 4.7 %collective-permute-start.5 = (bf16[352,128]{1,0:T(8,128)(2,1)S(1)}, bf16[352,128]{1,0:T(8,128)(2,1)S(1)}, u32[]{:S(2)}, u32[]{:S(2)}) collective-permute-start(bf16[352,128]{1,0:T(8,128)(2,1)S(1)} %get-tuple-element.45), channel_id=1, source_target_pairs={{0,1},{2,3},{4,5},{6,7},{8,9},{10,11},{12,13},{14,15},{1,0},{3,2},... | collective-permute-start | bytes 270344 | tf_op jit(solution)/shard_map/ppermute | solution.py:740
  66.5 2.4 %rows_step.1 = (f32[5,20,80,128]{3,2,1,0:T(8,128)S(1)}, f32[20,80,128]{2,1,0:T(8,128)S(1)}, f32[20,8,128]{2,1,0:T(8,128)S(1)}) custom-call(bf16[6,336,128]{2,1,0:T(8,128)(2,1)} %collective-permute-done.before_ref.refs_8_, bf16[8,336,128]{2,1,0:T(8,128)(2,1)S(1)} %rows.1.z_ref.refs_9_, bf16[6,336,128]{2,1,0:T(8,128)(2,1)} %collective-permute-done.1.after_ref.refs_10_, ...), custom_call_target="tpu_custom_call" | custom-call | flops 2000000000 | bytes 6000000 | tf_op jit(solution)/shard_map/rows_step/pallas_call | solution.py:742
  69.0 2.9 %edges_step.1 = (f32[5,7,80,128]{3,2,1,0:T(8,128)S(1)}, f32[7,80,128]{2,1,0:T(8,128)S(1)}, f32[7,80,128]{2,1,0:T(8,128)S(1)}, f32[7,8,128]{2,1,0:T(8,128)S(1)}, f32[7,16,128]{2,1,0:T(8,128)S(1)}) custom-call(s32[1,2]{1,0:T(1,128)S(1)} %add_bitcast_fusion.odd_ref, bf16[6,336,128]{2,1,0:T(8,128)(2,1)} %collective-permute-done.before_ref.refs_8_, ...), custom_call_target="tpu_custom_call" | custom-call | flops 1000000000 | bytes 3000000 | tf_op jit(solution)/shard_map/edges_step/pallas_call | solution.py:751
  71.9 0.7 copy-done.15
  72.7 5.0 %temperature.1 = (f32[2,640,128]{2,1,0:T(8,128)}, f32[512,128]{1,0:T(8,128)}) custom-call(f32[7,80,128]{2,1,0:T(8,128)S(1)} %get-tuple-element.53.refs_0_, f32[5,7,80,128]{3,2,1,0:T(8,128)S(1)} %get-tuple-element.50.refs_1_, f32[7,8,128]{2,1,0:T(8,128)S(1)} %get-tuple-element.51.refs_2_, bf16[80,240]{1,0:T(8,128)(2,1)S(1)} %pad_maximum_fusion.mix_ref.refs_3_, ...), custom_call_target="tpu_custom_call" | custom-call | flops 6000000000 | bytes 18000000 | tf_op jit(solution)/shard_map/temperature/pallas_call | solution.py:785
  77.8 14.4 %all-to-all-start.1 = ((f32[128,4,128]{2,1,0:T(4,128)}), f32[128,4,128]{2,1,0:T(4,128)S(1)}, u32[]{:S(2)}, u32[]{:S(2)}) async-start(f32[128,4,128]{2,1,0:T(4,128)} %bitcast.15), calls=%async_computation.1 | async-start | bytes 524288 | tf_op jit(solution)/shard_map/all_to_all | solution.py:795
  92.2 7.5 %salinity.1 = f32[2,640,128]{2,1,0:T(8,128)} custom-call(f32[7,80,128]{2,1,0:T(8,128)} %copy-done.15, f32[5,7,80,128]{3,2,1,0:T(8,128)} %copy-done.14, f32[7,8,128]{2,1,0:T(8,128)} %copy-done.21, bf16[80,240]{1,0:T(8,128)(2,1)} %copy-done.2, f32[128,128]{1,0:T(8,128)} %copy-done.19, bf16[5,16,128]{2,1,0:T(8,128)(2,1)} %copy-done.22, ...), custom_call_target="tpu_custom_call", output_to_operand_aliasing={{}: (12, {})} | custom-call | flops 6000000000 | bytes 18000000 | tf_op jit(solution)/shard_map/salinity/pallas_call | solution.py:796
  99.6 7.9 %all-to-all-done.1 = f32[128,4,128]{2,1,0:T(4,128)S(1)} async-done(((f32[128,4,128]{2,1,0:T(4,128)}), f32[128,4,128]{2,1,0:T(4,128)S(1)}, u32[]{:S(2)}, u32[]{:S(2)}) %all-to-all-start.1) | async-done | bytes 262176 | tf_op jit(solution)/shard_map/all_to_all | solution.py:795
  107.5 0.9 finish.1
  (45 shorter events, 0.1 us)
Async XLA Ops:
  0.6 4.7 %copy-start.3 = (f32[2,80,8,128]{3,2,1,0:T(8,128)S(1)}, f32[2,80,8,128]{3,2,1,0:T(8,128)}, u32[]{:S(2)}) copy-start(f32[2,80,8,128]{3,2,1,0:T(8,128)} %param.16) | copy-start | bytes 1966084
  0.6 4.7 %copy-start.6 = (bf16[2,80,8,128]{3,2,1,0:T(8,128)(2,1)S(1)}, bf16[2,80,8,128]{3,2,1,0:T(8,128)(2,1)}, u32[]{:S(2)}) copy-start(bf16[2,80,8,128]{3,2,1,0:T(8,128)(2,1)} %param.18) | copy-start | bytes 983044
  0.7 4.7 %copy-start.9 = (s32[8,128]{1,0:T(8,128)S(1)}, s32[8,128]{1,0:T(8,128)}, u32[]{:S(2)}) copy-start(s32[8,128]{1,0:T(8,128)} %wet_ref.2) | copy-start | bytes 12292
  5.3 25.0 %copy-start.1 = (f32[80,80]{1,0:T(8,128)S(1)}, f32[80,80]{1,0:T(8,128)}, u32[]{:S(2)}) copy-start(f32[80,80]{1,0:T(8,128)} %refs_11_.1) | copy-start | bytes 76804
  5.3 25.5 %copy-start.10 = (s32[1,1,64]{2,1,0:T(1,128)S(1)}, s32[1,1,64]{2,1,0:T(1,128)}, u32[]{:S(2)}) copy-start(s32[1,1,64]{2,1,0:T(1,128)} %param.23) | copy-start | bytes 772
  5.3 26.6 %copy-start.5 = (bf16[1,1,64,4096]{3,2,1,0:T(8,128)(2,1)S(1)}, bf16[1,1,64,4096]{3,2,1,0:T(8,128)(2,1)}, u32[]{:S(2)}) copy-start(bf16[1,1,64,4096]{3,2,1,0:T(8,128)(2,1)} %param.21) | copy-start | bytes 1572868
  5.6 63.4 %copy-start = (bf16[8,336,128]{2,1,0:T(8,128)(2,1)}, bf16[8,336,128]{2,1,0:T(8,128)(2,1)S(1)}, u32[]{:S(2)}) copy-start(bf16[8,336,128]{2,1,0:T(8,128)(2,1)S(1)} %rows.1.z_ref.refs_9_) | copy-start | bytes 2064388
  5.6 28.2 %copy-start.4 = (f32[4,72,512]{2,1,0:T(8,128)S(1)}, f32[4,72,512]{2,1,0:T(8,128)}, u32[]{:S(2)}) copy-start(f32[4,72,512]{2,1,0:T(8,128)} %a_ref.1) | copy-start | bytes 1769476
  5.6 28.2 %copy-start.7 = (f32[72,72]{1,0:T(8,128)S(1)}, f32[72,72]{1,0:T(8,128)}, u32[]{:S(2)}) copy-start(f32[72,72]{1,0:T(8,128)} %m_ref.1) | copy-start | bytes 62212
  5.6 28.2 %copy-start.24 = (f32[4,8,512]{2,1,0:T(8,128)S(1)}, f32[4,8,512]{2,1,0:T(8,128)}, u32[]{:S(2)}) copy-start(f32[4,8,512]{2,1,0:T(8,128)} %get-tuple-element.35.g_ref) | copy-start | bytes 196612
  6.8 51.5 %collective-permute-start = (bf16[6,336,128]{2,1,0:T(8,128)(2,1)}, bf16[6,336,128]{2,1,0:T(8,128)(2,1)}, u32[]{:S(2)}, u32[]{:S(2)}) collective-permute-start(bf16[6,336,128]{2,1,0:T(8,128)(2,1)} %get-tuple-element.64), channel_id=1, source_target_pairs={{0,16},{16,32},{32,48},{48,64},{64,80},{80,96},{96,112},{112,128},... | collective-permute-start | bytes 1548296 | tf_op jit(solution)/shard_map/ppermute | solution.py:699
  11.3 46.9 %collective-permute-start.1 = (bf16[6,336,128]{2,1,0:T(8,128)(2,1)}, bf16[6,336,128]{2,1,0:T(8,128)(2,1)}, u32[]{:S(2)}, u32[]{:S(2)}) collective-permute-start(bf16[6,336,128]{2,1,0:T(8,128)(2,1)} %get-tuple-element.63), channel_id=1, source_target_pairs={{16,0},{32,16},{48,32},{64,48},{80,64},{96,80},{112,96},{128,112},... | collective-permute-start | bytes 1548296 | tf_op jit(solution)/shard_map/ppermute | solution.py:700
  17.6 33.4 %all-to-all-start = ((bf16[128,16,128]{2,1,0:T(8,128)(2,1)}), bf16[128,16,128]{2,1,0:T(8,128)(2,1)S(1)}, u32[]{:S(2)}, u32[]{:S(2)}) async-start(bf16[128,16,128]{2,1,0:T(8,128)(2,1)} %bitcast.26), calls=%async_computation | async-start | bytes 1048576 | tf_op jit(solution)/shard_map/all_to_all | solution.py:688
  31.9 40.7 %copy-start.2 = (bf16[80,240]{1,0:T(8,128)(2,1)}, bf16[80,240]{1,0:T(8,128)(2,1)S(1)}, u32[]{:S(2)}) copy-start(bf16[80,240]{1,0:T(8,128)(2,1)S(1)} %pad_maximum_fusion.mix_ref.refs_3_) | copy-start | bytes 115204
  33.0 0.8 copy-start.16
  33.9 17.2 %copy-start.8 = (f32[2,8,128]{2,1,0:T(8,128)S(1)}, f32[2,8,128]{2,1,0:T(8,128)}, u32[]{:S(2)}) copy-start(f32[2,8,128]{2,1,0:T(8,128)} %u_ref.1) | copy-start | bytes 24580
  33.9 24.2 %copy-start.25 = (s32[1,1,128,2]{2,3,1,0:T(2,128)S(1)}, s32[1,1,128,2]{2,3,1,0:T(2,128)}, u32[]{:S(2)}) copy-start(s32[1,1,128,2]{2,3,1,0:T(2,128)} %param.22) | copy-start | bytes 3076
  51.1 1.0 copy-start.17
  53.6 19.0 %copy-start.19 = (f32[128,128]{1,0:T(8,128)}, f32[128,128]{1,0:T(8,128)S(1)}, u32[]{:S(2)}) copy-start(f32[128,128]{1,0:T(8,128)S(1)} %get-tuple-element.39.f_ref.refs_4_) | copy-start | bytes 196612
  53.6 5.1 %collective-permute-start.2 = (bf16[5,16,128]{2,1,0:T(8,128)(2,1)S(1)}, bf16[5,16,128]{2,1,0:T(8,128)(2,1)S(1)}, u32[]{:S(2)}, u32[]{:S(2)}) collective-permute-start(bf16[5,16,128]{2,1,0:T(8,128)(2,1)S(1)} %get-tuple-element.40), channel_id=1, source_target_pairs={{16,32},{48,64},{80,96},{112,128},{144,160},{176,192},{208,224},{2... | collective-permute-start | bytes 61448 | tf_op jit(solution)/shard_map/ppermute | solution.py:732
  56.0 3.1 %collective-permute-start.3 = (bf16[5,16,128]{2,1,0:T(8,128)(2,1)S(1)}, bf16[5,16,128]{2,1,0:T(8,128)(2,1)S(1)}, u32[]{:S(2)}, u32[]{:S(2)}) collective-permute-start(bf16[5,16,128]{2,1,0:T(8,128)(2,1)S(1)} %get-tuple-element.41), channel_id=1, source_target_pairs={{0,16},{32,48},{64,80},{96,112},{128,144},{160,176},{192,208},{224... | collective-permute-start | bytes 61448 | tf_op jit(solution)/shard_map/ppermute | solution.py:733
  61.0 11.7 %copy-start.22 = (bf16[5,16,128]{2,1,0:T(8,128)(2,1)}, bf16[5,16,128]{2,1,0:T(8,128)(2,1)S(1)}, u32[]{:S(2)}) copy-start(bf16[5,16,128]{2,1,0:T(8,128)(2,1)S(1)} %get-tuple-element.46.f_before_ref.refs_5_) | copy-start | bytes 61444
  61.0 11.7 %copy-start.23 = (bf16[5,16,128]{2,1,0:T(8,128)(2,1)}, bf16[5,16,128]{2,1,0:T(8,128)(2,1)S(1)}, u32[]{:S(2)}) copy-start(bf16[5,16,128]{2,1,0:T(8,128)(2,1)S(1)} %get-tuple-element.47.f_after_ref.refs_6_) | copy-start | bytes 61444
  61.0 8.0 %copy-start.11 = (bf16[256,896]{1,0:T(8,128)(2,1)S(1)}, bf16[256,896]{1,0:T(8,128)(2,1)}, u32[]{:S(2)}) copy-start(bf16[256,896]{1,0:T(8,128)(2,1)} %constant.67.clone.spread_ref) | copy-start | bytes 1376260
  61.0 8.0 %copy-start.12 = (bf16[384,128]{1,0:T(8,128)(2,1)S(1)}, bf16[384,128]{1,0:T(8,128)(2,1)}, u32[]{:S(2)}) copy-start(bf16[384,128]{1,0:T(8,128)(2,1)} %constant.68.clone.own_ref) | copy-start | bytes 294916
  61.0 11.6 %copy-start.13 = (f32[2,8,128]{2,1,0:T(8,128)S(1)}, f32[2,8,128]{2,1,0:T(8,128)}, u32[]{:S(2)}) copy-start(f32[2,8,128]{2,1,0:T(8,128)} %get-tuple-element.30.refs_14_) | copy-start | bytes 24580
  61.0 11.6 %copy-start.18 = (bf16[1024,256]{1,0:T(8,128)(2,1)S(1)}, bf16[1024,256]{1,0:T(8,128)(2,1)}, u32[]{:S(2)}) copy-start(bf16[1024,256]{1,0:T(8,128)(2,1)} %copy-done.16) | copy-start | bytes 1572868
  61.1 7.9 %collective-permute-start.4 = (bf16[352,128]{1,0:T(8,128)(2,1)S(1)}, bf16[352,128]{1,0:T(8,128)(2,1)S(1)}, u32[]{:S(2)}, u32[]{:S(2)}) collective-permute-start(bf16[352,128]{1,0:T(8,128)(2,1)S(1)} %get-tuple-element.44), channel_id=1, source_target_pairs={{1,2},{3,4},{5,6},{7,8},{9,10},{11,12},{13,14},{2,1},{4,3},{6,5},{... | collective-permute-start | bytes 270344 | tf_op jit(solution)/shard_map/ppermute | solution.py:739
  61.9 7.1 %collective-permute-start.5 = (bf16[352,128]{1,0:T(8,128)(2,1)S(1)}, bf16[352,128]{1,0:T(8,128)(2,1)S(1)}, u32[]{:S(2)}, u32[]{:S(2)}) collective-permute-start(bf16[352,128]{1,0:T(8,128)(2,1)S(1)} %get-tuple-element.45), channel_id=1, source_target_pairs={{0,1},{2,3},{4,5},{6,7},{8,9},{10,11},{12,13},{14,15},{1,0},{3,2},... | collective-permute-start | bytes 270344 | tf_op jit(solution)/shard_map/ppermute | solution.py:740
  71.9 0.7 copy-start.15
  72.6 5.1 %copy-start.14 = (f32[5,7,80,128]{3,2,1,0:T(8,128)}, f32[5,7,80,128]{3,2,1,0:T(8,128)S(1)}, u32[]{:S(2)}) copy-start(f32[5,7,80,128]{3,2,1,0:T(8,128)S(1)} %get-tuple-element.50.refs_1_) | copy-start | bytes 4300804
  72.6 5.1 %copy-start.20 = (f32[7,16,128]{2,1,0:T(8,128)}, f32[7,16,128]{2,1,0:T(8,128)S(1)}, u32[]{:S(2)}) copy-start(f32[7,16,128]{2,1,0:T(8,128)S(1)} %get-tuple-element.52.refs_7_) | copy-start | bytes 172036
  72.6 5.1 %copy-start.21 = (f32[7,8,128]{2,1,0:T(8,128)}, f32[7,8,128]{2,1,0:T(8,128)S(1)}, u32[]{:S(2)}) copy-start(f32[7,8,128]{2,1,0:T(8,128)S(1)} %get-tuple-element.51.refs_2_) | copy-start | bytes 86020
  77.8 29.7 %all-to-all-start.1 = ((f32[128,4,128]{2,1,0:T(4,128)}), f32[128,4,128]{2,1,0:T(4,128)S(1)}, u32[]{:S(2)}, u32[]{:S(2)}) async-start(f32[128,4,128]{2,1,0:T(4,128)} %bitcast.15), calls=%async_computation.1 | async-start | bytes 524288 | tf_op jit(solution)/shard_map/all_to_all | solution.py:795
